TPU v7x, 32 devices: a whole 2x2x4 slice. The times are simulated.
32 devices in a mesh: occ: 4 (over y, x), vir: 8 (over z, core).
Axes of the slice: x: 2, y: 2, z: 4, core: 2. Of those that a mesh axis runs over, the one named last changes fastest.
Arguments:
- amplitudes: bfloat16 [4096, 16384], P('occ', 'vir'), may hold values from -6 to 6
- integrals: bfloat16 [16384, 2048], P('vir', 'occ'), may hold values from -0.1875 to 0.1875
- ij_irrep: int32 [4096], P('occ'), may hold values from 0 to 7
- cd_irrep: int32 [16384], P('vir'), may hold values from 0 to 7
Outputs:
- ladder: float32 [4096, 2048], P('occ', 'vir')
All inputs are finite; a program needn't handle non-finite values.
Results may differ from a plain program's by a relative error of at most 0.0003.
Values may be sent and summed in bfloat16 or wider, within the bound.
No kernel may reach another device: no remote copies, remote signals or barrier semaphores. Data moves between devices by JAX's collectives and lax.ppermute only.
A program may use at most 64 MiB of HBM per device.

v0:
```python
import jax
import jax.numpy as jnp
from jax import lax
from jax.sharding import PartitionSpec as P


def body(amplitudes, integrals, ij_irrep, cd_irrep):
    masked = jnp.where(
        ij_irrep[:, None] == cd_irrep[None, :], amplitudes, jnp.zeros_like(amplitudes)
    )
    partial_sums = jnp.dot(
        masked,
        lax.all_gather(integrals, "occ", axis=1, tiled=True),
        preferred_element_type=jnp.float32,
    )
    ladder = lax.psum_scatter(partial_sums, "vir", scatter_dimension=1, tiled=True)
    return ladder


def solution(mesh):
    in_specs = (P("occ", "vir"), P("vir", "occ"), P("occ"), P("vir"))
    out_specs = P("occ", "vir")
    return jax.shard_map(body, mesh=mesh, in_specs=in_specs, out_specs=out_specs, check_vma=False)
```

profile of v0, /device:TPU:0, one launch (start us, length us, event | category | flops | bytes accessed | tf_op | source)
XLA Modules:
  0.0 210.6 jit_solution(5960883745846571095)
XLA Ops:
  6.5 0.0 all-gather.2.cloned.1.call-start
  6.5 0.7 all-gather.2.cloned.1.call-update
  7.3 0.0 reduce-scatter.2.cloned.1.call-start
  7.3 92.1 %all-gather.2.cloned.1.call-done = bf16[2048,2048]{1,0:T(8,128)(2,1)} async-done(((bf16[2048,512]{1,0:T(8,128)(2,1)}), bf16[2048,2048]{1,0:T(8,128)(2,1)}) %all-gather.2.cloned.1.call-update) | async-done | bytes 8388624 | tf_op jit(solution)/shard_map/all_gather | solution.py:13
  99.4 14.5 %fusion = f32[1024,2048]{1,0:T(8,128)} fusion(bf16[2048,2048]{1,0:T(8,128)(2,1)} %all-gather.2.cloned.1.call-done, bf16[1024,2048]{1,0:T(8,128)(2,1)} %param.4, s32[2048]{0:T(1024)} %param.7, s32[1024]{0:T(1024)} %param.6), kind=kOutput, calls=%fused_computation.1 | convolution fusion | flops 8594128896 | bytes 20983808 | tf_op jit(solution)/shard_map/dot_general | solution.py:11
  113.9 0.0 reduce-scatter.2.cloned.1.call-update
  114.0 89.8 %reduce-scatter.2.cloned.1.call-done = f32[1024,256]{1,0:T(8,128)} async-done(((f32[1024,2048]{1,0:T(8,128)}), f32[1024,256]{1,0:T(8,128)}) %reduce-scatter.2.cloned.1.call-update) | async-done | bytes 1048592 | tf_op jit(solution)/shard_map/reduce_scatter | solution.py:16
Async XLA Ops:
  6.5 92.9 %all-gather.2.cloned.1.call-start = ((), (), s32[]{:S(2)}) async-start(), calls=%async_computation.1 | async-start | bytes 10485760 | tf_op jit(solution)/shard_map/all_gather | solution.py:13
  7.3 196.5 %reduce-scatter.2.cloned.1.call-start = ((), (), s32[]{:S(2)}) async-start(), calls=%async_computation.2 | async-start | bytes 9437184 | tf_op jit(solution)/shard_map/reduce_scatter | solution.py:16
Sparse Core Ops, SparseCore 0:
  9.2 90.1 all-gather.1
  114.1 89.5 reduce-scatter.1
where the time goes:
time: 211 us
  waiting for transfers between devices  183 us (87%)
  matrix products  14.5 us (7%)
  between operations  13.4 us (6%)
    all_gather x1, waiting for transfers between devices, body(): lax.all_gather(integrals, 'occ', axis=1, tiled=True)  92.1 us
    reduce_scatter x1, waiting for transfers between devices, body(): lax.psum_scatter(partial_sums, 'vir', scatter_dimension=1, tiled=True)  89.8 us
    dot_general x1, matrix products, body(): jnp.dot(masked, lax.all_gather(integrals, 'occ', axis=1, tiled=True), pre...  14.5 us
  transfers between devices with their start and end apart: 2, of which 2 were waited for; matrix products, arithmetic and copies ran while one was open for 0% of the time, Pallas kernels for 0%

commit v1 on v0

v1 whole, which is shorter than its diff:
```python
import functools
import math

import jax
import jax.numpy as jnp
from jax import lax
from jax.experimental import pallas as pl
from jax.experimental.pallas import tpu as pltpu
from jax.sharding import PartitionSpec as P

AMPLITUDE_MAX = 6.0
INTEGRAL_MAX = 0.1875
HALF_MAX = 65504.0
GRANULES = 4
ROW_TILE = 256
VMEM_LIMIT = 32 * 1024 * 1024


def masked_amplitudes(amplitudes, ij_irrep, cd_irrep):
    return jnp.where(
        ij_irrep[:, None] == cd_irrep[None, :], amplitudes, jnp.zeros_like(amplitudes)
    )


def plain_body(amplitudes, integrals, ij_irrep, cd_irrep):
    partial_sums = jnp.dot(
        masked_amplitudes(amplitudes, ij_irrep, cd_irrep),
        lax.all_gather(integrals, "occ", axis=1, tiled=True),
        preferred_element_type=jnp.float32,
    )
    return lax.psum_scatter(partial_sums, "vir", scatter_dimension=1, tiled=True)


def product_kernel(scale, occ_ref, own_amps, other_amps, *refs):
    pieces, out_ref, own_rows, other_rows = refs[:8], refs[8], refs[9], refs[10]
    half = own_rows.shape[0] // 2
    width = pieces[0].shape[1] // 2

    @pl.when(pl.program_id(0) == 0)
    def _():
        for part in range(2):
            rows = pl.ds(part * half, half)
            blocks = [piece[...] for piece in pieces[part::2]]
            own_rows[rows, :] = jnp.concatenate([b[:, :width] for b in blocks], axis=1)
            other_rows[rows, :] = jnp.concatenate([b[:, width:] for b in blocks], axis=1)

    sums = jnp.dot(own_amps[...], own_rows[...], preferred_element_type=jnp.float32)
    sums += jnp.dot(other_amps[...], other_rows[...], preferred_element_type=jnp.float32)
    sums = sums * scale
    top = sums.shape[0] // 2
    for relation in range(4):
        block = sums[:, relation * width : (relation + 1) * width]
        packed = jnp.concatenate([block[:top], block[top:]], axis=1)
        out_ref[occ_ref[0] ^ relation] = packed


def product(occ, own_amps, other_amps, halves, scale):
    rows, depth = own_amps.shape
    lanes = halves[0][0].shape[1]
    in_specs = [
        pl.BlockSpec(memory_space=pltpu.SMEM),
        pl.BlockSpec((ROW_TILE, depth), lambda i: (i, 0)),
        pl.BlockSpec((ROW_TILE, depth), lambda i: (i, 0)),
    ]
    for _, part in halves:
        in_specs.append(pl.BlockSpec((depth // 2, lanes), functools.partial(lambda at, i: (at, 0), part)))
    return pl.pallas_call(
        functools.partial(product_kernel, scale),
        grid=(rows // ROW_TILE,),
        in_specs=in_specs,
        out_specs=pl.BlockSpec((4, ROW_TILE // 2, lanes), lambda i: (0, i, 0)),
        out_shape=jax.ShapeDtypeStruct((4, rows // 2, lanes), jnp.float32),
        scratch_shapes=[pltpu.VMEM((depth, 2 * lanes), jnp.bfloat16)] * 2,
        compiler_params=pltpu.CompilerParams(vmem_limit_bytes=VMEM_LIMIT),
        cost_estimate=pl.CostEstimate(
            flops=4 * rows * depth * 2 * lanes, bytes_accessed=4 * rows * depth, transcendentals=0
        ),
    )(occ, own_amps, other_amps, *[array for array, _ in halves])


def total_kernel(unscale, *refs):
    parts, out_ref = refs[:-1], refs[-1]
    columns = []
    for part in parts:
        total = part[...] * unscale
        width = total.shape[1] // 2
        columns.append(jnp.concatenate([total[:, :width], total[:, width:]], axis=0))
    out_ref[...] = jnp.concatenate(columns, axis=1)


def total(parts, unscale):
    rows, lanes = parts[0].shape
    return pl.pallas_call(
        functools.partial(total_kernel, unscale),
        grid=(2 * rows // ROW_TILE,),
        in_specs=[pl.BlockSpec((ROW_TILE // 2, lanes), lambda i: (i, 0))] * len(parts),
        out_specs=pl.BlockSpec((ROW_TILE, lanes // 2 * len(parts)), lambda i: (i, 0)),
        out_shape=jax.ShapeDtypeStruct((2 * rows, lanes // 2 * len(parts)), jnp.float32),
        compiler_params=pltpu.CompilerParams(vmem_limit_bytes=VMEM_LIMIT),
    )(*parts)


def solution(mesh):
    occ_size, vir_size = mesh.shape["occ"], mesh.shape["vir"]
    chips_z = vir_size // 2

    def send(array, target):
        pairs = [
            (o * vir_size + v, target(o, v)[0] * vir_size + target(o, v)[1])
            for o in range(occ_size)
            for v in range(vir_size)
        ]
        return lax.ppermute(array, ("occ", "vir"), pairs)

    to_x = functools.partial(send, target=lambda o, v: (o ^ 1, v))
    to_y = functools.partial(send, target=lambda o, v: (o ^ 2, v))
    to_core = functools.partial(send, target=lambda o, v: (o, v ^ 1))

    def body(amplitudes, integrals, ij_irrep, cd_irrep):
        depth, columns = integrals.shape
        width = columns // 2
        step = width // GRANULES
        bound = 2 * depth * AMPLITUDE_MAX * INTEGRAL_MAX
        scale = 2.0 ** math.floor(math.log2(HALF_MAX / bound))
        occ = lax.axis_index("occ").astype(jnp.int32).reshape(1)
        core = lax.axis_index("vir") % 2

        mine = lax.dynamic_slice_in_dim(integrals, core * width, width, axis=1)
        theirs = lax.dynamic_slice_in_dim(integrals, (1 - core) * width, width, axis=1)
        swapped = to_core(theirs)
        own_amps = masked_amplitudes(amplitudes, ij_irrep, cd_irrep)
        other_amps = to_core(own_amps)

        received = []
        for g in range(GRANULES):
            cut = slice(g * step, (g + 1) * step)
            own = jnp.concatenate([mine[:, cut], swapped[:, cut]], axis=1)
            top, bottom = own[: depth // 2], own[depth // 2 :]
            if g < GRANULES - 1:
                from_x, from_y = to_x(own), to_y(own)
                x_halves = [(from_x, 0), (from_x, 1)]
                y_halves = [(from_y, 0), (from_y, 1)]
                x_top, y_bottom = from_x[: depth // 2], from_y[depth // 2 :]
            else:
                x_top, y_bottom = to_x(top), to_y(bottom)
                x_halves = [(x_top, 0), (to_x(bottom), 0)]
                y_halves = [(to_y(top), 0), (y_bottom, 0)]
            far = [(to_y(x_top), 0), (to_x(y_bottom), 0)]
            halves = [(own, 0), (own, 1)] + x_halves + y_halves + far
            partials = product(occ, own_amps, other_amps, halves, scale)
            groups = [[z * 2 + k for z in range(chips_z)] for k in range(2)]
            arrived = lax.all_to_all(
                partials.astype(jnp.float16), "vir", 0, 0, axis_index_groups=groups, tiled=True
            )
            received.append(arrived.astype(jnp.float32).sum(axis=0))
        return total(received, 1.0 / scale)

    special = occ_size == 4 and vir_size == 8
    in_specs = (P("occ", "vir"), P("vir", "occ"), P("occ"), P("vir"))
    return jax.shard_map(
        body if special else plain_body,
        mesh=mesh,
        in_specs=in_specs,
        out_specs=P("occ", "vir"),
        check_vma=False,
    )
```

time: 211 us -> 129 us (0.61)
  waiting for transfers between devices: 183 us -> 38.8 us
  starting transfers between devices: 0.04 us -> 43 us
  Pallas kernels: 0 us -> 27.4 us
  matrix products: 14.5 us -> 0 us
  other arithmetic: 0 us -> 13.6 us
  between operations: 13.4 us -> 0.13 us
  local copies, waits for them, and re-layouts: 0 us -> 5.74 us
    all_gather x1 -> x0, waiting for transfers between devices: 92.1 us -> none  [body(): lax.all_gather(integrals, 'occ', axis=1, tiled=True)]
    reduce_scatter x1 -> x0, waiting for transfers between devices: 89.8 us -> none  [body(): lax.psum_scatter(partial_sums, 'vir', scatter_dimension=1, tiled=True)]
    ppermute x0 -> x20, waiting for transfers between devices: none -> 30.9 us  [send(): return lax.ppermute(array, ('occ', 'vir'), pairs)]
    pallas_call x0 -> x5, Pallas kernels: none -> 27.4 us  [the longest x4 25.4 us: product(): pl.pallas_call(functools.partial(product_kernel, scale), grid=(rows // RO...]
    ppermute x0 -> x20, starting transfers between devices: none -> 23.1 us  [send(): return lax.ppermute(array, ('occ', 'vir'), pairs)]
    all_to_all x0 -> x4, starting transfers between devices: none -> 19.9 us  [body(): lax.all_to_all(partials.astype(jnp.float16), 'vir', 0, 0, axis_index_grou...]
    dot_general x1 -> x0, matrix products: 14.5 us -> none  [body(): jnp.dot(masked, lax.all_gather(integrals, 'occ', axis=1, tiled=True), pre...]
    all_to_all x0 -> x4, waiting for transfers between devices: none -> 7.94 us  [body(): lax.all_to_all(partials.astype(jnp.float16), 'vir', 0, 0, axis_index_grou...]
  transfers between devices with their start and end apart: 2 -> 24, of which waited for: 2 -> 12; matrix products, arithmetic and copies ran while one was open for 0% -> 12% of each run, Pallas kernels for 0% -> 20%
where the time goes in v1:
time: 129 us
  starting transfers between devices  43 us (33%)
  waiting for transfers between devices  38.8 us (30%)
  Pallas kernels  27.4 us (21%)
  other arithmetic  13.6 us (11%)
  local copies, waits for them, and re-layouts  5.74 us (4%)
    ppermute x20, waiting for transfers between devices, send(): return lax.ppermute(array, ('occ', 'vir'), pairs)  30.9 us
    pallas_call x4, Pallas kernels, product(): pl.pallas_call(functools.partial(product_kernel, scale), grid=(rows // RO...  25.4 us
    ppermute x20, starting transfers between devices, send(): return lax.ppermute(array, ('occ', 'vir'), pairs)  23.1 us
    all_to_all x4, starting transfers between devices, body(): lax.all_to_all(partials.astype(jnp.float16), 'vir', 0, 0, axis_index_grou...  19.9 us
    all_to_all x4, waiting for transfers between devices, body(): lax.all_to_all(partials.astype(jnp.float16), 'vir', 0, 0, axis_index_grou...  7.94 us
    slice x2, local copies, waits for them, and re-layouts, body(): own = jnp.concatenate([mine[:, cut], swapped[:, cut]], axis=1)  4.58 us
    select_n x1, other arithmetic, masked_amplitudes(): jnp.where(ij_irrep[:, None] == cd_irrep[None, :], amplitudes, jnp.zeros_l...  4.31 us
    convert_element_type x4, other arithmetic, body(): partials.astype(jnp.float16)  3.48 us
  transfers between devices with their start and end apart: 24, of which 12 were waited for; matrix products, arithmetic and copies ran while one was open for 12% of the time, Pallas kernels for 20%

profile of v1, /device:TPU:0, one launch (start us, length us, event | category | flops | bytes accessed | tf_op | source)
XLA Modules:
  0.0 128.7 jit_solution(4920860874142379180)
XLA Ops:
  0.0 4.3 %compare_select_fusion.own_amps = bf16[1024,2048]{1,0:T(8,128)(2,1)} fusion(bf16[1024,2048]{1,0:T(8,128)(2,1)} %param.4, s32[2048]{0:T(1024)} %param.7, s32[1024]{0:T(1024)} %param.6), kind=kLoop, calls=%fused_computation | loop fusion | flops 4194304 | bytes 8400896 | tf_op jit(solution)/shard_map/jit(_where)/select_n | solution.py:20
  4.8 1.0 constant_dynamic-slice_fusion.3
  5.9 1.6 %constant_dynamic-slice_fusion.4 = (bf16[2048,64]{1,0:T(8,128)(2,1)S(1)}, bf16[2048,64]{1,0:T(8,128)(2,1)}, bf16[2048,64]{1,0:T(8,128)(2,1)S(1)}, bf16[2048,64]{1,0:T(8,128)(2,1)}) fusion(bf16[2048,512]{1,0:T(8,128)(2,1)S(1)} %copy-done, s32[]{:T(128)S(6)} %add.15, s32[]{:T(128)S(6)} %add.14, s32[]{:T(128)S(6)} %add.13, s32[]{:T(128)S(6)} %select_n.19), kind=kLoop, calls=%fused_computation.19 | loop fusion | bytes 2097168 | tf_op jit(solution)/shard_map/slice | solution.py:137
  7.5 5.9 %collective-permute-done.1 = bf16[2048,256]{1,0:T(8,128)(2,1)} collective-permute-done((bf16[2048,256]{1,0:T(8,128)(2,1)}, bf16[2048,256]{1,0:T(8,128)(2,1)}, u32[]{:S(2)}, u32[]{:S(2)}) %collective-permute-start.1) | collective-permute-done | bytes 1048608 | tf_op jit(solution)/shard_map/ppermute | solution.py:113
  13.4 3.0 %fusion.2 = (bf16[2048,64]{1,0:T(8,128)(2,1)S(1)}, bf16[2048,64]{1,0:T(8,128)(2,1)S(1)}, bf16[2048,64]{1,0:T(8,128)(2,1)}, bf16[2048,64]{1,0:T(8,128)(2,1)}) fusion(bf16[2048,256]{1,0:T(8,128)(2,1)} %collective-permute-done.1), kind=kLoop, calls=%fused_computation.20 | loop fusion | bytes 2097152 | tf_op jit(solution)/shard_map/slice | solution.py:137
  16.4 1.0 fusion.1
  17.4 2.9 %collective-permute-start.14 = (bf16[1024,128]{1,0:T(8,128)(2,1)S(1)}, bf16[1024,128]{1,0:T(8,128)(2,1)S(1)}, u32[]{:S(2)}, u32[]{:S(2)}) collective-permute-start(bf16[1024,128]{1,0:T(8,128)(2,1)S(1)} %get-tuple-element.10), channel_id=1, source_target_pairs={{0,8},{1,9},{2,10},{3,11},{4,12},{5,13},{6,14},{7,15},{8,0},{9,1},... | collective-permute-start | bytes 786440 | tf_op jit(solution)/shard_map/ppermute | solution.py:113
  20.2 1.6 %collective-permute-start.17 = (bf16[1024,128]{1,0:T(8,128)(2,1)}, bf16[1024,128]{1,0:T(8,128)(2,1)S(1)}, u32[]{:S(2)}, u32[]{:S(2)}) collective-permute-start(bf16[1024,128]{1,0:T(8,128)(2,1)} %get-tuple-element.9), channel_id=1, source_target_pairs={{0,16},{1,17},{2,18},{3,19},{4,20},{5,21},{6,22},{7,23},{8,24},{9,... | collective-permute-start | bytes 786440 | tf_op jit(solution)/shard_map/ppermute | solution.py:113
  21.8 0.5 collective-permute-start.15
  22.3 5.0 %collective-permute-done.14.refs_2_ = bf16[1024,128]{1,0:T(8,128)(2,1)S(1)} collective-permute-done((bf16[1024,128]{1,0:T(8,128)(2,1)S(1)}, bf16[1024,128]{1,0:T(8,128)(2,1)S(1)}, u32[]{:S(2)}, u32[]{:S(2)}) %collective-permute-start.14) | collective-permute-done | bytes 262176 | tf_op jit(solution)/shard_map/ppermute | solution.py:113
  27.3 2.1 %collective-permute-start.18 = (bf16[1024,128]{1,0:T(8,128)(2,1)S(1)}, bf16[1024,128]{1,0:T(8,128)(2,1)S(1)}, u32[]{:S(2)}, u32[]{:S(2)}) collective-permute-start(bf16[1024,128]{1,0:T(8,128)(2,1)S(1)} %collective-permute-done.14.refs_2_), channel_id=1, source_target_pairs={{0,16},{1,17},{2,18},{3,19},{4,20},{5,21},{6,22},{7,23},{8,24},{9,... | collective-permute-start | bytes 786440 | tf_op jit(solution)/shard_map/ppermute | solution.py:113
  29.6 1.3 %collective-permute-start.19 = (bf16[1024,128]{1,0:T(8,128)(2,1)S(1)}, bf16[1024,128]{1,0:T(8,128)(2,1)S(1)}, u32[]{:S(2)}, u32[]{:S(2)}) collective-permute-start(bf16[1024,128]{1,0:T(8,128)(2,1)S(1)} %collective-permute-done.17.refs_5_), channel_id=1, source_target_pairs={{0,8},{1,9},{2,10},{3,11},{4,12},{5,13},{6,14},{7,15},{8,0},{9,1},... | collective-permute-start | bytes 786440 | tf_op jit(solution)/shard_map/ppermute | solution.py:113
  31.6 1.4 %collective-permute-done.15.refs_3_ = bf16[1024,128]{1,0:T(8,128)(2,1)S(1)} collective-permute-done((bf16[1024,128]{1,0:T(8,128)(2,1)}, bf16[1024,128]{1,0:T(8,128)(2,1)S(1)}, u32[]{:S(2)}, u32[]{:S(2)}) %collective-permute-start.15) | collective-permute-done | bytes 262176 | tf_op jit(solution)/shard_map/ppermute | solution.py:113
  32.9 2.1 %collective-permute-start.10 = (bf16[2048,128]{1,0:T(8,128)(2,1)S(1)}, bf16[2048,128]{1,0:T(8,128)(2,1)S(1)}, u32[]{:S(2)}, u32[]{:S(2)}) collective-permute-start(bf16[2048,128]{1,0:T(8,128)(2,1)S(1)} %pad_maximum_fusion.2.refs_0_.refs_1_), channel_id=1, source_target_pairs={{0,8},{1,9},{2,10},{3,11},{4,12},{5,13},{6,14},{7,15},{8,0},{9,1},... | collective-permute-start | bytes 1572872 | tf_op jit(solution)/shard_map/ppermute | solution.py:113
  35.3 1.6 %collective-permute-start.11 = (bf16[2048,128]{1,0:T(8,128)(2,1)S(1)}, bf16[2048,128]{1,0:T(8,128)(2,1)S(1)}, u32[]{:S(2)}, u32[]{:S(2)}) collective-permute-start(bf16[2048,128]{1,0:T(8,128)(2,1)S(1)} %pad_maximum_fusion.2.refs_0_.refs_1_), channel_id=1, source_target_pairs={{0,16},{1,17},{2,18},{3,19},{4,20},{5,21},{6,22},{7,23},{8,24},{9,... | collective-permute-start | bytes 1572872 | tf_op jit(solution)/shard_map/ppermute | solution.py:113
  36.8 4.1 %collective-permute-done.18.refs_6_ = bf16[1024,128]{1,0:T(8,128)(2,1)S(1)} collective-permute-done((bf16[1024,128]{1,0:T(8,128)(2,1)S(1)}, bf16[1024,128]{1,0:T(8,128)(2,1)S(1)}, u32[]{:S(2)}, u32[]{:S(2)}) %collective-permute-start.18) | collective-permute-done | bytes 262176 | tf_op jit(solution)/shard_map/ppermute | solution.py:113
  40.9 6.4 %shard_map.49 = f32[4,512,128]{2,1,0:T(8,128)S(1)} custom-call(s32[1]{0:T(128)} %bitcast.occ_ref, bf16[1024,2048]{1,0:T(8,128)(2,1)} %compare_select_fusion.own_amps, bf16[1024,2048]{1,0:T(8,128)(2,1)} %collective-permute-done.other_amps, bf16[2048,128]{1,0:T(8,128)(2,1)S(1)} %pad_maximum_fusion.3.refs_0_.refs_1_, ...), custom_call_target="tpu_custom_call" | custom-call | flops 2147483648 | bytes 8388608 | tf_op jit(solution)/shard_map/pallas_call | solution.py:67
  47.3 0.9 convert_element_type.30
  48.2 4.9 %all-to-all-start.3 = ((f16[4,512,128]{2,1,0:T(8,128)(2,1)}), f16[4,512,128]{2,1,0:T(8,128)(2,1)}, u32[]{:S(2)}, u32[]{:S(2)}) async-start(f16[4,512,128]{2,1,0:T(8,128)(2,1)} %convert_element_type.30), calls=%async_computation.3 | async-start | bytes 1048576 | tf_op jit(solution)/shard_map/all_to_all | solution.py:152
  53.1 1.6 %collective-permute-start.12 = (bf16[1024,128]{1,0:T(8,128)(2,1)S(1)}, bf16[1024,128]{1,0:T(8,128)(2,1)S(1)}, u32[]{:S(2)}, u32[]{:S(2)}) collective-permute-start(bf16[1024,128]{1,0:T(8,128)(2,1)S(1)} %slice.71), channel_id=1, source_target_pairs={{0,16},{1,17},{2,18},{3,19},{4,20},{5,21},{6,22},{7,23},{8,24},{9,... | collective-permute-start | bytes 786440 | tf_op jit(solution)/shard_map/ppermute | solution.py:113
  54.7 0.6 collective-permute-start.13
  55.6 1.6 %collective-permute-start.6 = (bf16[2048,128]{1,0:T(8,128)(2,1)S(1)}, bf16[2048,128]{1,0:T(8,128)(2,1)S(1)}, u32[]{:S(2)}, u32[]{:S(2)}) collective-permute-start(bf16[2048,128]{1,0:T(8,128)(2,1)S(1)} %pad_maximum_fusion.1.refs_0_.refs_1_), channel_id=1, source_target_pairs={{0,8},{1,9},{2,10},{3,11},{4,12},{5,13},{6,14},{7,15},{8,0},{9,1},... | collective-permute-start | bytes 1572872 | tf_op jit(solution)/shard_map/ppermute | solution.py:113
  57.1 0.5 collective-permute-start.7
  57.6 4.7 %collective-permute-done.12.refs_6_ = bf16[1024,128]{1,0:T(8,128)(2,1)S(1)} collective-permute-done((bf16[1024,128]{1,0:T(8,128)(2,1)S(1)}, bf16[1024,128]{1,0:T(8,128)(2,1)S(1)}, u32[]{:S(2)}, u32[]{:S(2)}) %collective-permute-start.12) | collective-permute-done | bytes 262176 | tf_op jit(solution)/shard_map/ppermute | solution.py:113
  62.3 1.7 %collective-permute-done.13.refs_7_ = bf16[1024,128]{1,0:T(8,128)(2,1)S(1)} collective-permute-done((bf16[1024,128]{1,0:T(8,128)(2,1)S(1)}, bf16[1024,128]{1,0:T(8,128)(2,1)S(1)}, u32[]{:S(2)}, u32[]{:S(2)}) %collective-permute-start.13) | collective-permute-done | bytes 262176 | tf_op jit(solution)/shard_map/ppermute | solution.py:113
  64.0 6.3 %shard_map.48 = f32[4,512,128]{2,1,0:T(8,128)S(1)} custom-call(s32[1]{0:T(128)} %bitcast.occ_ref, bf16[1024,2048]{1,0:T(8,128)(2,1)} %compare_select_fusion.own_amps, bf16[1024,2048]{1,0:T(8,128)(2,1)} %collective-permute-done.other_amps, bf16[2048,128]{1,0:T(8,128)(2,1)S(1)} %pad_maximum_fusion.2.refs_0_.refs_1_, ...), custom_call_target="tpu_custom_call" | custom-call | flops 2147483648 | bytes 8388608 | tf_op jit(solution)/shard_map/pallas_call | solution.py:67
  70.3 0.9 convert_element_type.28
  71.2 5.1 %all-to-all-start.2 = ((f16[4,512,128]{2,1,0:T(8,128)(2,1)}), f16[4,512,128]{2,1,0:T(8,128)(2,1)}, u32[]{:S(2)}, u32[]{:S(2)}) async-start(f16[4,512,128]{2,1,0:T(8,128)(2,1)} %convert_element_type.28), calls=%async_computation.2 | async-start | bytes 1048576 | tf_op jit(solution)/shard_map/all_to_all | solution.py:152
  76.3 0.6 collective-permute-start.8
  76.9 0.6 collective-permute-start.9
  77.5 1.5 %pad_maximum_fusion.refs_0_.refs_1_ = bf16[2048,128]{1,0:T(8,128)(2,1)S(1)} fusion(bf16[2048,64]{1,0:T(8,128)(2,1)} %get-tuple-element.14, bf16[2048,64]{1,0:T(8,128)(2,1)} %get-tuple-element.8), kind=kLoop, calls=%fused_computation.5 | loop fusion | flops 1048576 | bytes 1048576 | tf_op jit(solution)/shard_map/concatenate | solution.py:137
  79.0 1.6 %collective-permute-start.2 = (bf16[2048,128]{1,0:T(8,128)(2,1)S(1)}, bf16[2048,128]{1,0:T(8,128)(2,1)S(1)}, u32[]{:S(2)}, u32[]{:S(2)}) collective-permute-start(bf16[2048,128]{1,0:T(8,128)(2,1)S(1)} %pad_maximum_fusion.refs_0_.refs_1_), channel_id=1, source_target_pairs={{0,8},{1,9},{2,10},{3,11},{4,12},{5,13},{6,14},{7,15},{8,0},{9,1},... | collective-permute-start | bytes 1572872 | tf_op jit(solution)/shard_map/ppermute | solution.py:113
  80.6 1.5 %collective-permute-start.3 = (bf16[2048,128]{1,0:T(8,128)(2,1)S(1)}, bf16[2048,128]{1,0:T(8,128)(2,1)S(1)}, u32[]{:S(2)}, u32[]{:S(2)}) collective-permute-start(bf16[2048,128]{1,0:T(8,128)(2,1)S(1)} %pad_maximum_fusion.refs_0_.refs_1_), channel_id=1, source_target_pairs={{0,16},{1,17},{2,18},{3,19},{4,20},{5,21},{6,22},{7,23},{8,24},{9,... | collective-permute-start | bytes 1572872 | tf_op jit(solution)/shard_map/ppermute | solution.py:113
  82.1 1.8 %collective-permute-done.8.refs_6_ = bf16[1024,128]{1,0:T(8,128)(2,1)S(1)} collective-permute-done((bf16[1024,128]{1,0:T(8,128)(2,1)S(1)}, bf16[1024,128]{1,0:T(8,128)(2,1)S(1)}, u32[]{:S(2)}, u32[]{:S(2)}) %collective-permute-start.8) | collective-permute-done | bytes 262176 | tf_op jit(solution)/shard_map/ppermute | solution.py:113
  83.9 6.3 %shard_map.47 = f32[4,512,128]{2,1,0:T(8,128)S(1)} custom-call(s32[1]{0:T(128)} %bitcast.occ_ref, bf16[1024,2048]{1,0:T(8,128)(2,1)} %compare_select_fusion.own_amps, bf16[1024,2048]{1,0:T(8,128)(2,1)} %collective-permute-done.other_amps, bf16[2048,128]{1,0:T(8,128)(2,1)S(1)} %pad_maximum_fusion.1.refs_0_.refs_1_, ...), custom_call_target="tpu_custom_call" | custom-call | flops 2147483648 | bytes 8388608 | tf_op jit(solution)/shard_map/pallas_call | solution.py:67
  90.2 0.9 convert_element_type.26
  91.1 4.8 %all-to-all-start.1 = ((f16[4,512,128]{2,1,0:T(8,128)(2,1)}), f16[4,512,128]{2,1,0:T(8,128)(2,1)S(1)}, u32[]{:S(2)}, u32[]{:S(2)}) async-start(f16[4,512,128]{2,1,0:T(8,128)(2,1)} %convert_element_type.26), calls=%async_computation.1 | async-start | bytes 1048576 | tf_op jit(solution)/shard_map/all_to_all | solution.py:152
  95.9 1.6 %collective-permute-start.4 = (bf16[1024,128]{1,0:T(8,128)(2,1)S(1)}, bf16[1024,128]{1,0:T(8,128)(2,1)S(1)}, u32[]{:S(2)}, u32[]{:S(2)}) collective-permute-start(bf16[1024,128]{1,0:T(8,128)(2,1)S(1)} %slice.65), channel_id=1, source_target_pairs={{0,16},{1,17},{2,18},{3,19},{4,20},{5,21},{6,22},{7,23},{8,24},{9,... | collective-permute-start | bytes 786440 | tf_op jit(solution)/shard_map/ppermute | solution.py:113
  97.6 0.6 collective-permute-start.5
  98.2 4.2 %collective-permute-done.4.refs_6_ = bf16[1024,128]{1,0:T(8,128)(2,1)S(1)} collective-permute-done((bf16[1024,128]{1,0:T(8,128)(2,1)S(1)}, bf16[1024,128]{1,0:T(8,128)(2,1)S(1)}, u32[]{:S(2)}, u32[]{:S(2)}) %collective-permute-start.4) | collective-permute-done | bytes 262176 | tf_op jit(solution)/shard_map/ppermute | solution.py:113
  102.4 1.6 %collective-permute-done.5.refs_7_ = bf16[1024,128]{1,0:T(8,128)(2,1)S(1)} collective-permute-done((bf16[1024,128]{1,0:T(8,128)(2,1)S(1)}, bf16[1024,128]{1,0:T(8,128)(2,1)S(1)}, u32[]{:S(2)}, u32[]{:S(2)}) %collective-permute-start.5) | collective-permute-done | bytes 262176 | tf_op jit(solution)/shard_map/ppermute | solution.py:113
  104.0 6.3 %shard_map.46 = f32[4,512,128]{2,1,0:T(8,128)S(1)} custom-call(s32[1]{0:T(128)} %bitcast.occ_ref, bf16[1024,2048]{1,0:T(8,128)(2,1)} %compare_select_fusion.own_amps, bf16[1024,2048]{1,0:T(8,128)(2,1)} %collective-permute-done.other_amps, bf16[2048,128]{1,0:T(8,128)(2,1)S(1)} %pad_maximum_fusion.refs_0_.refs_1_, ...), custom_call_target="tpu_custom_call" | custom-call | flops 2147483648 | bytes 8388608 | tf_op jit(solution)/shard_map/pallas_call | solution.py:67
  110.3 0.9 convert_element_type.24
  111.2 5.1 %all-to-all-start = ((f16[4,512,128]{2,1,0:T(8,128)(2,1)}), f16[4,512,128]{2,1,0:T(8,128)(2,1)S(1)}, u32[]{:S(2)}, u32[]{:S(2)}) async-start(f16[4,512,128]{2,1,0:T(8,128)(2,1)} %convert_element_type.24), calls=%async_computation | async-start | bytes 1048576 | tf_op jit(solution)/shard_map/all_to_all | solution.py:152
  116.3 1.1 convert_reduce_fusion.refs_3_
  117.4 1.1 convert_reduce_fusion.1.refs_2_
  118.7 7.9 %all-to-all-done = f16[4,512,128]{2,1,0:T(8,128)(2,1)S(1)} async-done(((f16[4,512,128]{2,1,0:T(8,128)(2,1)}), f16[4,512,128]{2,1,0:T(8,128)(2,1)S(1)}, u32[]{:S(2)}, u32[]{:S(2)}) %all-to-all-start) | async-done | bytes 524320 | tf_op jit(solution)/shard_map/all_to_all | solution.py:152
  126.7 2.0 %shard_map.50 = f32[1024,256]{1,0:T(8,128)} custom-call(f32[512,128]{1,0:T(8,128)S(1)} %convert_reduce_fusion.3.refs_0_, f32[512,128]{1,0:T(8,128)S(1)} %convert_reduce_fusion.2.refs_1_, f32[512,128]{1,0:T(8,128)S(1)} %convert_reduce_fusion.1.refs_2_, f32[512,128]{1,0:T(8,128)S(1)} %convert_reduce_fusion.refs_3_), custom_call_target="tpu_custom_call" | custom-call | tf_op jit(solution)/shard_map/pallas_call | solution.py:93
  (34 shorter events, 2.1 us)
Async XLA Ops:
  0.0 4.8 %copy-start = (bf16[2048,512]{1,0:T(8,128)(2,1)S(1)}, bf16[2048,512]{1,0:T(8,128)(2,1)}, u32[]{:S(2)}) copy-start(bf16[2048,512]{1,0:T(8,128)(2,1)} %param.5) | copy-start | bytes 6291460
  4.3 36.6 %collective-permute-start = (bf16[1024,2048]{1,0:T(8,128)(2,1)}, bf16[1024,2048]{1,0:T(8,128)(2,1)}, u32[]{:S(2)}, u32[]{:S(2)}) collective-permute-start(bf16[1024,2048]{1,0:T(8,128)(2,1)} %compare_select_fusion.own_amps), channel_id=1, source_target_pairs={{0,1},{1,0},{2,3},{3,2},{4,5},{5,4},{6,7},{7,6},{8,9},{9,8},{10,11... | collective-permute-start | bytes 12582920 | tf_op jit(solution)/shard_map/ppermute | solution.py:113
  5.8 7.6 %collective-permute-start.1 = (bf16[2048,256]{1,0:T(8,128)(2,1)}, bf16[2048,256]{1,0:T(8,128)(2,1)}, u32[]{:S(2)}, u32[]{:S(2)}) collective-permute-start(bf16[2048,256]{1,0:T(8,128)(2,1)} %constant_dynamic-slice_fusion.3), channel_id=1, source_target_pairs={{0,1},{1,0},{2,3},{3,2},{4,5},{5,4},{6,7},{7,6},{8,9},{9,8},{10,11... | collective-permute-start | bytes 3145736 | tf_op jit(solution)/shard_map/ppermute | solution.py:113
  7.5 23.8 %copy-start.2 = (bf16[2048,64]{1,0:T(8,128)(2,1)S(1)}, bf16[2048,64]{1,0:T(8,128)(2,1)}, u32[]{:S(2)}) copy-start(bf16[2048,64]{1,0:T(8,128)(2,1)} %get-tuple-element.6) | copy-start | bytes 786436
  17.4 9.9 %collective-permute-start.14 = (bf16[1024,128]{1,0:T(8,128)(2,1)S(1)}, bf16[1024,128]{1,0:T(8,128)(2,1)S(1)}, u32[]{:S(2)}, u32[]{:S(2)}) collective-permute-start(bf16[1024,128]{1,0:T(8,128)(2,1)S(1)} %get-tuple-element.10), channel_id=1, source_target_pairs={{0,8},{1,9},{2,10},{3,11},{4,12},{5,13},{6,14},{7,15},{8,0},{9,1},... | collective-permute-start | bytes 786440 | tf_op jit(solution)/shard_map/ppermute | solution.py:113
  20.2 9.4 %collective-permute-start.17 = (bf16[1024,128]{1,0:T(8,128)(2,1)}, bf16[1024,128]{1,0:T(8,128)(2,1)S(1)}, u32[]{:S(2)}, u32[]{:S(2)}) collective-permute-start(bf16[1024,128]{1,0:T(8,128)(2,1)} %get-tuple-element.9), channel_id=1, source_target_pairs={{0,16},{1,17},{2,18},{3,19},{4,20},{5,21},{6,22},{7,23},{8,24},{9,... | collective-permute-start | bytes 786440 | tf_op jit(solution)/shard_map/ppermute | solution.py:113
  21.8 11.2 %collective-permute-start.15 = (bf16[1024,128]{1,0:T(8,128)(2,1)}, bf16[1024,128]{1,0:T(8,128)(2,1)S(1)}, u32[]{:S(2)}, u32[]{:S(2)}) collective-permute-start(bf16[1024,128]{1,0:T(8,128)(2,1)} %get-tuple-element.9), channel_id=1, source_target_pairs={{0,8},{1,9},{2,10},{3,11},{4,12},{5,13},{6,14},{7,15},{8,0},{9,1},... | collective-permute-start | bytes 786440 | tf_op jit(solution)/shard_map/ppermute | solution.py:113
  22.3 13.0 %collective-permute-start.16 = (bf16[1024,128]{1,0:T(8,128)(2,1)S(1)}, bf16[1024,128]{1,0:T(8,128)(2,1)S(1)}, u32[]{:S(2)}, u32[]{:S(2)}) collective-permute-start(bf16[1024,128]{1,0:T(8,128)(2,1)S(1)} %get-tuple-element.10), channel_id=1, source_target_pairs={{0,16},{1,17},{2,18},{3,19},{4,20},{5,21},{6,22},{7,23},{8,24},{9,... | collective-permute-start | bytes 786440 | tf_op jit(solution)/shard_map/ppermute | solution.py:113
  27.3 13.6 %collective-permute-start.18 = (bf16[1024,128]{1,0:T(8,128)(2,1)S(1)}, bf16[1024,128]{1,0:T(8,128)(2,1)S(1)}, u32[]{:S(2)}, u32[]{:S(2)}) collective-permute-start(bf16[1024,128]{1,0:T(8,128)(2,1)S(1)} %collective-permute-done.14.refs_2_), channel_id=1, source_target_pairs={{0,16},{1,17},{2,18},{3,19},{4,20},{5,21},{6,22},{7,23},{8,24},{9,... | collective-permute-start | bytes 786440 | tf_op jit(solution)/shard_map/ppermute | solution.py:113
  29.6 11.2 %collective-permute-start.19 = (bf16[1024,128]{1,0:T(8,128)(2,1)S(1)}, bf16[1024,128]{1,0:T(8,128)(2,1)S(1)}, u32[]{:S(2)}, u32[]{:S(2)}) collective-permute-start(bf16[1024,128]{1,0:T(8,128)(2,1)S(1)} %collective-permute-done.17.refs_5_), channel_id=1, source_target_pairs={{0,8},{1,9},{2,10},{3,11},{4,12},{5,13},{6,14},{7,15},{8,0},{9,1},... | collective-permute-start | bytes 786440 | tf_op jit(solution)/shard_map/ppermute | solution.py:113
  32.9 20.1 %collective-permute-start.10 = (bf16[2048,128]{1,0:T(8,128)(2,1)S(1)}, bf16[2048,128]{1,0:T(8,128)(2,1)S(1)}, u32[]{:S(2)}, u32[]{:S(2)}) collective-permute-start(bf16[2048,128]{1,0:T(8,128)(2,1)S(1)} %pad_maximum_fusion.2.refs_0_.refs_1_), channel_id=1, source_target_pairs={{0,8},{1,9},{2,10},{3,11},{4,12},{5,13},{6,14},{7,15},{8,0},{9,1},... | collective-permute-start | bytes 1572872 | tf_op jit(solution)/shard_map/ppermute | solution.py:113
  35.3 19.4 %collective-permute-start.11 = (bf16[2048,128]{1,0:T(8,128)(2,1)S(1)}, bf16[2048,128]{1,0:T(8,128)(2,1)S(1)}, u32[]{:S(2)}, u32[]{:S(2)}) collective-permute-start(bf16[2048,128]{1,0:T(8,128)(2,1)S(1)} %pad_maximum_fusion.2.refs_0_.refs_1_), channel_id=1, source_target_pairs={{0,16},{1,17},{2,18},{3,19},{4,20},{5,21},{6,22},{7,23},{8,24},{9,... | collective-permute-start | bytes 1572872 | tf_op jit(solution)/shard_map/ppermute | solution.py:113
  40.9 14.4 %copy-start.1 = (bf16[2048,64]{1,0:T(8,128)(2,1)S(1)}, bf16[2048,64]{1,0:T(8,128)(2,1)}, u32[]{:S(2)}) copy-start(bf16[2048,64]{1,0:T(8,128)(2,1)} %get-tuple-element.13) | copy-start | bytes 786436
  48.2 23.0 %all-to-all-start.3 = ((f16[4,512,128]{2,1,0:T(8,128)(2,1)}), f16[4,512,128]{2,1,0:T(8,128)(2,1)}, u32[]{:S(2)}, u32[]{:S(2)}) async-start(f16[4,512,128]{2,1,0:T(8,128)(2,1)} %convert_element_type.30), calls=%async_computation.3 | async-start | bytes 1048576 | tf_op jit(solution)/shard_map/all_to_all | solution.py:152
  53.1 9.2 %collective-permute-start.12 = (bf16[1024,128]{1,0:T(8,128)(2,1)S(1)}, bf16[1024,128]{1,0:T(8,128)(2,1)S(1)}, u32[]{:S(2)}, u32[]{:S(2)}) collective-permute-start(bf16[1024,128]{1,0:T(8,128)(2,1)S(1)} %slice.71), channel_id=1, source_target_pairs={{0,16},{1,17},{2,18},{3,19},{4,20},{5,21},{6,22},{7,23},{8,24},{9,... | collective-permute-start | bytes 786440 | tf_op jit(solution)/shard_map/ppermute | solution.py:113
  54.7 9.3 %collective-permute-start.13 = (bf16[1024,128]{1,0:T(8,128)(2,1)S(1)}, bf16[1024,128]{1,0:T(8,128)(2,1)S(1)}, u32[]{:S(2)}, u32[]{:S(2)}) collective-permute-start(bf16[1024,128]{1,0:T(8,128)(2,1)S(1)} %slice.72), channel_id=1, source_target_pairs={{0,8},{1,9},{2,10},{3,11},{4,12},{5,13},{6,14},{7,15},{8,0},{9,1},... | collective-permute-start | bytes 786440 | tf_op jit(solution)/shard_map/ppermute | solution.py:113
  55.6 20.7 %collective-permute-start.6 = (bf16[2048,128]{1,0:T(8,128)(2,1)S(1)}, bf16[2048,128]{1,0:T(8,128)(2,1)S(1)}, u32[]{:S(2)}, u32[]{:S(2)}) collective-permute-start(bf16[2048,128]{1,0:T(8,128)(2,1)S(1)} %pad_maximum_fusion.1.refs_0_.refs_1_), channel_id=1, source_target_pairs={{0,8},{1,9},{2,10},{3,11},{4,12},{5,13},{6,14},{7,15},{8,0},{9,1},... | collective-permute-start | bytes 1572872 | tf_op jit(solution)/shard_map/ppermute | solution.py:113
  57.1 19.8 %collective-permute-start.7 = (bf16[2048,128]{1,0:T(8,128)(2,1)S(1)}, bf16[2048,128]{1,0:T(8,128)(2,1)S(1)}, u32[]{:S(2)}, u32[]{:S(2)}) collective-permute-start(bf16[2048,128]{1,0:T(8,128)(2,1)S(1)} %pad_maximum_fusion.1.refs_0_.refs_1_), channel_id=1, source_target_pairs={{0,16},{1,17},{2,18},{3,19},{4,20},{5,21},{6,22},{7,23},{8,24},{9,... | collective-permute-start | bytes 1572872 | tf_op jit(solution)/shard_map/ppermute | solution.py:113
  71.2 19.9 %all-to-all-start.2 = ((f16[4,512,128]{2,1,0:T(8,128)(2,1)}), f16[4,512,128]{2,1,0:T(8,128)(2,1)}, u32[]{:S(2)}, u32[]{:S(2)}) async-start(f16[4,512,128]{2,1,0:T(8,128)(2,1)} %convert_element_type.28), calls=%async_computation.2 | async-start | bytes 1048576 | tf_op jit(solution)/shard_map/all_to_all | solution.py:152
  76.3 7.5 %collective-permute-start.8 = (bf16[1024,128]{1,0:T(8,128)(2,1)S(1)}, bf16[1024,128]{1,0:T(8,128)(2,1)S(1)}, u32[]{:S(2)}, u32[]{:S(2)}) collective-permute-start(bf16[1024,128]{1,0:T(8,128)(2,1)S(1)} %slice.68), channel_id=1, source_target_pairs={{0,16},{1,17},{2,18},{3,19},{4,20},{5,21},{6,22},{7,23},{8,24},{9,... | collective-permute-start | bytes 786440 | tf_op jit(solution)/shard_map/ppermute | solution.py:113
  76.9 7.0 %collective-permute-start.9 = (bf16[1024,128]{1,0:T(8,128)(2,1)S(1)}, bf16[1024,128]{1,0:T(8,128)(2,1)S(1)}, u32[]{:S(2)}, u32[]{:S(2)}) collective-permute-start(bf16[1024,128]{1,0:T(8,128)(2,1)S(1)} %slice.69), channel_id=1, source_target_pairs={{0,8},{1,9},{2,10},{3,11},{4,12},{5,13},{6,14},{7,15},{8,0},{9,1},... | collective-permute-start | bytes 786440 | tf_op jit(solution)/shard_map/ppermute | solution.py:113
  79.0 16.9 %collective-permute-start.2 = (bf16[2048,128]{1,0:T(8,128)(2,1)S(1)}, bf16[2048,128]{1,0:T(8,128)(2,1)S(1)}, u32[]{:S(2)}, u32[]{:S(2)}) collective-permute-start(bf16[2048,128]{1,0:T(8,128)(2,1)S(1)} %pad_maximum_fusion.refs_0_.refs_1_), channel_id=1, source_target_pairs={{0,8},{1,9},{2,10},{3,11},{4,12},{5,13},{6,14},{7,15},{8,0},{9,1},... | collective-permute-start | bytes 1572872 | tf_op jit(solution)/shard_map/ppermute | solution.py:113
  80.6 17.0 %collective-permute-start.3 = (bf16[2048,128]{1,0:T(8,128)(2,1)S(1)}, bf16[2048,128]{1,0:T(8,128)(2,1)S(1)}, u32[]{:S(2)}, u32[]{:S(2)}) collective-permute-start(bf16[2048,128]{1,0:T(8,128)(2,1)S(1)} %pad_maximum_fusion.refs_0_.refs_1_), channel_id=1, source_target_pairs={{0,16},{1,17},{2,18},{3,19},{4,20},{5,21},{6,22},{7,23},{8,24},{9,... | collective-permute-start | bytes 1572872 | tf_op jit(solution)/shard_map/ppermute | solution.py:113
  91.1 20.1 %all-to-all-start.1 = ((f16[4,512,128]{2,1,0:T(8,128)(2,1)}), f16[4,512,128]{2,1,0:T(8,128)(2,1)S(1)}, u32[]{:S(2)}, u32[]{:S(2)}) async-start(f16[4,512,128]{2,1,0:T(8,128)(2,1)} %convert_element_type.26), calls=%async_computation.1 | async-start | bytes 1048576 | tf_op jit(solution)/shard_map/all_to_all | solution.py:152
  95.9 6.4 %collective-permute-start.4 = (bf16[1024,128]{1,0:T(8,128)(2,1)S(1)}, bf16[1024,128]{1,0:T(8,128)(2,1)S(1)}, u32[]{:S(2)}, u32[]{:S(2)}) collective-permute-start(bf16[1024,128]{1,0:T(8,128)(2,1)S(1)} %slice.65), channel_id=1, source_target_pairs={{0,16},{1,17},{2,18},{3,19},{4,20},{5,21},{6,22},{7,23},{8,24},{9,... | collective-permute-start | bytes 786440 | tf_op jit(solution)/shard_map/ppermute | solution.py:113
  97.6 6.4 %collective-permute-start.5 = (bf16[1024,128]{1,0:T(8,128)(2,1)S(1)}, bf16[1024,128]{1,0:T(8,128)(2,1)S(1)}, u32[]{:S(2)}, u32[]{:S(2)}) collective-permute-start(bf16[1024,128]{1,0:T(8,128)(2,1)S(1)} %slice.66), channel_id=1, source_target_pairs={{0,8},{1,9},{2,10},{3,11},{4,12},{5,13},{6,14},{7,15},{8,0},{9,1},... | collective-permute-start | bytes 786440 | tf_op jit(solution)/shard_map/ppermute | solution.py:113
  111.2 15.4 %all-to-all-start = ((f16[4,512,128]{2,1,0:T(8,128)(2,1)}), f16[4,512,128]{2,1,0:T(8,128)(2,1)S(1)}, u32[]{:S(2)}, u32[]{:S(2)}) async-start(f16[4,512,128]{2,1,0:T(8,128)(2,1)} %convert_element_type.24), calls=%async_computation | async-start | bytes 1048576 | tf_op jit(solution)/shard_map/all_to_all | solution.py:152

commit v2 on v0

v2 whole, which is shorter than its diff:
```python
import functools
import math

import jax
import jax.numpy as jnp
from jax import lax
from jax.experimental import pallas as pl
from jax.experimental.pallas import tpu as pltpu
from jax.sharding import PartitionSpec as P

AMPLITUDE_MAX = 6.0
INTEGRAL_MAX = 0.1875
HALF_MAX = 65504.0
SHARES = (1, 1, 1, 1)
ORDER = (('near', 0), ('rest', 0), ('near', 1), ('far', 0), ('rest', 1), ('near', 2), ('far', 1), ('rest', 2), ('near', 3), ('far', 2), ('rest', 3), ('far', 3))
DEPTH = 4
STRICT = 1
ZMODE = ('pair', 'pair', 'pair', 'pair')
RAW_SWAP = True
SWAP_CUTS = 1
SWAP_WHOLE = True
LATE = False
GATES = {('far', 1): [('product', 0)], ('far', 2): [('product', 1)], ('rest', 3): [('pair', 0)], ('product', 2): [('pair', 1)], ('product', 3): [('product', 2)], ('near', 2): ['masked']}
ROW_TILE = 256
VMEM_LIMIT = 14680064


def masked_amplitudes(amplitudes, ij_irrep, cd_irrep):
    rows, columns = ij_irrep.astype(amplitudes.dtype), cd_irrep.astype(amplitudes.dtype)
    return jnp.where(rows[:, None] == columns[None, :], amplitudes, jnp.zeros_like(amplitudes))


def in_vmem(array):
    return pltpu.with_memory_space_constraint(array, pltpu.VMEM)


def plain_body(amplitudes, integrals, ij_irrep, cd_irrep):
    partial_sums = jnp.dot(
        masked_amplitudes(amplitudes, ij_irrep, cd_irrep),
        lax.all_gather(integrals, "occ", axis=1, tiled=True),
        preferred_element_type=jnp.float32,
    )
    return lax.psum_scatter(partial_sums, "vir", scatter_dimension=1, tiled=True)


def product_kernel(scale, slot_ref, own_amps, other_amps, *refs):
    pieces, out_ref, own_rows, other_rows = refs[:8], refs[8], refs[9], refs[10]
    depth, width = own_rows.shape[0], own_rows.shape[1] // 4
    folds = depth // pieces[0].shape[0]
    part = depth // folds
    for target, blocks in ((own_rows, pieces[0::2]), (other_rows, pieces[1::2])):
        for f in range(folds):
            cut = slice(f * width, (f + 1) * width)
            target[pl.ds(f * part, part), :] = jnp.concatenate([b[:, cut] for b in blocks], axis=1)

    for i in range(own_amps.shape[0] // ROW_TILE):
        at = pl.ds(i * ROW_TILE, ROW_TILE)
        sums = jnp.dot(own_amps[at, :], own_rows[...], preferred_element_type=jnp.float32)
        sums += jnp.dot(other_amps[at, :], other_rows[...], preferred_element_type=jnp.float32)
        sums = sums * scale
        rows = ROW_TILE // folds
        for relation in range(4):
            block = sums[:, relation * width : (relation + 1) * width]
            if folds > 1:
                block = jnp.concatenate([block[f * rows : (f + 1) * rows] for f in range(folds)], axis=1)
            out_ref[slot_ref[relation], pl.ds(i * rows, rows), :] = block


def product(slots, own_amps, other_amps, pieces, scale, depth):
    lanes = pieces[0].shape[1]
    folds = depth // pieces[0].shape[0]
    return pl.pallas_call(
        functools.partial(product_kernel, scale),
        in_specs=[pl.BlockSpec(memory_space=pltpu.SMEM)]
        + [pl.BlockSpec(memory_space=pltpu.VMEM)] * (2 + len(pieces)),
        out_specs=pl.BlockSpec(memory_space=pltpu.VMEM),
        out_shape=jax.ShapeDtypeStruct((4, own_amps.shape[0] // folds, lanes), jnp.float32),
        scratch_shapes=[pltpu.VMEM((depth, 4 * lanes // folds), jnp.bfloat16)] * 2,
        compiler_params=pltpu.CompilerParams(vmem_limit_bytes=VMEM_LIMIT),
        cost_estimate=pl.CostEstimate(flops=0, bytes_accessed=0, transcendentals=0),
    )(slots, own_amps, other_amps, *pieces)


def total_kernel(unscale, *refs):
    parts, out_ref = refs[:-1], refs[-1]
    rows = out_ref.shape[0]
    for i in range(rows // ROW_TILE):
        columns = []
        for part in parts:
            folds = rows // part.shape[0]
            tile = ROW_TILE // folds
            total = part[pl.ds(i * tile, tile), :] * unscale
            width = total.shape[1] // folds
            if folds > 1:
                total = jnp.concatenate([total[:, f * width : (f + 1) * width] for f in range(folds)], axis=0)
            columns.append(total)
        out_ref[pl.ds(i * ROW_TILE, ROW_TILE), :] = jnp.concatenate(columns, axis=1)


def total(parts, unscale, rows, columns):
    return pl.pallas_call(
        functools.partial(total_kernel, unscale),
        in_specs=[pl.BlockSpec(memory_space=pltpu.VMEM)] * len(parts),
        out_specs=pl.BlockSpec(memory_space=pltpu.VMEM),
        out_shape=jax.ShapeDtypeStruct((rows, columns), jnp.float32),
        compiler_params=pltpu.CompilerParams(vmem_limit_bytes=VMEM_LIMIT),
        cost_estimate=pl.CostEstimate(flops=0, bytes_accessed=0, transcendentals=0),
    )(*parts)


def solution(mesh):
    occ_size, vir_size = mesh.shape["occ"], mesh.shape["vir"]
    chips_z = vir_size // 2

    def send(array, target):
        pairs = [
            (o * vir_size + v, target(o, v)[0] * vir_size + target(o, v)[1])
            for o in range(occ_size)
            for v in range(vir_size)
        ]
        return lax.ppermute(array, ("occ", "vir"), pairs)

    to_x = functools.partial(send, target=lambda o, v: (o ^ 1, v))
    to_y = functools.partial(send, target=lambda o, v: (o ^ 2, v))
    to_x_across = functools.partial(send, target=lambda o, v: (o ^ 1, v ^ 1))
    to_y_across = functools.partial(send, target=lambda o, v: (o ^ 2, v ^ 1))
    to_core = functools.partial(send, target=lambda o, v: (o, v ^ 1))

    def along_z(array, hop):
        return send(array, lambda o, v: (o, v ^ (2 * hop)))

    def body(amplitudes, integrals, ij_irrep, cd_irrep):
        depth, columns = integrals.shape
        width = columns // 2
        bound = 2 * depth * AMPLITUDE_MAX * INTEGRAL_MAX
        scale = 2.0 ** math.floor(math.log2(HALF_MAX / bound))
        core = lax.axis_index("vir") % 2
        chip = lax.axis_index("vir") // 2
        owners = lax.axis_index("occ") ^ jnp.arange(4, dtype=jnp.int32)
        hops = owners ^ chip
        ends = [width * sum(SHARES[: g + 1]) // sum(SHARES) for g in range(len(SHARES))]
        granules = range(len(SHARES))

        def piece(array, g):
            cut = array[:, (ends[g - 1] if g else 0) : ends[g]]
            if cut.shape[1] % 128 == 0:
                return cut
            folds = 128 // cut.shape[1]
            return jnp.concatenate(jnp.split(cut, folds), axis=1)

        def columns_of(array, which):
            return lax.dynamic_slice_in_dim(array, which * width, width, axis=1)

        first = (piece(columns_of(integrals, core), 0), piece(columns_of(integrals, 1 - core), 0))
        first, integrals = lax.optimization_barrier((first, integrals))
        mine, theirs = columns_of(integrals, core), columns_of(integrals, 1 - core)
        theirs_late, cd_late = theirs, cd_irrep
        if RAW_SWAP:
            cut = amplitudes.shape[0] // SWAP_CUTS
            chunks = [to_core(amplitudes[at : at + cut]) for at in range(0, amplitudes.shape[0], cut)]
            other_raw = jnp.concatenate(chunks, axis=0) if SWAP_CUTS > 1 else chunks[0]
            if LATE:
                theirs_late, cd_late, other_raw = lax.optimization_barrier((theirs, cd_irrep, other_raw))
            own_amps = masked_amplitudes(amplitudes, ij_irrep, cd_irrep)
            other_amps = masked_amplitudes(other_raw, ij_irrep, to_core(cd_late))
        else:
            if LATE:
                amplitudes, _ = lax.optimization_barrier((amplitudes, first))
            own_amps = masked_amplitudes(amplitudes, ij_irrep, cd_irrep)
            other_amps = to_core(own_amps)
        same = [first[0]] + [piece(mine, g) for g in granules[1:]]
        cross = [first[1]] + [piece(theirs, g) for g in granules[1:]]
        if SWAP_WHOLE:
            swapped = to_core(theirs_late)
            swapped = [piece(swapped, g) for g in granules]
        else:
            swapped = [to_core(block) for block in cross]

        values, on_x, on_y, sums = {"masked": (own_amps, other_amps)}, {}, {}, {}
        order = list(ORDER)

        def gated(load, name):
            waits = [values[other] for other in GATES.get(name, ()) if other in values]
            return lax.optimization_barrier((load, waits))[0] if waits else load

        for kind, g in ORDER:
            if kind == "far":
                loads = (on_y["near", g], on_x["near", g])
                ways = (to_x, to_y)
            elif kind == "near":
                loads = (same[g], cross[g])
                ways = (to_x, to_y_across)
            else:
                loads = (cross[g], same[g])
                ways = (to_x_across, to_y)
            loads = gated(loads, (kind, g))
            back = order.index((kind, g)) - DEPTH
            if back >= 0:
                earlier = [values[name] for name in order[max(back - STRICT, 0) : back + 1]]
                loads, _ = lax.optimization_barrier((loads, earlier))
            on_x[kind, g], on_y[kind, g] = ways[0](loads[0]), ways[1](loads[1])
            values[kind, g] = (on_x[kind, g], on_y[kind, g])
            if not all((k, g) in on_x for k in ("near", "rest", "far")):
                continue
            pieces = [
                same[g], swapped[g],
                on_x["near", g], on_x["rest", g],
                on_y["rest", g], on_y["near", g],
                on_y["far", g], on_x["far", g],
            ]
            pieces = gated(pieces, ("product", g))
            pairwise = ZMODE[g] == "pair"
            slots = hops // 2 + 2 * (hops % 2) if pairwise else owners if ZMODE[g] == "swap" else hops
            partials = product(slots, own_amps, other_amps, pieces, scale, depth)
            values["product", g] = partials
            if pairwise:
                kept, sent = partials[:2], partials[2:].astype(jnp.float16)
                pair = kept + along_z(sent, 1).astype(jnp.float32)
                values["pair", g] = pair
                sums[g] = pair[0] + along_z(pair[1].astype(jnp.float16), 2).astype(jnp.float32)
            elif ZMODE[g] == "swap":
                groups = [[z * 2 + k for z in range(chips_z)] for k in range(2)]
                halved = partials.astype(jnp.float16)
                arrived = lax.all_to_all(halved, "vir", 0, 0, axis_index_groups=groups, tiled=True)
                sums[g] = arrived.astype(jnp.float32).sum(axis=0)
            else:
                halved = partials.astype(jnp.float16)
                sums[g] = partials[0]
                for hop in range(1, chips_z):
                    arrived = along_z(halved[hop], hop)
                    if hop == 1:
                        values["pair", g] = arrived
                    sums[g] += arrived.astype(jnp.float32)
            values["sum", g] = sums[g]
        return total([sums[g] for g in granules], 1.0 / scale, amplitudes.shape[0], width)

    special = occ_size == 4 and vir_size == 8
    in_specs = (P("occ", "vir"), P("vir", "occ"), P("occ"), P("vir"))
    return jax.shard_map(
        body if special else plain_body,
        mesh=mesh,
        in_specs=in_specs,
        out_specs=P("occ", "vir"),
        check_vma=False,
    )
```

time: 211 us -> 106 us (0.50)
  waiting for transfers between devices: 183 us -> 35.3 us
  starting transfers between devices: 0.04 us -> 42.3 us
  matrix products: 14.5 us -> 0 us
  Pallas kernels: 0 us -> 14.2 us
  between operations: 13.4 us -> 0.39 us
  other arithmetic: 0 us -> 7.21 us
  local copies, waits for them, and re-layouts: 0 us -> 6.81 us
    all_gather x1 -> x0, waiting for transfers between devices: 92.1 us -> none  [body(): lax.all_gather(integrals, 'occ', axis=1, tiled=True)]
    reduce_scatter x1 -> x0, waiting for transfers between devices: 89.8 us -> none  [body(): lax.psum_scatter(partial_sums, 'vir', scatter_dimension=1, tiled=True)]
    ppermute x0 -> x35, starting transfers between devices: none -> 42.3 us  [send(): return lax.ppermute(array, ('occ', 'vir'), pairs)]
    ppermute x0 -> x35, waiting for transfers between devices: none -> 35.3 us  [send(): return lax.ppermute(array, ('occ', 'vir'), pairs)]
    dot_general x1 -> x0, matrix products: 14.5 us -> none  [body(): jnp.dot(masked, lax.all_gather(integrals, 'occ', axis=1, tiled=True), pre...]
    pallas_call x0 -> x5, Pallas kernels: none -> 14.2 us  [the longest x4 12.7 us: product(): pl.pallas_call(functools.partial(product_kernel, scale), in_specs=[pl.Blo...]
    split x0 -> x3, local copies, waits for them, and re-layouts: none -> 5.74 us  [piece(): return jnp.concatenate(jnp.split(cut, folds), axis=1)]
    concatenate x0 -> x11, other arithmetic: none -> 3.67 us  [piece(): return jnp.concatenate(jnp.split(cut, folds), axis=1)]
  transfers between devices with their start and end apart: 2 -> 35, of which waited for: 2 -> 16; matrix products, arithmetic and copies ran while one was open for 0% -> 13% of each run, Pallas kernels for 0% -> 12%
where the time goes in v2:
time: 106 us
  starting transfers between devices  42.3 us (40%)
  waiting for transfers between devices  35.3 us (33%)
  Pallas kernels  14.2 us (13%)
  other arithmetic  7.21 us (7%)
  local copies, waits for them, and re-layouts  6.81 us (6%)
    ppermute x35, starting transfers between devices, send(): return lax.ppermute(array, ('occ', 'vir'), pairs)  42.3 us
    ppermute x35, waiting for transfers between devices, send(): return lax.ppermute(array, ('occ', 'vir'), pairs)  35.3 us
    pallas_call x4, Pallas kernels, product(): pl.pallas_call(functools.partial(product_kernel, scale), in_specs=[pl.Blo...  12.7 us
    split x3, local copies, waits for them, and re-layouts, piece(): return jnp.concatenate(jnp.split(cut, folds), axis=1)  5.74 us
    concatenate x11, other arithmetic, piece(): return jnp.concatenate(jnp.split(cut, folds), axis=1)  3.67 us
    select_n x1, other arithmetic, masked_amplitudes(): jnp.where(rows[:, None] == columns[None, :], amplitudes, jnp.zeros_like(a...  2.93 us
  transfers between devices with their start and end apart: 35, of which 16 were waited for; matrix products, arithmetic and copies ran while one was open for 13% of the time, Pallas kernels for 12%

profile of v2, /device:TPU:0, one launch (start us, length us, event | category | flops | bytes accessed | tf_op | source)
XLA Modules:
  0.0 106.3 jit_solution(335438550072352359)
XLA Ops:
  0.5 1.8 %constant_dynamic-slice_fusion.4 = (bf16[1024,64]{1,0:T(8,128)(2,1)S(1)}, bf16[1024,64]{1,0:T(8,128)(2,1)S(1)}, bf16[1024,64]{1,0:T(8,128)(2,1)S(1)}, bf16[1024,64]{1,0:T(8,128)(2,1)S(1)}) fusion(bf16[2048,512]{1,0:T(8,128)(2,1)} %param.5, s32[]{:T(128)S(6)} %select_n.53, s32[]{:T(128)S(6)} %select_n.52, s32[]{:T(128)S(6)} %add.69), kind=kLoop, calls=%fused_computation.42 | loop fusion | bytes 1048588 | tf_op jit(solution)/shard_map/split | solution.py:149
  2.2 1.0 pad_maximum_fusion
  3.2 1.0 constant_dynamic-slice_fusion.7
  4.8 2.5 %collective-permute-start.3 = (bf16[1024,128]{1,0:T(8,128)(2,1)S(1)}, bf16[1024,128]{1,0:T(8,128)(2,1)S(1)}, u32[]{:S(2)}, u32[]{:S(2)}) collective-permute-start(bf16[1024,128]{1,0:T(8,128)(2,1)S(1)} %get-tuple-element.48.refs_0_), channel_id=1, source_target_pairs={{0,8},{1,9},{2,10},{3,11},{4,12},{5,13},{6,14},{7,15},{8,0},{9,1},... | collective-permute-start | bytes 786440 | tf_op jit(solution)/shard_map/ppermute | solution.py:121
  7.3 1.2 %collective-permute-start.6 = (bf16[1024,128]{1,0:T(8,128)(2,1)}, bf16[1024,128]{1,0:T(8,128)(2,1)S(1)}, u32[]{:S(2)}, u32[]{:S(2)}) collective-permute-start(bf16[1024,128]{1,0:T(8,128)(2,1)} %get-tuple-element.50), channel_id=1, source_target_pairs={{0,17},{1,16},{2,19},{3,18},{4,21},{5,20},{6,23},{7,22},{8,25},{9,... | collective-permute-start | bytes 786440 | tf_op jit(solution)/shard_map/ppermute | solution.py:121
  8.5 2.0 %constant_dynamic-slice_fusion.2 = (bf16[1024,64]{1,0:T(8,128)(2,1)}, bf16[1024,64]{1,0:T(8,128)(2,1)}, bf16[1024,64]{1,0:T(8,128)(2,1)}, bf16[1024,64]{1,0:T(8,...) fusion(bf16[2048,512]{1,0:T(8,128)(2,1)S(1)} %copy-done, ...), kind=kLoop, calls=%fused_computation.40 | loop fusion | bytes 3145756 | tf_op jit(solution)/shard_map/split | solution.py:149
  11.2 1.3 %pad_maximum_fusion.9.refs_0_ = bf16[1024,128]{1,0:T(8,128)(2,1)S(1)} fusion(bf16[1024,64]{1,0:T(8,128)(2,1)} %get-tuple-element.102, bf16[1024,64]{1,0:T(8,128)(2,1)} %get-tuple-element.93), kind=kLoop, calls=%fused_computation.31 | loop fusion | flops 524288 | bytes 524288 | tf_op jit(solution)/shard_map/concatenate | solution.py:149
  13.2 0.8 collective-permute-done.3.refs_2_
  14.1 1.8 %collective-permute-start.5 = (bf16[1024,128]{1,0:T(8,128)(2,1)S(1)}, bf16[1024,128]{1,0:T(8,128)(2,1)S(1)}, u32[]{:S(2)}, u32[]{:S(2)}) collective-permute-start(bf16[1024,128]{1,0:T(8,128)(2,1)S(1)} %get-tuple-element.48.refs_0_), channel_id=1, source_target_pairs={{0,16},{1,17},{2,18},{3,19},{4,20},{5,21},{6,22},{7,23},{8,24},{9,... | collective-permute-start | bytes 786440 | tf_op jit(solution)/shard_map/ppermute | solution.py:121
  15.9 2.1 %collective-permute-start.11 = (bf16[1024,128]{1,0:T(8,128)(2,1)S(1)}, bf16[1024,128]{1,0:T(8,128)(2,1)S(1)}, u32[]{:S(2)}, u32[]{:S(2)}) collective-permute-start(bf16[1024,128]{1,0:T(8,128)(2,1)S(1)} %pad_maximum_fusion.3.refs_0_), channel_id=1, source_target_pairs={{0,8},{1,9},{2,10},{3,11},{4,12},{5,13},{6,14},{7,15},{8,0},{9,1},... | collective-permute-start | bytes 786440 | tf_op jit(solution)/shard_map/ppermute | solution.py:121
  18.0 1.9 %fusion.10 = (bf16[1024,64]{1,0:T(8,128)(2,1)S(1)}, bf16[1024,64]{1,0:T(8,128)(2,1)S(1)}, bf16[1024,64]{1,0:T(8,128)(2,1)S(1)}, bf16[1024,64]{1,0:T(8,128)(2,1)S...) fusion(bf16[2048,256]{1,0:T(8,128)(2,1)} %collective-permute-done.2), kind=kLoop, calls=%fused_computation.54 | loop fusion | bytes 2097152 | tf_op jit(solution)/shard_map/split | solution.py:149
  20.0 1.5 %collective-permute-start.8 = (bf16[1024,128]{1,0:T(8,128)(2,1)S(1)}, bf16[1024,128]{1,0:T(8,128)(2,1)S(1)}, u32[]{:S(2)}, u32[]{:S(2)}) collective-permute-start(bf16[1024,128]{1,0:T(8,128)(2,1)S(1)} %collective-permute-done.6.refs_5_), channel_id=1, source_target_pairs={{0,8},{1,9},{2,10},{3,11},{4,12},{5,13},{6,14},{7,15},{8,0},{9,1},... | collective-permute-start | bytes 786440 | tf_op jit(solution)/shard_map/ppermute | solution.py:121
  21.6 2.9 %compare_select_fusion = (bf16[1024,2048]{1,0:T(8,128)(2,1)S(1)}, bf16[1024,2048]{1,0:T(8,128)(2,1)S(1)}) fusion(bf16[1024,2048]{1,0:T(8,128)(2,1)} %collective-permute-done.1, bf16[2048]{0:T(1024)(128)(2,1)S(1)} %convert_element_type.56, bf16[1024]{0:T(1024)(128)(2,1)S(1)} %convert_element_type.54, bf16[1024,2048]{1,0:T(8,128)(2,1)S(1)} %copy-done.1, ...), kind=kLoop, calls=%fused_computation | loop fusion | flops 8388608 | bytes 16787456 | tf_op jit(solution)/shard_map/jit(_where)/select_n | solution.py:30
  24.6 2.3 %collective-permute-start.12 = (bf16[1024,128]{1,0:T(8,128)(2,1)S(1)}, bf16[1024,128]{1,0:T(8,128)(2,1)S(1)}, u32[]{:S(2)}, u32[]{:S(2)}) collective-permute-start(bf16[1024,128]{1,0:T(8,128)(2,1)S(1)} %pad_maximum_fusion.5), channel_id=1, source_target_pairs={{0,9},{1,8},{2,11},{3,10},{4,13},{5,12},{6,15},{7,14},{8,1},{9,0},... | collective-permute-start | bytes 786440 | tf_op jit(solution)/shard_map/ppermute | solution.py:121
  26.9 0.9 collective-permute-done.7.refs_6_
  27.8 2.3 %collective-permute-start.13 = (bf16[1024,128]{1,0:T(8,128)(2,1)S(1)}, bf16[1024,128]{1,0:T(8,128)(2,1)S(1)}, u32[]{:S(2)}, u32[]{:S(2)}) collective-permute-start(bf16[1024,128]{1,0:T(8,128)(2,1)S(1)} %pad_maximum_fusion.3.refs_0_), channel_id=1, source_target_pairs={{0,16},{1,17},{2,18},{3,19},{4,20},{5,21},{6,22},{7,23},{8,24},{9,... | collective-permute-start | bytes 786440 | tf_op jit(solution)/shard_map/ppermute | solution.py:121
  30.1 3.2 %collective-permute-done.8.refs_7_ = bf16[1024,128]{1,0:T(8,128)(2,1)S(1)} collective-permute-done((bf16[1024,128]{1,0:T(8,128)(2,1)S(1)}, bf16[1024,128]{1,0:T(8,128)(2,1)S(1)}, u32[]{:S(2)}, u32[]{:S(2)}) %collective-permute-start.8) | collective-permute-done | bytes 262176 | tf_op jit(solution)/shard_map/ppermute | solution.py:121
  33.3 3.2 %shard_map.46 = f32[4,512,128]{2,1,0:T(8,128)S(1)} custom-call(s32[4]{0:T(128)S(1)} %fusion.9.slot_ref, bf16[1024,2048]{1,0:T(8,128)(2,1)S(1)} %get-tuple-element.116.own_amps, bf16[1024,2048]{1,0:T(8,128)(2,1)S(1)} %get-tuple-element.115.other_amps, bf16[1024,128]{1,0:T(8,128)(2,1)S(1)} %get-tuple-element.48.refs_0_, ...), custom_call_target="tpu_custom_call" | custom-call | tf_op jit(solution)/shard_map/pallas_call | solution.py:72
  36.5 1.6 %collective-permute-start.9 = (f16[2,512,128]{2,1,0:T(8,128)(2,1)S(1)}, f16[2,512,128]{2,1,0:T(8,128)(2,1)S(1)}, u32[]{:S(2)}, u32[]{:S(2)}) collective-permute-start(f16[2,512,128]{2,1,0:T(8,128)(2,1)S(1)} %slice_convert_fusion.3), channel_id=1, source_target_pairs={{0,2},{1,3},{2,0},{3,1},{4,6},{5,7},{6,4},{7,5},{8,10},{9,11},{10,... | collective-permute-start | bytes 786440 | tf_op jit(solution)/shard_map/ppermute | solution.py:121
  39.3 1.5 %collective-permute-start.15 = (bf16[1024,128]{1,0:T(8,128)(2,1)S(1)}, bf16[1024,128]{1,0:T(8,128)(2,1)S(1)}, u32[]{:S(2)}, u32[]{:S(2)}) collective-permute-start(bf16[1024,128]{1,0:T(8,128)(2,1)S(1)} %collective-permute-done.11.refs_2_), channel_id=1, source_target_pairs={{0,16},{1,17},{2,18},{3,19},{4,20},{5,21},{6,22},{7,23},{8,24},{9,... | collective-permute-start | bytes 786440 | tf_op jit(solution)/shard_map/ppermute | solution.py:121
  40.8 1.5 %collective-permute-start.16 = (bf16[1024,128]{1,0:T(8,128)(2,1)S(1)}, bf16[1024,128]{1,0:T(8,128)(2,1)S(1)}, u32[]{:S(2)}, u32[]{:S(2)}) collective-permute-start(bf16[1024,128]{1,0:T(8,128)(2,1)S(1)} %collective-permute-done.14.refs_5_), channel_id=1, source_target_pairs={{0,8},{1,9},{2,10},{3,11},{4,12},{5,13},{6,14},{7,15},{8,0},{9,1},... | collective-permute-start | bytes 786440 | tf_op jit(solution)/shard_map/ppermute | solution.py:121
  42.8 0.9 collective-permute-done.9
  43.8 4.7 %collective-permute-done.15.refs_6_ = bf16[1024,128]{1,0:T(8,128)(2,1)S(1)} collective-permute-done((bf16[1024,128]{1,0:T(8,128)(2,1)S(1)}, bf16[1024,128]{1,0:T(8,128)(2,1)S(1)}, u32[]{:S(2)}, u32[]{:S(2)}) %collective-permute-start.15) | collective-permute-done | bytes 262176 | tf_op jit(solution)/shard_map/ppermute | solution.py:121
  48.5 1.1 %collective-permute-start.21 = (bf16[1024,128]{1,0:T(8,128)(2,1)S(1)}, bf16[1024,128]{1,0:T(8,128)(2,1)S(1)}, u32[]{:S(2)}, u32[]{:S(2)}) collective-permute-start(bf16[1024,128]{1,0:T(8,128)(2,1)S(1)} %pad_maximum_fusion.6.refs_0_), channel_id=1, source_target_pairs={{0,16},{1,17},{2,18},{3,19},{4,20},{5,21},{6,22},{7,23},{8,24},{9,... | collective-permute-start | bytes 786440 | tf_op jit(solution)/shard_map/ppermute | solution.py:121
  49.6 1.2 %collective-permute-done.16.refs_7_ = bf16[1024,128]{1,0:T(8,128)(2,1)S(1)} collective-permute-done((bf16[1024,128]{1,0:T(8,128)(2,1)S(1)}, bf16[1024,128]{1,0:T(8,128)(2,1)S(1)}, u32[]{:S(2)}, u32[]{:S(2)}) %collective-permute-start.16) | collective-permute-done | bytes 262176 | tf_op jit(solution)/shard_map/ppermute | solution.py:121
  50.8 2.4 %collective-permute-start.27 = (bf16[1024,128]{1,0:T(8,128)(2,1)S(1)}, bf16[1024,128]{1,0:T(8,128)(2,1)S(1)}, u32[]{:S(2)}, u32[]{:S(2)}) collective-permute-start(bf16[1024,128]{1,0:T(8,128)(2,1)S(1)} %pad_maximum_fusion.9.refs_0_), channel_id=1, source_target_pairs={{0,8},{1,9},{2,10},{3,11},{4,12},{5,13},{6,14},{7,15},{8,0},{9,1},... | collective-permute-start | bytes 786440 | tf_op jit(solution)/shard_map/ppermute | solution.py:121
  53.2 3.2 %shard_map.47 = f32[4,512,128]{2,1,0:T(8,128)S(1)} custom-call(s32[4]{0:T(128)S(1)} %fusion.9.slot_ref, bf16[1024,2048]{1,0:T(8,128)(2,1)S(1)} %get-tuple-element.116.own_amps, bf16[1024,2048]{1,0:T(8,128)(2,1)S(1)} %get-tuple-element.115.other_amps, bf16[1024,128]{1,0:T(8,128)(2,1)S(1)} %pad_maximum_fusion.3.refs_0_, ...), custom_call_target="tpu_custom_call" | custom-call | tf_op jit(solution)/shard_map/pallas_call | solution.py:72
  56.6 2.6 %collective-permute-start.10 = (f16[512,128]{1,0:T(8,128)(2,1)S(1)}, f16[512,128]{1,0:T(8,128)(2,1)S(1)}, u32[]{:S(2)}, u32[]{:S(2)}) collective-permute-start(f16[512,128]{1,0:T(8,128)(2,1)S(1)} %fusion.4), channel_id=1, source_target_pairs={{0,4},{1,5},{2,6},{3,7},{4,0},{5,1},{6,2},{7,3},{8,12},{9,13},{10,... | collective-permute-start | bytes 393224 | tf_op jit(solution)/shard_map/ppermute | solution.py:121
  59.3 0.7 collective-permute-start.17
  60.1 1.1 collective-permute-start.23
  61.2 0.8 collective-permute-done.27.refs_2_
  62.0 2.3 %collective-permute-start.24 = (bf16[1024,128]{1,0:T(8,128)(2,1)S(1)}, bf16[1024,128]{1,0:T(8,128)(2,1)S(1)}, u32[]{:S(2)}, u32[]{:S(2)}) collective-permute-start(bf16[1024,128]{1,0:T(8,128)(2,1)S(1)} %collective-permute-done.22.refs_5_), channel_id=1, source_target_pairs={{0,8},{1,9},{2,10},{3,11},{4,12},{5,13},{6,14},{7,15},{8,0},{9,1},... | collective-permute-start | bytes 786440 | tf_op jit(solution)/shard_map/ppermute | solution.py:121
  65.0 1.5 %collective-permute-start.28 = (bf16[1024,128]{1,0:T(8,128)(2,1)S(1)}, bf16[1024,128]{1,0:T(8,128)(2,1)S(1)}, u32[]{:S(2)}, u32[]{:S(2)}) collective-permute-start(bf16[1024,128]{1,0:T(8,128)(2,1)S(1)} %pad_maximum_fusion.11), channel_id=1, source_target_pairs={{0,9},{1,8},{2,11},{3,10},{4,13},{5,12},{6,15},{7,14},{8,1},{9,0},... | collective-permute-start | bytes 786440 | tf_op jit(solution)/shard_map/ppermute | solution.py:121
  66.6 1.2 %collective-permute-start.29 = (bf16[1024,128]{1,0:T(8,128)(2,1)S(1)}, bf16[1024,128]{1,0:T(8,128)(2,1)S(1)}, u32[]{:S(2)}, u32[]{:S(2)}) collective-permute-start(bf16[1024,128]{1,0:T(8,128)(2,1)S(1)} %pad_maximum_fusion.9.refs_0_), channel_id=1, source_target_pairs={{0,16},{1,17},{2,18},{3,19},{4,20},{5,21},{6,22},{7,23},{8,24},{9,... | collective-permute-start | bytes 786440 | tf_op jit(solution)/shard_map/ppermute | solution.py:121
  67.9 2.9 %collective-permute-done.17 = f16[2,512,128]{2,1,0:T(8,128)(2,1)S(1)} collective-permute-done((f16[2,512,128]{2,1,0:T(8,128)(2,1)S(1)}, f16[2,512,128]{2,1,0:T(8,128)(2,1)S(1)}, u32[]{:S(2)}, u32[]{:S(2)}) %collective-permute-start.17) | collective-permute-done | bytes 262176 | tf_op jit(solution)/shard_map/ppermute | solution.py:121
  70.8 1.3 %collective-permute-start.31 = (bf16[1024,128]{1,0:T(8,128)(2,1)S(1)}, bf16[1024,128]{1,0:T(8,128)(2,1)S(1)}, u32[]{:S(2)}, u32[]{:S(2)}) collective-permute-start(bf16[1024,128]{1,0:T(8,128)(2,1)S(1)} %collective-permute-done.27.refs_2_), channel_id=1, source_target_pairs={{0,16},{1,17},{2,18},{3,19},{4,20},{5,21},{6,22},{7,23},{8,24},{9,... | collective-permute-start | bytes 786440 | tf_op jit(solution)/shard_map/ppermute | solution.py:121
  72.2 1.0 collective-permute-start.32
  73.2 1.9 %collective-permute-start.18 = (f16[512,128]{1,0:T(8,128)(2,1)S(1)}, f16[512,128]{1,0:T(8,128)(2,1)S(1)}, u32[]{:S(2)}, u32[]{:S(2)}) collective-permute-start(f16[512,128]{1,0:T(8,128)(2,1)S(1)} %fusion.5), channel_id=1, source_target_pairs={{0,4},{1,5},{2,6},{3,7},{4,0},{5,1},{6,2},{7,3},{8,12},{9,13},{10,... | collective-permute-start | bytes 393224 | tf_op jit(solution)/shard_map/ppermute | solution.py:121
  75.1 3.2 %shard_map.48 = f32[4,512,128]{2,1,0:T(8,128)S(1)} custom-call(s32[4]{0:T(128)S(1)} %fusion.9.slot_ref, bf16[1024,2048]{1,0:T(8,128)(2,1)S(1)} %get-tuple-element.116.own_amps, bf16[1024,2048]{1,0:T(8,128)(2,1)S(1)} %get-tuple-element.115.other_amps, bf16[1024,128]{1,0:T(8,128)(2,1)S(1)} %pad_maximum_fusion.6.refs_0_, ...), custom_call_target="tpu_custom_call" | custom-call | tf_op jit(solution)/shard_map/pallas_call | solution.py:72
  78.3 0.8 collective-permute-start.25
  79.1 2.6 %collective-permute-done.31.refs_6_ = bf16[1024,128]{1,0:T(8,128)(2,1)S(1)} collective-permute-done((bf16[1024,128]{1,0:T(8,128)(2,1)S(1)}, bf16[1024,128]{1,0:T(8,128)(2,1)S(1)}, u32[]{:S(2)}, u32[]{:S(2)}) %collective-permute-start.31) | collective-permute-done | bytes 262176 | tf_op jit(solution)/shard_map/ppermute | solution.py:121
  81.7 0.8 collective-permute-done.32.refs_7_
  82.5 3.2 %shard_map.49 = f32[4,512,128]{2,1,0:T(8,128)S(1)} custom-call(s32[4]{0:T(128)S(1)} %fusion.9.slot_ref, bf16[1024,2048]{1,0:T(8,128)(2,1)S(1)} %get-tuple-element.116.own_amps, bf16[1024,2048]{1,0:T(8,128)(2,1)S(1)} %get-tuple-element.115.other_amps, bf16[1024,128]{1,0:T(8,128)(2,1)S(1)} %pad_maximum_fusion.9.refs_0_, ...), custom_call_target="tpu_custom_call" | custom-call | tf_op jit(solution)/shard_map/pallas_call | solution.py:72
  86.8 2.3 %collective-permute-start.26 = (f16[512,128]{1,0:T(8,128)(2,1)S(1)}, f16[512,128]{1,0:T(8,128)(2,1)S(1)}, u32[]{:S(2)}, u32[]{:S(2)}) collective-permute-start(f16[512,128]{1,0:T(8,128)(2,1)S(1)} %fusion.6), channel_id=1, source_target_pairs={{0,4},{1,5},{2,6},{3,7},{4,0},{5,1},{6,2},{7,3},{8,12},{9,13},{10,... | collective-permute-start | bytes 393224 | tf_op jit(solution)/shard_map/ppermute | solution.py:121
  89.0 7.6 %collective-permute-done.33 = f16[2,512,128]{2,1,0:T(8,128)(2,1)S(1)} collective-permute-done((f16[2,512,128]{2,1,0:T(8,128)(2,1)S(1)}, f16[2,512,128]{2,1,0:T(8,128)(2,1)S(1)}, u32[]{:S(2)}, u32[]{:S(2)}) %collective-permute-start.33) | collective-permute-done | bytes 262176 | tf_op jit(solution)/shard_map/ppermute | solution.py:121
  96.7 1.0 collective-permute-start.34
  97.8 7.0 %collective-permute-done.34 = f16[512,128]{1,0:T(8,128)(2,1)S(1)} collective-permute-done((f16[512,128]{1,0:T(8,128)(2,1)S(1)}, f16[512,128]{1,0:T(8,128)(2,1)S(1)}, u32[]{:S(2)}, u32[]{:S(2)}) %collective-permute-start.34) | collective-permute-done | bytes 131104 | tf_op jit(solution)/shard_map/ppermute | solution.py:121
  104.7 1.6 %shard_map.50 = f32[1024,256]{1,0:T(8,128)} custom-call(f32[512,128]{1,0:T(8,128)S(1)} %fusion.3.refs_0_, f32[512,128]{1,0:T(8,128)S(1)} %fusion.2.refs_1_, f32[512,128]{1,0:T(8,128)S(1)} %fusion.1.refs_2_, f32[512,128]{1,0:T(8,128)S(1)} %fusion.refs_3_), custom_call_target="tpu_custom_call" | custom-call | tf_op jit(solution)/shard_map/pallas_call | solution.py:101
  (75 shorter events, 6.9 us)
Async XLA Ops:
  0.0 3.2 %copy-start = (bf16[2048,512]{1,0:T(8,128)(2,1)S(1)}, bf16[2048,512]{1,0:T(8,128)(2,1)}, u32[]{:S(2)}) copy-start(bf16[2048,512]{1,0:T(8,128)(2,1)} %param.5) | copy-start | bytes 6291460
  0.0 4.3 %copy-start.4 = (s32[2048]{0:T(1024)S(1)}, s32[2048]{0:T(1024)}, u32[]{:S(2)}) copy-start(s32[2048]{0:T(1024)} %param.7) | copy-start | bytes 24580
  0.0 20.0 %collective-permute-start.1 = (bf16[1024,2048]{1,0:T(8,128)(2,1)}, bf16[1024,2048]{1,0:T(8,128)(2,1)}, u32[]{:S(2)}, u32[]{:S(2)}) collective-permute-start(bf16[1024,2048]{1,0:T(8,128)(2,1)} %param.4), channel_id=1, source_target_pairs={{0,1},{1,0},{2,3},{3,2},{4,5},{5,4},{6,7},{7,6},{8,9},{9,8},{10,11... | collective-permute-start | bytes 12582920 | tf_op jit(solution)/shard_map/ppermute | solution.py:121
  4.3 13.7 %collective-permute-start.2 = (bf16[2048,256]{1,0:T(8,128)(2,1)}, bf16[2048,256]{1,0:T(8,128)(2,1)}, u32[]{:S(2)}, u32[]{:S(2)}) collective-permute-start(bf16[2048,256]{1,0:T(8,128)(2,1)} %constant_dynamic-slice_fusion.7), channel_id=1, source_target_pairs={{0,1},{1,0},{2,3},{3,2},{4,5},{5,4},{6,7},{7,6},{8,9},{9,8},{10,11... | collective-permute-start | bytes 3145736 | tf_op jit(solution)/shard_map/ppermute | solution.py:121
  4.3 8.2 %collective-permute-start = (s32[2048]{0:T(1024)S(1)}, s32[2048]{0:T(1024)S(1)}, u32[]{:S(2)}, u32[]{:S(2)}) collective-permute-start(s32[2048]{0:T(1024)S(1)} %copy-done.4), channel_id=1, source_target_pairs={{0,1},{1,0},{2,3},{3,2},{4,5},{5,4},{6,7},{7,6},{8,9},{9,8},{10,11... | collective-permute-start | bytes 24584 | tf_op jit(solution)/shard_map/ppermute | solution.py:121
  4.8 9.3 %collective-permute-start.3 = (bf16[1024,128]{1,0:T(8,128)(2,1)S(1)}, bf16[1024,128]{1,0:T(8,128)(2,1)S(1)}, u32[]{:S(2)}, u32[]{:S(2)}) collective-permute-start(bf16[1024,128]{1,0:T(8,128)(2,1)S(1)} %get-tuple-element.48.refs_0_), channel_id=1, source_target_pairs={{0,8},{1,9},{2,10},{3,11},{4,12},{5,13},{6,14},{7,15},{8,0},{9,1},... | collective-permute-start | bytes 786440 | tf_op jit(solution)/shard_map/ppermute | solution.py:121
  7.3 8.6 %collective-permute-start.6 = (bf16[1024,128]{1,0:T(8,128)(2,1)}, bf16[1024,128]{1,0:T(8,128)(2,1)S(1)}, u32[]{:S(2)}, u32[]{:S(2)}) collective-permute-start(bf16[1024,128]{1,0:T(8,128)(2,1)} %get-tuple-element.50), channel_id=1, source_target_pairs={{0,17},{1,16},{2,19},{3,18},{4,21},{5,20},{6,23},{7,22},{8,25},{9,... | collective-permute-start | bytes 786440 | tf_op jit(solution)/shard_map/ppermute | solution.py:121
  8.5 4.1 %copy-start.5 = (s32[1024]{0:T(1024)S(1)}, s32[1024]{0:T(1024)}, u32[]{:S(2)}) copy-start(s32[1024]{0:T(1024)} %param.6) | copy-start | bytes 12292
  11.1 10.4 %copy-start.1 = (bf16[1024,2048]{1,0:T(8,128)(2,1)S(1)}, bf16[1024,2048]{1,0:T(8,128)(2,1)}, u32[]{:S(2)}) copy-start(bf16[1024,2048]{1,0:T(8,128)(2,1)} %param.4) | copy-start | bytes 12582916
  12.6 12.0 %collective-permute-start.4 = (bf16[1024,128]{1,0:T(8,128)(2,1)}, bf16[1024,128]{1,0:T(8,128)(2,1)S(1)}, u32[]{:S(2)}, u32[]{:S(2)}) collective-permute-start(bf16[1024,128]{1,0:T(8,128)(2,1)} %get-tuple-element.50), channel_id=1, source_target_pairs={{0,9},{1,8},{2,11},{3,10},{4,13},{5,12},{6,15},{7,14},{8,1},{9,0},... | collective-permute-start | bytes 786440 | tf_op jit(solution)/shard_map/ppermute | solution.py:121
  14.1 10.5 %collective-permute-start.5 = (bf16[1024,128]{1,0:T(8,128)(2,1)S(1)}, bf16[1024,128]{1,0:T(8,128)(2,1)S(1)}, u32[]{:S(2)}, u32[]{:S(2)}) collective-permute-start(bf16[1024,128]{1,0:T(8,128)(2,1)S(1)} %get-tuple-element.48.refs_0_), channel_id=1, source_target_pairs={{0,16},{1,17},{2,18},{3,19},{4,20},{5,21},{6,22},{7,23},{8,24},{9,... | collective-permute-start | bytes 786440 | tf_op jit(solution)/shard_map/ppermute | solution.py:121
  15.9 22.4 %collective-permute-start.11 = (bf16[1024,128]{1,0:T(8,128)(2,1)S(1)}, bf16[1024,128]{1,0:T(8,128)(2,1)S(1)}, u32[]{:S(2)}, u32[]{:S(2)}) collective-permute-start(bf16[1024,128]{1,0:T(8,128)(2,1)S(1)} %pad_maximum_fusion.3.refs_0_), channel_id=1, source_target_pairs={{0,8},{1,9},{2,10},{3,11},{4,12},{5,13},{6,14},{7,15},{8,0},{9,1},... | collective-permute-start | bytes 786440 | tf_op jit(solution)/shard_map/ppermute | solution.py:121
  17.9 9.9 %collective-permute-start.7 = (bf16[1024,128]{1,0:T(8,128)(2,1)S(1)}, bf16[1024,128]{1,0:T(8,128)(2,1)S(1)}, u32[]{:S(2)}, u32[]{:S(2)}) collective-permute-start(bf16[1024,128]{1,0:T(8,128)(2,1)S(1)} %collective-permute-done.3.refs_2_), channel_id=1, source_target_pairs={{0,16},{1,17},{2,18},{3,19},{4,20},{5,21},{6,22},{7,23},{8,24},{9,... | collective-permute-start | bytes 786440 | tf_op jit(solution)/shard_map/ppermute | solution.py:121
  20.0 13.2 %collective-permute-start.8 = (bf16[1024,128]{1,0:T(8,128)(2,1)S(1)}, bf16[1024,128]{1,0:T(8,128)(2,1)S(1)}, u32[]{:S(2)}, u32[]{:S(2)}) collective-permute-start(bf16[1024,128]{1,0:T(8,128)(2,1)S(1)} %collective-permute-done.6.refs_5_), channel_id=1, source_target_pairs={{0,8},{1,9},{2,10},{3,11},{4,12},{5,13},{6,14},{7,15},{8,0},{9,1},... | collective-permute-start | bytes 786440 | tf_op jit(solution)/shard_map/ppermute | solution.py:121
  24.5 13.8 %collective-permute-start.14 = (bf16[1024,128]{1,0:T(8,128)(2,1)S(1)}, bf16[1024,128]{1,0:T(8,128)(2,1)S(1)}, u32[]{:S(2)}, u32[]{:S(2)}) collective-permute-start(bf16[1024,128]{1,0:T(8,128)(2,1)S(1)} %pad_maximum_fusion.5), channel_id=1, source_target_pairs={{0,17},{1,16},{2,19},{3,18},{4,21},{5,20},{6,23},{7,22},{8,25},{9,... | collective-permute-start | bytes 786440 | tf_op jit(solution)/shard_map/ppermute | solution.py:121
  24.6 13.8 %collective-permute-start.12 = (bf16[1024,128]{1,0:T(8,128)(2,1)S(1)}, bf16[1024,128]{1,0:T(8,128)(2,1)S(1)}, u32[]{:S(2)}, u32[]{:S(2)}) collective-permute-start(bf16[1024,128]{1,0:T(8,128)(2,1)S(1)} %pad_maximum_fusion.5), channel_id=1, source_target_pairs={{0,9},{1,8},{2,11},{3,10},{4,13},{5,12},{6,15},{7,14},{8,1},{9,0},... | collective-permute-start | bytes 786440 | tf_op jit(solution)/shard_map/ppermute | solution.py:121
  27.8 11.1 %collective-permute-start.13 = (bf16[1024,128]{1,0:T(8,128)(2,1)S(1)}, bf16[1024,128]{1,0:T(8,128)(2,1)S(1)}, u32[]{:S(2)}, u32[]{:S(2)}) collective-permute-start(bf16[1024,128]{1,0:T(8,128)(2,1)S(1)} %pad_maximum_fusion.3.refs_0_), channel_id=1, source_target_pairs={{0,16},{1,17},{2,18},{3,19},{4,20},{5,21},{6,22},{7,23},{8,24},{9,... | collective-permute-start | bytes 786440 | tf_op jit(solution)/shard_map/ppermute | solution.py:121
  33.3 4.9 %copy-start.2 = (bf16[1024,64]{1,0:T(8,128)(2,1)S(1)}, bf16[1024,64]{1,0:T(8,128)(2,1)}, u32[]{:S(2)}) copy-start(bf16[1024,64]{1,0:T(8,128)(2,1)} %get-tuple-element.91) | copy-start | bytes 393220
  33.3 4.9 %copy-start.3 = (bf16[1024,64]{1,0:T(8,128)(2,1)S(1)}, bf16[1024,64]{1,0:T(8,128)(2,1)}, u32[]{:S(2)}) copy-start(bf16[1024,64]{1,0:T(8,128)(2,1)} %get-tuple-element.92) | copy-start | bytes 393220
  36.5 7.2 %collective-permute-start.9 = (f16[2,512,128]{2,1,0:T(8,128)(2,1)S(1)}, f16[2,512,128]{2,1,0:T(8,128)(2,1)S(1)}, u32[]{:S(2)}, u32[]{:S(2)}) collective-permute-start(f16[2,512,128]{2,1,0:T(8,128)(2,1)S(1)} %slice_convert_fusion.3), channel_id=1, source_target_pairs={{0,2},{1,3},{2,0},{3,1},{4,6},{5,7},{6,4},{7,5},{8,10},{9,11},{10,... | collective-permute-start | bytes 786440 | tf_op jit(solution)/shard_map/ppermute | solution.py:121
  38.3 18.0 %collective-permute-start.20 = (bf16[1024,128]{1,0:T(8,128)(2,1)S(1)}, bf16[1024,128]{1,0:T(8,128)(2,1)S(1)}, u32[]{:S(2)}, u32[]{:S(2)}) collective-permute-start(bf16[1024,128]{1,0:T(8,128)(2,1)S(1)} %pad_maximum_fusion.8), channel_id=1, source_target_pairs={{0,9},{1,8},{2,11},{3,10},{4,13},{5,12},{6,15},{7,14},{8,1},{9,0},... | collective-permute-start | bytes 786440 | tf_op jit(solution)/shard_map/ppermute | solution.py:121
  39.3 9.2 %collective-permute-start.15 = (bf16[1024,128]{1,0:T(8,128)(2,1)S(1)}, bf16[1024,128]{1,0:T(8,128)(2,1)S(1)}, u32[]{:S(2)}, u32[]{:S(2)}) collective-permute-start(bf16[1024,128]{1,0:T(8,128)(2,1)S(1)} %collective-permute-done.11.refs_2_), channel_id=1, source_target_pairs={{0,16},{1,17},{2,18},{3,19},{4,20},{5,21},{6,22},{7,23},{8,24},{9,... | collective-permute-start | bytes 786440 | tf_op jit(solution)/shard_map/ppermute | solution.py:121
  40.8 10.0 %collective-permute-start.16 = (bf16[1024,128]{1,0:T(8,128)(2,1)S(1)}, bf16[1024,128]{1,0:T(8,128)(2,1)S(1)}, u32[]{:S(2)}, u32[]{:S(2)}) collective-permute-start(bf16[1024,128]{1,0:T(8,128)(2,1)S(1)} %collective-permute-done.14.refs_5_), channel_id=1, source_target_pairs={{0,8},{1,9},{2,10},{3,11},{4,12},{5,13},{6,14},{7,15},{8,0},{9,1},... | collective-permute-start | bytes 786440 | tf_op jit(solution)/shard_map/ppermute | solution.py:121
  42.3 14.3 %collective-permute-start.19 = (bf16[1024,128]{1,0:T(8,128)(2,1)S(1)}, bf16[1024,128]{1,0:T(8,128)(2,1)S(1)}, u32[]{:S(2)}, u32[]{:S(2)}) collective-permute-start(bf16[1024,128]{1,0:T(8,128)(2,1)S(1)} %pad_maximum_fusion.6.refs_0_), channel_id=1, source_target_pairs={{0,8},{1,9},{2,10},{3,11},{4,12},{5,13},{6,14},{7,15},{8,0},{9,1},... | collective-permute-start | bytes 786440 | tf_op jit(solution)/shard_map/ppermute | solution.py:121
  43.7 15.6 %collective-permute-start.22 = (bf16[1024,128]{1,0:T(8,128)(2,1)S(1)}, bf16[1024,128]{1,0:T(8,128)(2,1)S(1)}, u32[]{:S(2)}, u32[]{:S(2)}) collective-permute-start(bf16[1024,128]{1,0:T(8,128)(2,1)S(1)} %pad_maximum_fusion.8), channel_id=1, source_target_pairs={{0,17},{1,16},{2,19},{3,18},{4,21},{5,20},{6,23},{7,22},{8,25},{9,... | collective-permute-start | bytes 786440 | tf_op jit(solution)/shard_map/ppermute | solution.py:121
  48.5 11.6 %collective-permute-start.21 = (bf16[1024,128]{1,0:T(8,128)(2,1)S(1)}, bf16[1024,128]{1,0:T(8,128)(2,1)S(1)}, u32[]{:S(2)}, u32[]{:S(2)}) collective-permute-start(bf16[1024,128]{1,0:T(8,128)(2,1)S(1)} %pad_maximum_fusion.6.refs_0_), channel_id=1, source_target_pairs={{0,16},{1,17},{2,18},{3,19},{4,20},{5,21},{6,22},{7,23},{8,24},{9,... | collective-permute-start | bytes 786440 | tf_op jit(solution)/shard_map/ppermute | solution.py:121
  50.8 11.2 %collective-permute-start.27 = (bf16[1024,128]{1,0:T(8,128)(2,1)S(1)}, bf16[1024,128]{1,0:T(8,128)(2,1)S(1)}, u32[]{:S(2)}, u32[]{:S(2)}) collective-permute-start(bf16[1024,128]{1,0:T(8,128)(2,1)S(1)} %pad_maximum_fusion.9.refs_0_), channel_id=1, source_target_pairs={{0,8},{1,9},{2,10},{3,11},{4,12},{5,13},{6,14},{7,15},{8,0},{9,1},... | collective-permute-start | bytes 786440 | tf_op jit(solution)/shard_map/ppermute | solution.py:121
  56.4 8.7 %collective-permute-start.30 = (bf16[1024,128]{1,0:T(8,128)(2,1)S(1)}, bf16[1024,128]{1,0:T(8,128)(2,1)S(1)}, u32[]{:S(2)}, u32[]{:S(2)}) collective-permute-start(bf16[1024,128]{1,0:T(8,128)(2,1)S(1)} %pad_maximum_fusion.11), channel_id=1, source_target_pairs={{0,17},{1,16},{2,19},{3,18},{4,21},{5,20},{6,23},{7,22},{8,25},{9,... | collective-permute-start | bytes 786440 | tf_op jit(solution)/shard_map/ppermute | solution.py:121
  56.6 10.0 %collective-permute-start.10 = (f16[512,128]{1,0:T(8,128)(2,1)S(1)}, f16[512,128]{1,0:T(8,128)(2,1)S(1)}, u32[]{:S(2)}, u32[]{:S(2)}) collective-permute-start(f16[512,128]{1,0:T(8,128)(2,1)S(1)} %fusion.4), channel_id=1, source_target_pairs={{0,4},{1,5},{2,6},{3,7},{4,0},{5,1},{6,2},{7,3},{8,12},{9,13},{10,... | collective-permute-start | bytes 393224 | tf_op jit(solution)/shard_map/ppermute | solution.py:121
  59.3 11.5 %collective-permute-start.17 = (f16[2,512,128]{2,1,0:T(8,128)(2,1)S(1)}, f16[2,512,128]{2,1,0:T(8,128)(2,1)S(1)}, u32[]{:S(2)}, u32[]{:S(2)}) collective-permute-start(f16[2,512,128]{2,1,0:T(8,128)(2,1)S(1)} %slice_convert_fusion.2), channel_id=1, source_target_pairs={{0,2},{1,3},{2,0},{3,1},{4,6},{5,7},{6,4},{7,5},{8,10},{9,11},{10,... | collective-permute-start | bytes 786440 | tf_op jit(solution)/shard_map/ppermute | solution.py:121
  60.1 12.1 %collective-permute-start.23 = (bf16[1024,128]{1,0:T(8,128)(2,1)S(1)}, bf16[1024,128]{1,0:T(8,128)(2,1)S(1)}, u32[]{:S(2)}, u32[]{:S(2)}) collective-permute-start(bf16[1024,128]{1,0:T(8,128)(2,1)S(1)} %collective-permute-done.19.refs_2_), channel_id=1, source_target_pairs={{0,16},{1,17},{2,18},{3,19},{4,20},{5,21},{6,22},{7,23},{8,24},{9,... | collective-permute-start | bytes 786440 | tf_op jit(solution)/shard_map/ppermute | solution.py:121
  62.0 11.2 %collective-permute-start.24 = (bf16[1024,128]{1,0:T(8,128)(2,1)S(1)}, bf16[1024,128]{1,0:T(8,128)(2,1)S(1)}, u32[]{:S(2)}, u32[]{:S(2)}) collective-permute-start(bf16[1024,128]{1,0:T(8,128)(2,1)S(1)} %collective-permute-done.22.refs_5_), channel_id=1, source_target_pairs={{0,8},{1,9},{2,10},{3,11},{4,12},{5,13},{6,14},{7,15},{8,0},{9,1},... | collective-permute-start | bytes 786440 | tf_op jit(solution)/shard_map/ppermute | solution.py:121
  65.0 13.3 %collective-permute-start.28 = (bf16[1024,128]{1,0:T(8,128)(2,1)S(1)}, bf16[1024,128]{1,0:T(8,128)(2,1)S(1)}, u32[]{:S(2)}, u32[]{:S(2)}) collective-permute-start(bf16[1024,128]{1,0:T(8,128)(2,1)S(1)} %pad_maximum_fusion.11), channel_id=1, source_target_pairs={{0,9},{1,8},{2,11},{3,10},{4,13},{5,12},{6,15},{7,14},{8,1},{9,0},... | collective-permute-start | bytes 786440 | tf_op jit(solution)/shard_map/ppermute | solution.py:121
  66.6 12.5 %collective-permute-start.29 = (bf16[1024,128]{1,0:T(8,128)(2,1)S(1)}, bf16[1024,128]{1,0:T(8,128)(2,1)S(1)}, u32[]{:S(2)}, u32[]{:S(2)}) collective-permute-start(bf16[1024,128]{1,0:T(8,128)(2,1)S(1)} %pad_maximum_fusion.9.refs_0_), channel_id=1, source_target_pairs={{0,16},{1,17},{2,18},{3,19},{4,20},{5,21},{6,22},{7,23},{8,24},{9,... | collective-permute-start | bytes 786440 | tf_op jit(solution)/shard_map/ppermute | solution.py:121
  70.8 10.9 %collective-permute-start.31 = (bf16[1024,128]{1,0:T(8,128)(2,1)S(1)}, bf16[1024,128]{1,0:T(8,128)(2,1)S(1)}, u32[]{:S(2)}, u32[]{:S(2)}) collective-permute-start(bf16[1024,128]{1,0:T(8,128)(2,1)S(1)} %collective-permute-done.27.refs_2_), channel_id=1, source_target_pairs={{0,16},{1,17},{2,18},{3,19},{4,20},{5,21},{6,22},{7,23},{8,24},{9,... | collective-permute-start | bytes 786440 | tf_op jit(solution)/shard_map/ppermute | solution.py:121
  72.2 10.3 %collective-permute-start.32 = (bf16[1024,128]{1,0:T(8,128)(2,1)S(1)}, bf16[1024,128]{1,0:T(8,128)(2,1)S(1)}, u32[]{:S(2)}, u32[]{:S(2)}) collective-permute-start(bf16[1024,128]{1,0:T(8,128)(2,1)S(1)} %collective-permute-done.30.refs_5_), channel_id=1, source_target_pairs={{0,8},{1,9},{2,10},{3,11},{4,12},{5,13},{6,14},{7,15},{8,0},{9,1},... | collective-permute-start | bytes 786440 | tf_op jit(solution)/shard_map/ppermute | solution.py:121
  73.2 13.0 %collective-permute-start.18 = (f16[512,128]{1,0:T(8,128)(2,1)S(1)}, f16[512,128]{1,0:T(8,128)(2,1)S(1)}, u32[]{:S(2)}, u32[]{:S(2)}) collective-permute-start(f16[512,128]{1,0:T(8,128)(2,1)S(1)} %fusion.5), channel_id=1, source_target_pairs={{0,4},{1,5},{2,6},{3,7},{4,0},{5,1},{6,2},{7,3},{8,12},{9,13},{10,... | collective-permute-start | bytes 393224 | tf_op jit(solution)/shard_map/ppermute | solution.py:121
  78.3 8.4 %collective-permute-start.25 = (f16[2,512,128]{2,1,0:T(8,128)(2,1)S(1)}, f16[2,512,128]{2,1,0:T(8,128)(2,1)S(1)}, u32[]{:S(2)}, u32[]{:S(2)}) collective-permute-start(f16[2,512,128]{2,1,0:T(8,128)(2,1)S(1)} %slice_convert_fusion.1), channel_id=1, source_target_pairs={{0,2},{1,3},{2,0},{3,1},{4,6},{5,7},{6,4},{7,5},{8,10},{9,11},{10,... | collective-permute-start | bytes 786440 | tf_op jit(solution)/shard_map/ppermute | solution.py:121
  85.7 10.9 %collective-permute-start.33 = (f16[2,512,128]{2,1,0:T(8,128)(2,1)S(1)}, f16[2,512,128]{2,1,0:T(8,128)(2,1)S(1)}, u32[]{:S(2)}, u32[]{:S(2)}) collective-permute-start(f16[2,512,128]{2,1,0:T(8,128)(2,1)S(1)} %slice_convert_fusion), channel_id=1, source_target_pairs={{0,2},{1,3},{2,0},{3,1},{4,6},{5,7},{6,4},{7,5},{8,10},{9,11},{10,... | collective-permute-start | bytes 786440 | tf_op jit(solution)/shard_map/ppermute | solution.py:121
  86.8 11.0 %collective-permute-start.26 = (f16[512,128]{1,0:T(8,128)(2,1)S(1)}, f16[512,128]{1,0:T(8,128)(2,1)S(1)}, u32[]{:S(2)}, u32[]{:S(2)}) collective-permute-start(f16[512,128]{1,0:T(8,128)(2,1)S(1)} %fusion.6), channel_id=1, source_target_pairs={{0,4},{1,5},{2,6},{3,7},{4,0},{5,1},{6,2},{7,3},{8,12},{9,13},{10,... | collective-permute-start | bytes 393224 | tf_op jit(solution)/shard_map/ppermute | solution.py:121
  96.7 8.0 %collective-permute-start.34 = (f16[512,128]{1,0:T(8,128)(2,1)S(1)}, f16[512,128]{1,0:T(8,128)(2,1)S(1)}, u32[]{:S(2)}, u32[]{:S(2)}) collective-permute-start(f16[512,128]{1,0:T(8,128)(2,1)S(1)} %fusion.7), channel_id=1, source_target_pairs={{0,4},{1,5},{2,6},{3,7},{4,0},{5,1},{6,2},{7,3},{8,12},{9,13},{10,... | collective-permute-start | bytes 393224 | tf_op jit(solution)/shard_map/ppermute | solution.py:121

commit v3 on v2

--- a/solution.py
+++ b/solution.py
@@ -11,27 +11,19 @@
 AMPLITUDE_MAX = 6.0
 INTEGRAL_MAX = 0.1875
 HALF_MAX = 65504.0
-SHARES = (1, 1, 1, 1)
+SHARES = (2, 2, 2, 2)
 ORDER = (('near', 0), ('rest', 0), ('near', 1), ('far', 0), ('rest', 1), ('near', 2), ('far', 1), ('rest', 2), ('near', 3), ('far', 2), ('rest', 3), ('far', 3))
 DEPTH = 4
 STRICT = 1
-ZMODE = ('pair', 'pair', 'pair', 'pair')
-RAW_SWAP = True
-SWAP_CUTS = 1
-SWAP_WHOLE = True
-LATE = False
+ZSPLIT = (1, 1, 2, 2)
 GATES = {('far', 1): [('product', 0)], ('far', 2): [('product', 1)], ('rest', 3): [('pair', 0)], ('product', 2): [('pair', 1)], ('product', 3): [('product', 2)], ('near', 2): ['masked']}
-ROW_TILE = 256
-VMEM_LIMIT = 14680064
+ROW_TILE = 512
+VMEM_LIMIT = 14 * 1024 * 1024
 
 
 def masked_amplitudes(amplitudes, ij_irrep, cd_irrep):
     rows, columns = ij_irrep.astype(amplitudes.dtype), cd_irrep.astype(amplitudes.dtype)
     return jnp.where(rows[:, None] == columns[None, :], amplitudes, jnp.zeros_like(amplitudes))
-
-
-def in_vmem(array):
-    return pltpu.with_memory_space_constraint(array, pltpu.VMEM)
 
 
 def plain_body(amplitudes, integrals, ij_irrep, cd_irrep):
@@ -132,7 +124,7 @@
     def body(amplitudes, integrals, ij_irrep, cd_irrep):
         depth, columns = integrals.shape
         width = columns // 2
-        bound = 2 * depth * AMPLITUDE_MAX * INTEGRAL_MAX
+        bound = 4 * depth * AMPLITUDE_MAX * INTEGRAL_MAX
         scale = 2.0 ** math.floor(math.log2(HALF_MAX / bound))
         core = lax.axis_index("vir") % 2
         chip = lax.axis_index("vir") // 2
@@ -154,27 +146,13 @@
         first = (piece(columns_of(integrals, core), 0), piece(columns_of(integrals, 1 - core), 0))
         first, integrals = lax.optimization_barrier((first, integrals))
         mine, theirs = columns_of(integrals, core), columns_of(integrals, 1 - core)
-        theirs_late, cd_late = theirs, cd_irrep
-        if RAW_SWAP:
-            cut = amplitudes.shape[0] // SWAP_CUTS
-            chunks = [to_core(amplitudes[at : at + cut]) for at in range(0, amplitudes.shape[0], cut)]
-            other_raw = jnp.concatenate(chunks, axis=0) if SWAP_CUTS > 1 else chunks[0]
-            if LATE:
-                theirs_late, cd_late, other_raw = lax.optimization_barrier((theirs, cd_irrep, other_raw))
-            own_amps = masked_amplitudes(amplitudes, ij_irrep, cd_irrep)
-            other_amps = masked_amplitudes(other_raw, ij_irrep, to_core(cd_late))
-        else:
-            if LATE:
-                amplitudes, _ = lax.optimization_barrier((amplitudes, first))
-            own_amps = masked_amplitudes(amplitudes, ij_irrep, cd_irrep)
-            other_amps = to_core(own_amps)
+        other_raw = to_core(amplitudes)
+        own_amps = masked_amplitudes(amplitudes, ij_irrep, cd_irrep)
+        other_amps = masked_amplitudes(other_raw, ij_irrep, to_core(cd_irrep))
         same = [first[0]] + [piece(mine, g) for g in granules[1:]]
         cross = [first[1]] + [piece(theirs, g) for g in granules[1:]]
-        if SWAP_WHOLE:
-            swapped = to_core(theirs_late)
-            swapped = [piece(swapped, g) for g in granules]
-        else:
-            swapped = [to_core(block) for block in cross]
+        swapped = to_core(theirs)
+        swapped = [piece(swapped, g) for g in granules]
 
         values, on_x, on_y, sums = {"masked": (own_amps, other_amps)}, {}, {}, {}
         order = list(ORDER)
@@ -209,28 +187,15 @@
                 on_y["far", g], on_x["far", g],
             ]
             pieces = gated(pieces, ("product", g))
-            pairwise = ZMODE[g] == "pair"
-            slots = hops // 2 + 2 * (hops % 2) if pairwise else owners if ZMODE[g] == "swap" else hops
+            slots = hops // 2 + 2 * (hops % 2)
             partials = product(slots, own_amps, other_amps, pieces, scale, depth)
             values["product", g] = partials
-            if pairwise:
-                kept, sent = partials[:2], partials[2:].astype(jnp.float16)
-                pair = kept + along_z(sent, 1).astype(jnp.float32)
-                values["pair", g] = pair
-                sums[g] = pair[0] + along_z(pair[1].astype(jnp.float16), 2).astype(jnp.float32)
-            elif ZMODE[g] == "swap":
-                groups = [[z * 2 + k for z in range(chips_z)] for k in range(2)]
-                halved = partials.astype(jnp.float16)
-                arrived = lax.all_to_all(halved, "vir", 0, 0, axis_index_groups=groups, tiled=True)
-                sums[g] = arrived.astype(jnp.float32).sum(axis=0)
-            else:
-                halved = partials.astype(jnp.float16)
-                sums[g] = partials[0]
-                for hop in range(1, chips_z):
-                    arrived = along_z(halved[hop], hop)
-                    if hop == 1:
-                        values["pair", g] = arrived
-                    sums[g] += arrived.astype(jnp.float32)
+            parts = []
+            for kept in jnp.split(partials, ZSPLIT[g], axis=1):
+                pair = kept[:2] + along_z(kept[2:].astype(jnp.float16), 1).astype(jnp.float32)
+                parts.append(pair[0] + along_z(pair[1].astype(jnp.float16), 2).astype(jnp.float32))
+            values["pair", g] = pair
+            sums[g] = jnp.concatenate(parts, axis=0) if len(parts) > 1 else parts[0]
             values["sum", g] = sums[g]
         return total([sums[g] for g in granules], 1.0 / scale, amplitudes.shape[0], width)
 

time: 106 us -> 105 us (level)
  waiting for transfers between devices: 35.3 us -> 28.6 us
  starting transfers between devices: 42.3 us -> 47.6 us
    ppermute x35 -> x39, waiting for transfers between devices: 35.3 us -> 28.6 us  [send(): return lax.ppermute(array, ('occ', 'vir'), pairs)]
    ppermute x35 -> x39, starting transfers between devices: 42.3 us -> 47.6 us  [send(): return lax.ppermute(array, ('occ', 'vir'), pairs)]
  transfers between devices with their start and end apart: 35 -> 39, of which waited for: 16 -> 17; matrix products, arithmetic and copies ran while one was open for 13% -> 13% of each run, Pallas kernels for 12% -> 12%
where the time goes in v3:
time: 105 us
  starting transfers between devices  47.6 us (45%)
  waiting for transfers between devices  28.6 us (27%)
  Pallas kernels  14.4 us (14%)
  other arithmetic  7.3 us (7%)
  local copies, waits for them, and re-layouts  6.9 us (7%)
    ppermute x39, starting transfers between devices, send(): return lax.ppermute(array, ('occ', 'vir'), pairs)  47.6 us
    ppermute x39, waiting for transfers between devices, send(): return lax.ppermute(array, ('occ', 'vir'), pairs)  28.6 us
    pallas_call x4, Pallas kernels, product(): pl.pallas_call(functools.partial(product_kernel, scale), in_specs=[pl.Blo...  12.9 us
    split x3, local copies, waits for them, and re-layouts, piece(): return jnp.concatenate(jnp.split(cut, folds), axis=1)  5.73 us
    concatenate x11, other arithmetic, piece(): return jnp.concatenate(jnp.split(cut, folds), axis=1)  3.64 us
    select_n x1, other arithmetic, masked_amplitudes(): jnp.where(rows[:, None] == columns[None, :], amplitudes, jnp.zeros_like(a...  2.93 us
  transfers between devices with their start and end apart: 39, of which 17 were waited for; matrix products, arithmetic and copies ran while one was open for 13% of the time, Pallas kernels for 12%

profile of v3, /device:TPU:0, one launch (start us, length us, event | category | flops | bytes accessed | tf_op | source)
XLA Modules:
  0.0 105.3 jit_solution(3378783239761041033)
XLA Ops:
  0.5 1.8 %constant_dynamic-slice_fusion.4 = (bf16[1024,64]{1,0:T(8,128)(2,1)S(1)}, bf16[1024,64]{1,0:T(8,128)(2,1)S(1)}, bf16[1024,64]{1,0:T(8,128)(2,1)S(1)}, bf16[1024,64]{1,0:T(8,128)(2,1)S(1)}) fusion(bf16[2048,512]{1,0:T(8,128)(2,1)} %param.5, s32[]{:T(128)S(6)} %select_n.53, s32[]{:T(128)S(6)} %select_n.52, s32[]{:T(128)S(6)} %add.85), kind=kLoop, calls=%fused_computation.52 | loop fusion | bytes 1048588 | tf_op jit(solution)/shard_map/split | solution.py:141
  2.2 1.0 pad_maximum_fusion
  3.2 1.0 constant_dynamic-slice_fusion.7
  4.8 2.5 %collective-permute-start.3 = (bf16[1024,128]{1,0:T(8,128)(2,1)S(1)}, bf16[1024,128]{1,0:T(8,128)(2,1)S(1)}, u32[]{:S(2)}, u32[]{:S(2)}) collective-permute-start(bf16[1024,128]{1,0:T(8,128)(2,1)S(1)} %get-tuple-element.48.refs_0_), channel_id=1, source_target_pairs={{0,8},{1,9},{2,10},{3,11},{4,12},{5,13},{6,14},{7,15},{8,0},{9,1},... | collective-permute-start | bytes 786440 | tf_op jit(solution)/shard_map/ppermute | solution.py:113
  7.3 1.2 %collective-permute-start.6 = (bf16[1024,128]{1,0:T(8,128)(2,1)}, bf16[1024,128]{1,0:T(8,128)(2,1)S(1)}, u32[]{:S(2)}, u32[]{:S(2)}) collective-permute-start(bf16[1024,128]{1,0:T(8,128)(2,1)} %get-tuple-element.50), channel_id=1, source_target_pairs={{0,17},{1,16},{2,19},{3,18},{4,21},{5,20},{6,23},{7,22},{8,25},{9,... | collective-permute-start | bytes 786440 | tf_op jit(solution)/shard_map/ppermute | solution.py:113
  8.4 2.0 %constant_dynamic-slice_fusion.2 = (bf16[1024,64]{1,0:T(8,128)(2,1)}, bf16[1024,64]{1,0:T(8,128)(2,1)}, bf16[1024,64]{1,0:T(8,128)(2,1)}, bf16[1024,64]{1,0:T(8,...) fusion(bf16[2048,512]{1,0:T(8,128)(2,1)S(1)} %copy-done, ...), kind=kLoop, calls=%fused_computation.50 | loop fusion | bytes 3145756 | tf_op jit(solution)/shard_map/split | solution.py:141
  11.1 1.3 %pad_maximum_fusion.10.refs_0_ = bf16[1024,128]{1,0:T(8,128)(2,1)S(1)} fusion(bf16[1024,64]{1,0:T(8,128)(2,1)} %get-tuple-element.102, bf16[1024,64]{1,0:T(8,128)(2,1)} %get-tuple-element.93), kind=kLoop, calls=%fused_computation.26 | loop fusion | flops 524288 | bytes 524288 | tf_op jit(solution)/shard_map/concatenate | solution.py:141
  13.2 0.8 collective-permute-done.3.refs_2_
  14.0 1.8 %collective-permute-start.5 = (bf16[1024,128]{1,0:T(8,128)(2,1)S(1)}, bf16[1024,128]{1,0:T(8,128)(2,1)S(1)}, u32[]{:S(2)}, u32[]{:S(2)}) collective-permute-start(bf16[1024,128]{1,0:T(8,128)(2,1)S(1)} %get-tuple-element.48.refs_0_), channel_id=1, source_target_pairs={{0,16},{1,17},{2,18},{3,19},{4,20},{5,21},{6,22},{7,23},{8,24},{9,... | collective-permute-start | bytes 786440 | tf_op jit(solution)/shard_map/ppermute | solution.py:113
  15.9 2.1 %collective-permute-start.11 = (bf16[1024,128]{1,0:T(8,128)(2,1)S(1)}, bf16[1024,128]{1,0:T(8,128)(2,1)S(1)}, u32[]{:S(2)}, u32[]{:S(2)}) collective-permute-start(bf16[1024,128]{1,0:T(8,128)(2,1)S(1)} %pad_maximum_fusion.3.refs_0_), channel_id=1, source_target_pairs={{0,8},{1,9},{2,10},{3,11},{4,12},{5,13},{6,14},{7,15},{8,0},{9,1},... | collective-permute-start | bytes 786440 | tf_op jit(solution)/shard_map/ppermute | solution.py:113
  17.9 1.9 %fusion.14 = (bf16[1024,64]{1,0:T(8,128)(2,1)S(1)}, bf16[1024,64]{1,0:T(8,128)(2,1)S(1)}, bf16[1024,64]{1,0:T(8,128)(2,1)S(1)}, bf16[1024,64]{1,0:T(8,128)(2,1)S...) fusion(bf16[2048,256]{1,0:T(8,128)(2,1)} %collective-permute-done.2), kind=kLoop, calls=%fused_computation.64 | loop fusion | bytes 2097152 | tf_op jit(solution)/shard_map/split | solution.py:141
  20.0 1.5 %collective-permute-start.8 = (bf16[1024,128]{1,0:T(8,128)(2,1)S(1)}, bf16[1024,128]{1,0:T(8,128)(2,1)S(1)}, u32[]{:S(2)}, u32[]{:S(2)}) collective-permute-start(bf16[1024,128]{1,0:T(8,128)(2,1)S(1)} %collective-permute-done.6.refs_5_), channel_id=1, source_target_pairs={{0,8},{1,9},{2,10},{3,11},{4,12},{5,13},{6,14},{7,15},{8,0},{9,1},... | collective-permute-start | bytes 786440 | tf_op jit(solution)/shard_map/ppermute | solution.py:113
  21.5 2.9 %compare_select_fusion = (bf16[1024,2048]{1,0:T(8,128)(2,1)S(1)}, bf16[1024,2048]{1,0:T(8,128)(2,1)S(1)}) fusion(bf16[1024,2048]{1,0:T(8,128)(2,1)} %collective-permute-done.1, bf16[2048]{0:T(1024)(128)(2,1)S(1)} %convert_element_type.78, bf16[1024]{0:T(1024)(128)(2,1)S(1)} %convert_element_type.76, bf16[1024,2048]{1,0:T(8,128)(2,1)S(1)} %copy-done.1, ...), kind=kLoop, calls=%fused_computation | loop fusion | flops 8388608 | bytes 16787456 | tf_op jit(solution)/shard_map/jit(_where)/select_n | solution.py:26
  24.6 2.3 %collective-permute-start.12 = (bf16[1024,128]{1,0:T(8,128)(2,1)S(1)}, bf16[1024,128]{1,0:T(8,128)(2,1)S(1)}, u32[]{:S(2)}, u32[]{:S(2)}) collective-permute-start(bf16[1024,128]{1,0:T(8,128)(2,1)S(1)} %pad_maximum_fusion.5), channel_id=1, source_target_pairs={{0,9},{1,8},{2,11},{3,10},{4,13},{5,12},{6,15},{7,14},{8,1},{9,0},... | collective-permute-start | bytes 786440 | tf_op jit(solution)/shard_map/ppermute | solution.py:113
  26.8 1.0 collective-permute-done.7.refs_6_
  27.8 2.3 %collective-permute-start.13 = (bf16[1024,128]{1,0:T(8,128)(2,1)S(1)}, bf16[1024,128]{1,0:T(8,128)(2,1)S(1)}, u32[]{:S(2)}, u32[]{:S(2)}) collective-permute-start(bf16[1024,128]{1,0:T(8,128)(2,1)S(1)} %pad_maximum_fusion.3.refs_0_), channel_id=1, source_target_pairs={{0,16},{1,17},{2,18},{3,19},{4,20},{5,21},{6,22},{7,23},{8,24},{9,... | collective-permute-start | bytes 786440 | tf_op jit(solution)/shard_map/ppermute | solution.py:113
  30.1 3.1 %collective-permute-done.8.refs_7_ = bf16[1024,128]{1,0:T(8,128)(2,1)S(1)} collective-permute-done((bf16[1024,128]{1,0:T(8,128)(2,1)S(1)}, bf16[1024,128]{1,0:T(8,128)(2,1)S(1)}, u32[]{:S(2)}, u32[]{:S(2)}) %collective-permute-start.8) | collective-permute-done | bytes 262176 | tf_op jit(solution)/shard_map/ppermute | solution.py:113
  33.2 3.2 %shard_map.46 = f32[4,512,128]{2,1,0:T(8,128)S(1)} custom-call(s32[4]{0:T(128)S(1)} %fusion.13.slot_ref, bf16[1024,2048]{1,0:T(8,128)(2,1)S(1)} %get-tuple-element.124.own_amps, bf16[1024,2048]{1,0:T(8,128)(2,1)S(1)} %get-tuple-element.123.other_amps, bf16[1024,128]{1,0:T(8,128)(2,1)S(1)} %get-tuple-element.48.refs_0_, ...), custom_call_target="tpu_custom_call" | custom-call | tf_op jit(solution)/shard_map/pallas_call | solution.py:64
  36.5 1.6 %collective-permute-start.9 = (f16[2,512,128]{2,1,0:T(8,128)(2,1)S(1)}, f16[2,512,128]{2,1,0:T(8,128)(2,1)S(1)}, u32[]{:S(2)}, u32[]{:S(2)}) collective-permute-start(f16[2,512,128]{2,1,0:T(8,128)(2,1)S(1)} %slice_convert_fusion.1), channel_id=1, source_target_pairs={{0,2},{1,3},{2,0},{3,1},{4,6},{5,7},{6,4},{7,5},{8,10},{9,11},{10,... | collective-permute-start | bytes 786440 | tf_op jit(solution)/shard_map/ppermute | solution.py:113
  39.3 1.5 %collective-permute-start.15 = (bf16[1024,128]{1,0:T(8,128)(2,1)S(1)}, bf16[1024,128]{1,0:T(8,128)(2,1)S(1)}, u32[]{:S(2)}, u32[]{:S(2)}) collective-permute-start(bf16[1024,128]{1,0:T(8,128)(2,1)S(1)} %collective-permute-done.11.refs_2_), channel_id=1, source_target_pairs={{0,16},{1,17},{2,18},{3,19},{4,20},{5,21},{6,22},{7,23},{8,24},{9,... | collective-permute-start | bytes 786440 | tf_op jit(solution)/shard_map/ppermute | solution.py:113
  40.8 1.5 %collective-permute-start.16 = (bf16[1024,128]{1,0:T(8,128)(2,1)S(1)}, bf16[1024,128]{1,0:T(8,128)(2,1)S(1)}, u32[]{:S(2)}, u32[]{:S(2)}) collective-permute-start(bf16[1024,128]{1,0:T(8,128)(2,1)S(1)} %collective-permute-done.14.refs_5_), channel_id=1, source_target_pairs={{0,8},{1,9},{2,10},{3,11},{4,12},{5,13},{6,14},{7,15},{8,0},{9,1},... | collective-permute-start | bytes 786440 | tf_op jit(solution)/shard_map/ppermute | solution.py:113
  42.8 0.9 collective-permute-done.9
  43.8 4.7 %collective-permute-done.15.refs_6_ = bf16[1024,128]{1,0:T(8,128)(2,1)S(1)} collective-permute-done((bf16[1024,128]{1,0:T(8,128)(2,1)S(1)}, bf16[1024,128]{1,0:T(8,128)(2,1)S(1)}, u32[]{:S(2)}, u32[]{:S(2)}) %collective-permute-start.15) | collective-permute-done | bytes 262176 | tf_op jit(solution)/shard_map/ppermute | solution.py:113
  48.5 1.2 %collective-permute-start.21 = (bf16[1024,128]{1,0:T(8,128)(2,1)S(1)}, bf16[1024,128]{1,0:T(8,128)(2,1)S(1)}, u32[]{:S(2)}, u32[]{:S(2)}) collective-permute-start(bf16[1024,128]{1,0:T(8,128)(2,1)S(1)} %pad_maximum_fusion.6.refs_0_), channel_id=1, source_target_pairs={{0,16},{1,17},{2,18},{3,19},{4,20},{5,21},{6,22},{7,23},{8,24},{9,... | collective-permute-start | bytes 786440 | tf_op jit(solution)/shard_map/ppermute | solution.py:113
  49.7 1.2 %collective-permute-done.16.refs_7_ = bf16[1024,128]{1,0:T(8,128)(2,1)S(1)} collective-permute-done((bf16[1024,128]{1,0:T(8,128)(2,1)S(1)}, bf16[1024,128]{1,0:T(8,128)(2,1)S(1)}, u32[]{:S(2)}, u32[]{:S(2)}) %collective-permute-start.16) | collective-permute-done | bytes 262176 | tf_op jit(solution)/shard_map/ppermute | solution.py:113
  50.8 2.4 %collective-permute-start.29 = (bf16[1024,128]{1,0:T(8,128)(2,1)S(1)}, bf16[1024,128]{1,0:T(8,128)(2,1)S(1)}, u32[]{:S(2)}, u32[]{:S(2)}) collective-permute-start(bf16[1024,128]{1,0:T(8,128)(2,1)S(1)} %pad_maximum_fusion.10.refs_0_), channel_id=1, source_target_pairs={{0,8},{1,9},{2,10},{3,11},{4,12},{5,13},{6,14},{7,15},{8,0},{9,1},... | collective-permute-start | bytes 786440 | tf_op jit(solution)/shard_map/ppermute | solution.py:113
  53.2 3.2 %shard_map.47 = f32[4,512,128]{2,1,0:T(8,128)S(1)} custom-call(s32[4]{0:T(128)S(1)} %fusion.13.slot_ref, bf16[1024,2048]{1,0:T(8,128)(2,1)S(1)} %get-tuple-element.124.own_amps, bf16[1024,2048]{1,0:T(8,128)(2,1)S(1)} %get-tuple-element.123.other_amps, bf16[1024,128]{1,0:T(8,128)(2,1)S(1)} %pad_maximum_fusion.3.refs_0_, ...), custom_call_target="tpu_custom_call" | custom-call | tf_op jit(solution)/shard_map/pallas_call | solution.py:64
  56.7 2.6 %collective-permute-start.10 = (f16[512,128]{1,0:T(8,128)(2,1)S(1)}, f16[512,128]{1,0:T(8,128)(2,1)S(1)}, u32[]{:S(2)}, u32[]{:S(2)}) collective-permute-start(f16[512,128]{1,0:T(8,128)(2,1)S(1)} %fusion.2), channel_id=1, source_target_pairs={{0,4},{1,5},{2,6},{3,7},{4,0},{5,1},{6,2},{7,3},{8,12},{9,13},{10,... | collective-permute-start | bytes 393224 | tf_op jit(solution)/shard_map/ppermute | solution.py:113
  60.1 1.2 %collective-permute-start.23 = (bf16[1024,128]{1,0:T(8,128)(2,1)S(1)}, bf16[1024,128]{1,0:T(8,128)(2,1)S(1)}, u32[]{:S(2)}, u32[]{:S(2)}) collective-permute-start(bf16[1024,128]{1,0:T(8,128)(2,1)S(1)} %collective-permute-done.19.refs_2_), channel_id=1, source_target_pairs={{0,16},{1,17},{2,18},{3,19},{4,20},{5,21},{6,22},{7,23},{8,24},{9,... | collective-permute-start | bytes 786440 | tf_op jit(solution)/shard_map/ppermute | solution.py:113
  62.1 2.3 %collective-permute-start.24 = (bf16[1024,128]{1,0:T(8,128)(2,1)S(1)}, bf16[1024,128]{1,0:T(8,128)(2,1)S(1)}, u32[]{:S(2)}, u32[]{:S(2)}) collective-permute-start(bf16[1024,128]{1,0:T(8,128)(2,1)S(1)} %collective-permute-done.22.refs_5_), channel_id=1, source_target_pairs={{0,8},{1,9},{2,10},{3,11},{4,12},{5,13},{6,14},{7,15},{8,0},{9,1},... | collective-permute-start | bytes 786440 | tf_op jit(solution)/shard_map/ppermute | solution.py:113
  65.1 1.3 %collective-permute-start.30 = (bf16[1024,128]{1,0:T(8,128)(2,1)S(1)}, bf16[1024,128]{1,0:T(8,128)(2,1)S(1)}, u32[]{:S(2)}, u32[]{:S(2)}) collective-permute-start(bf16[1024,128]{1,0:T(8,128)(2,1)S(1)} %pad_maximum_fusion.12), channel_id=1, source_target_pairs={{0,9},{1,8},{2,11},{3,10},{4,13},{5,12},{6,15},{7,14},{8,1},{9,0},... | collective-permute-start | bytes 786440 | tf_op jit(solution)/shard_map/ppermute | solution.py:113
  66.8 1.0 collective-permute-start.31
  67.9 3.1 %collective-permute-done.17 = f16[2,512,128]{2,1,0:T(8,128)(2,1)S(1)} collective-permute-done((f16[2,512,128]{2,1,0:T(8,128)(2,1)S(1)}, f16[2,512,128]{2,1,0:T(8,128)(2,1)S(1)}, u32[]{:S(2)}, u32[]{:S(2)}) %collective-permute-start.17) | collective-permute-done | bytes 262176 | tf_op jit(solution)/shard_map/ppermute | solution.py:113
  71.1 1.1 %collective-permute-start.33 = (bf16[1024,128]{1,0:T(8,128)(2,1)S(1)}, bf16[1024,128]{1,0:T(8,128)(2,1)S(1)}, u32[]{:S(2)}, u32[]{:S(2)}) collective-permute-start(bf16[1024,128]{1,0:T(8,128)(2,1)S(1)} %collective-permute-done.29.refs_2_), channel_id=1, source_target_pairs={{0,16},{1,17},{2,18},{3,19},{4,20},{5,21},{6,22},{7,23},{8,24},{9,... | collective-permute-start | bytes 786440 | tf_op jit(solution)/shard_map/ppermute | solution.py:113
  72.2 1.0 collective-permute-start.34
  73.2 1.8 %collective-permute-start.18 = (f16[512,128]{1,0:T(8,128)(2,1)S(1)}, f16[512,128]{1,0:T(8,128)(2,1)S(1)}, u32[]{:S(2)}, u32[]{:S(2)}) collective-permute-start(f16[512,128]{1,0:T(8,128)(2,1)S(1)} %fusion.3), channel_id=1, source_target_pairs={{0,4},{1,5},{2,6},{3,7},{4,0},{5,1},{6,2},{7,3},{8,12},{9,13},{10,... | collective-permute-start | bytes 393224 | tf_op jit(solution)/shard_map/ppermute | solution.py:113
  75.1 3.2 %shard_map.48 = f32[4,512,128]{2,1,0:T(8,128)S(1)} custom-call(s32[4]{0:T(128)S(1)} %fusion.13.slot_ref, bf16[1024,2048]{1,0:T(8,128)(2,1)S(1)} %get-tuple-element.124.own_amps, bf16[1024,2048]{1,0:T(8,128)(2,1)S(1)} %get-tuple-element.123.other_amps, bf16[1024,128]{1,0:T(8,128)(2,1)S(1)} %pad_maximum_fusion.6.refs_0_, ...), custom_call_target="tpu_custom_call" | custom-call | tf_op jit(solution)/shard_map/pallas_call | solution.py:64
  79.2 1.3 %collective-permute-start.27 = (f16[2,256,128]{2,1,0:T(8,128)(2,1)S(1)}, f16[2,256,128]{2,1,0:T(8,128)(2,1)S(1)}, u32[]{:S(2)}, u32[]{:S(2)}) collective-permute-start(f16[2,256,128]{2,1,0:T(8,128)(2,1)S(1)} %get-tuple-element.122), channel_id=1, source_target_pairs={{0,2},{1,3},{2,0},{3,1},{4,6},{5,7},{6,4},{7,5},{8,10},{9,11},{10,... | collective-permute-start | bytes 393224 | tf_op jit(solution)/shard_map/ppermute | solution.py:113
  80.5 1.3 %collective-permute-done.33.refs_6_ = bf16[1024,128]{1,0:T(8,128)(2,1)S(1)} collective-permute-done((bf16[1024,128]{1,0:T(8,128)(2,1)S(1)}, bf16[1024,128]{1,0:T(8,128)(2,1)S(1)}, u32[]{:S(2)}, u32[]{:S(2)}) %collective-permute-start.33) | collective-permute-done | bytes 262176 | tf_op jit(solution)/shard_map/ppermute | solution.py:113
  82.5 3.2 %shard_map.49 = f32[4,512,128]{2,1,0:T(8,128)S(1)} custom-call(s32[4]{0:T(128)S(1)} %fusion.13.slot_ref, bf16[1024,2048]{1,0:T(8,128)(2,1)S(1)} %get-tuple-element.124.own_amps, bf16[1024,2048]{1,0:T(8,128)(2,1)S(1)} %get-tuple-element.123.other_amps, bf16[1024,128]{1,0:T(8,128)(2,1)S(1)} %pad_maximum_fusion.10.refs_0_, ...), custom_call_target="tpu_custom_call" | custom-call | tf_op jit(solution)/shard_map/pallas_call | solution.py:64
  86.4 1.6 %collective-permute-start.37 = (f16[2,256,128]{2,1,0:T(8,128)(2,1)S(1)}, f16[2,256,128]{2,1,0:T(8,128)(2,1)S(1)}, u32[]{:S(2)}, u32[]{:S(2)}) collective-permute-start(f16[2,256,128]{2,1,0:T(8,128)(2,1)S(1)} %get-tuple-element.120), channel_id=1, source_target_pairs={{0,2},{1,3},{2,0},{3,1},{4,6},{5,7},{6,4},{7,5},{8,10},{9,11},{10,... | collective-permute-start | bytes 393224 | tf_op jit(solution)/shard_map/ppermute | solution.py:113
  88.1 2.7 %collective-permute-start.28 = (f16[256,128]{1,0:T(8,128)(2,1)S(1)}, f16[256,128]{1,0:T(8,128)(2,1)S(1)}, u32[]{:S(2)}, u32[]{:S(2)}) collective-permute-start(f16[256,128]{1,0:T(8,128)(2,1)S(1)} %fusion.9), channel_id=1, source_target_pairs={{0,4},{1,5},{2,6},{3,7},{4,0},{5,1},{6,2},{7,3},{8,12},{9,13},{10,... | collective-permute-start | bytes 196616 | tf_op jit(solution)/shard_map/ppermute | solution.py:113
  91.2 3.3 %collective-permute-done.35 = f16[2,256,128]{2,1,0:T(8,128)(2,1)S(1)} collective-permute-done((f16[2,256,128]{2,1,0:T(8,128)(2,1)S(1)}, f16[2,256,128]{2,1,0:T(8,128)(2,1)S(1)}, u32[]{:S(2)}, u32[]{:S(2)}) %collective-permute-start.35) | collective-permute-done | bytes 131104 | tf_op jit(solution)/shard_map/ppermute | solution.py:113
  94.5 2.4 %collective-permute-done.37 = f16[2,256,128]{2,1,0:T(8,128)(2,1)S(1)} collective-permute-done((f16[2,256,128]{2,1,0:T(8,128)(2,1)S(1)}, f16[2,256,128]{2,1,0:T(8,128)(2,1)S(1)}, u32[]{:S(2)}, u32[]{:S(2)}) %collective-permute-start.37) | collective-permute-done | bytes 131104 | tf_op jit(solution)/shard_map/ppermute | solution.py:113
  96.9 1.0 collective-permute-start.38
  97.9 2.1 %collective-permute-start.36 = (f16[256,128]{1,0:T(8,128)(2,1)S(1)}, f16[256,128]{1,0:T(8,128)(2,1)S(1)}, u32[]{:S(2)}, u32[]{:S(2)}) collective-permute-start(f16[256,128]{1,0:T(8,128)(2,1)S(1)} %fusion.10), channel_id=1, source_target_pairs={{0,4},{1,5},{2,6},{3,7},{4,0},{5,1},{6,2},{7,3},{8,12},{9,13},{10,... | collective-permute-start | bytes 196616 | tf_op jit(solution)/shard_map/ppermute | solution.py:113
  100.1 3.0 %collective-permute-done.38 = f16[256,128]{1,0:T(8,128)(2,1)S(1)} collective-permute-done((f16[256,128]{1,0:T(8,128)(2,1)S(1)}, f16[256,128]{1,0:T(8,128)(2,1)S(1)}, u32[]{:S(2)}, u32[]{:S(2)}) %collective-permute-start.38) | collective-permute-done | bytes 65568 | tf_op jit(solution)/shard_map/ppermute | solution.py:113
  103.8 1.4 %shard_map.50 = f32[1024,256]{1,0:T(8,128)} custom-call(f32[512,128]{1,0:T(8,128)S(1)} %fusion.1.refs_0_, f32[512,128]{1,0:T(8,128)S(1)} %fusion.refs_1_, f32[512,128]{1,0:T(8,128)S(1)} %pad_maximum_fusion.9.refs_2_, f32[512,128]{1,0:T(8,128)S(1)} %pad_maximum_fusion.13.refs_3_), custom_call_target="tpu_custom_call" | custom-call | tf_op jit(solution)/shard_map/pallas_call | solution.py:93
  (91 shorter events, 10.9 us)
Async XLA Ops:
  0.0 3.2 %copy-start = (bf16[2048,512]{1,0:T(8,128)(2,1)S(1)}, bf16[2048,512]{1,0:T(8,128)(2,1)}, u32[]{:S(2)}) copy-start(bf16[2048,512]{1,0:T(8,128)(2,1)} %param.5) | copy-start | bytes 6291460
  0.0 4.3 %copy-start.4 = (s32[2048]{0:T(1024)S(1)}, s32[2048]{0:T(1024)}, u32[]{:S(2)}) copy-start(s32[2048]{0:T(1024)} %param.7) | copy-start | bytes 24580
  0.0 20.0 %collective-permute-start.1 = (bf16[1024,2048]{1,0:T(8,128)(2,1)}, bf16[1024,2048]{1,0:T(8,128)(2,1)}, u32[]{:S(2)}, u32[]{:S(2)}) collective-permute-start(bf16[1024,2048]{1,0:T(8,128)(2,1)} %param.4), channel_id=1, source_target_pairs={{0,1},{1,0},{2,3},{3,2},{4,5},{5,4},{6,7},{7,6},{8,9},{9,8},{10,11... | collective-permute-start | bytes 12582920 | tf_op jit(solution)/shard_map/ppermute | solution.py:113
  4.3 13.7 %collective-permute-start.2 = (bf16[2048,256]{1,0:T(8,128)(2,1)}, bf16[2048,256]{1,0:T(8,128)(2,1)}, u32[]{:S(2)}, u32[]{:S(2)}) collective-permute-start(bf16[2048,256]{1,0:T(8,128)(2,1)} %constant_dynamic-slice_fusion.7), channel_id=1, source_target_pairs={{0,1},{1,0},{2,3},{3,2},{4,5},{5,4},{6,7},{7,6},{8,9},{9,8},{10,11... | collective-permute-start | bytes 3145736 | tf_op jit(solution)/shard_map/ppermute | solution.py:113
  4.3 8.2 %collective-permute-start = (s32[2048]{0:T(1024)S(1)}, s32[2048]{0:T(1024)S(1)}, u32[]{:S(2)}, u32[]{:S(2)}) collective-permute-start(s32[2048]{0:T(1024)S(1)} %copy-done.4), channel_id=1, source_target_pairs={{0,1},{1,0},{2,3},{3,2},{4,5},{5,4},{6,7},{7,6},{8,9},{9,8},{10,11... | collective-permute-start | bytes 24584 | tf_op jit(solution)/shard_map/ppermute | solution.py:113
  4.8 9.3 %collective-permute-start.3 = (bf16[1024,128]{1,0:T(8,128)(2,1)S(1)}, bf16[1024,128]{1,0:T(8,128)(2,1)S(1)}, u32[]{:S(2)}, u32[]{:S(2)}) collective-permute-start(bf16[1024,128]{1,0:T(8,128)(2,1)S(1)} %get-tuple-element.48.refs_0_), channel_id=1, source_target_pairs={{0,8},{1,9},{2,10},{3,11},{4,12},{5,13},{6,14},{7,15},{8,0},{9,1},... | collective-permute-start | bytes 786440 | tf_op jit(solution)/shard_map/ppermute | solution.py:113
  7.3 8.6 %collective-permute-start.6 = (bf16[1024,128]{1,0:T(8,128)(2,1)}, bf16[1024,128]{1,0:T(8,128)(2,1)S(1)}, u32[]{:S(2)}, u32[]{:S(2)}) collective-permute-start(bf16[1024,128]{1,0:T(8,128)(2,1)} %get-tuple-element.50), channel_id=1, source_target_pairs={{0,17},{1,16},{2,19},{3,18},{4,21},{5,20},{6,23},{7,22},{8,25},{9,... | collective-permute-start | bytes 786440 | tf_op jit(solution)/shard_map/ppermute | solution.py:113
  8.4 4.1 %copy-start.5 = (s32[1024]{0:T(1024)S(1)}, s32[1024]{0:T(1024)}, u32[]{:S(2)}) copy-start(s32[1024]{0:T(1024)} %param.6) | copy-start | bytes 12292
  11.1 10.4 %copy-start.1 = (bf16[1024,2048]{1,0:T(8,128)(2,1)S(1)}, bf16[1024,2048]{1,0:T(8,128)(2,1)}, u32[]{:S(2)}) copy-start(bf16[1024,2048]{1,0:T(8,128)(2,1)} %param.4) | copy-start | bytes 12582916
  12.5 12.0 %collective-permute-start.4 = (bf16[1024,128]{1,0:T(8,128)(2,1)}, bf16[1024,128]{1,0:T(8,128)(2,1)S(1)}, u32[]{:S(2)}, u32[]{:S(2)}) collective-permute-start(bf16[1024,128]{1,0:T(8,128)(2,1)} %get-tuple-element.50), channel_id=1, source_target_pairs={{0,9},{1,8},{2,11},{3,10},{4,13},{5,12},{6,15},{7,14},{8,1},{9,0},... | collective-permute-start | bytes 786440 | tf_op jit(solution)/shard_map/ppermute | solution.py:113
  14.0 10.5 %collective-permute-start.5 = (bf16[1024,128]{1,0:T(8,128)(2,1)S(1)}, bf16[1024,128]{1,0:T(8,128)(2,1)S(1)}, u32[]{:S(2)}, u32[]{:S(2)}) collective-permute-start(bf16[1024,128]{1,0:T(8,128)(2,1)S(1)} %get-tuple-element.48.refs_0_), channel_id=1, source_target_pairs={{0,16},{1,17},{2,18},{3,19},{4,20},{5,21},{6,22},{7,23},{8,24},{9,... | collective-permute-start | bytes 786440 | tf_op jit(solution)/shard_map/ppermute | solution.py:113
  15.9 22.5 %collective-permute-start.11 = (bf16[1024,128]{1,0:T(8,128)(2,1)S(1)}, bf16[1024,128]{1,0:T(8,128)(2,1)S(1)}, u32[]{:S(2)}, u32[]{:S(2)}) collective-permute-start(bf16[1024,128]{1,0:T(8,128)(2,1)S(1)} %pad_maximum_fusion.3.refs_0_), channel_id=1, source_target_pairs={{0,8},{1,9},{2,10},{3,11},{4,12},{5,13},{6,14},{7,15},{8,0},{9,1},... | collective-permute-start | bytes 786440 | tf_op jit(solution)/shard_map/ppermute | solution.py:113
  17.9 9.9 %collective-permute-start.7 = (bf16[1024,128]{1,0:T(8,128)(2,1)S(1)}, bf16[1024,128]{1,0:T(8,128)(2,1)S(1)}, u32[]{:S(2)}, u32[]{:S(2)}) collective-permute-start(bf16[1024,128]{1,0:T(8,128)(2,1)S(1)} %collective-permute-done.3.refs_2_), channel_id=1, source_target_pairs={{0,16},{1,17},{2,18},{3,19},{4,20},{5,21},{6,22},{7,23},{8,24},{9,... | collective-permute-start | bytes 786440 | tf_op jit(solution)/shard_map/ppermute | solution.py:113
  20.0 13.2 %collective-permute-start.8 = (bf16[1024,128]{1,0:T(8,128)(2,1)S(1)}, bf16[1024,128]{1,0:T(8,128)(2,1)S(1)}, u32[]{:S(2)}, u32[]{:S(2)}) collective-permute-start(bf16[1024,128]{1,0:T(8,128)(2,1)S(1)} %collective-permute-done.6.refs_5_), channel_id=1, source_target_pairs={{0,8},{1,9},{2,10},{3,11},{4,12},{5,13},{6,14},{7,15},{8,0},{9,1},... | collective-permute-start | bytes 786440 | tf_op jit(solution)/shard_map/ppermute | solution.py:113
  24.5 13.9 %collective-permute-start.14 = (bf16[1024,128]{1,0:T(8,128)(2,1)S(1)}, bf16[1024,128]{1,0:T(8,128)(2,1)S(1)}, u32[]{:S(2)}, u32[]{:S(2)}) collective-permute-start(bf16[1024,128]{1,0:T(8,128)(2,1)S(1)} %pad_maximum_fusion.5), channel_id=1, source_target_pairs={{0,17},{1,16},{2,19},{3,18},{4,21},{5,20},{6,23},{7,22},{8,25},{9,... | collective-permute-start | bytes 786440 | tf_op jit(solution)/shard_map/ppermute | solution.py:113
  24.6 13.9 %collective-permute-start.12 = (bf16[1024,128]{1,0:T(8,128)(2,1)S(1)}, bf16[1024,128]{1,0:T(8,128)(2,1)S(1)}, u32[]{:S(2)}, u32[]{:S(2)}) collective-permute-start(bf16[1024,128]{1,0:T(8,128)(2,1)S(1)} %pad_maximum_fusion.5), channel_id=1, source_target_pairs={{0,9},{1,8},{2,11},{3,10},{4,13},{5,12},{6,15},{7,14},{8,1},{9,0},... | collective-permute-start | bytes 786440 | tf_op jit(solution)/shard_map/ppermute | solution.py:113
  27.8 11.1 %collective-permute-start.13 = (bf16[1024,128]{1,0:T(8,128)(2,1)S(1)}, bf16[1024,128]{1,0:T(8,128)(2,1)S(1)}, u32[]{:S(2)}, u32[]{:S(2)}) collective-permute-start(bf16[1024,128]{1,0:T(8,128)(2,1)S(1)} %pad_maximum_fusion.3.refs_0_), channel_id=1, source_target_pairs={{0,16},{1,17},{2,18},{3,19},{4,20},{5,21},{6,22},{7,23},{8,24},{9,... | collective-permute-start | bytes 786440 | tf_op jit(solution)/shard_map/ppermute | solution.py:113
  33.2 4.9 %copy-start.2 = (bf16[1024,64]{1,0:T(8,128)(2,1)S(1)}, bf16[1024,64]{1,0:T(8,128)(2,1)}, u32[]{:S(2)}) copy-start(bf16[1024,64]{1,0:T(8,128)(2,1)} %get-tuple-element.91) | copy-start | bytes 393220
  33.2 4.9 %copy-start.3 = (bf16[1024,64]{1,0:T(8,128)(2,1)S(1)}, bf16[1024,64]{1,0:T(8,128)(2,1)}, u32[]{:S(2)}) copy-start(bf16[1024,64]{1,0:T(8,128)(2,1)} %get-tuple-element.92) | copy-start | bytes 393220
  36.5 7.2 %collective-permute-start.9 = (f16[2,512,128]{2,1,0:T(8,128)(2,1)S(1)}, f16[2,512,128]{2,1,0:T(8,128)(2,1)S(1)}, u32[]{:S(2)}, u32[]{:S(2)}) collective-permute-start(f16[2,512,128]{2,1,0:T(8,128)(2,1)S(1)} %slice_convert_fusion.1), channel_id=1, source_target_pairs={{0,2},{1,3},{2,0},{3,1},{4,6},{5,7},{6,4},{7,5},{8,10},{9,11},{10,... | collective-permute-start | bytes 786440 | tf_op jit(solution)/shard_map/ppermute | solution.py:113
  38.4 18.1 %collective-permute-start.20 = (bf16[1024,128]{1,0:T(8,128)(2,1)S(1)}, bf16[1024,128]{1,0:T(8,128)(2,1)S(1)}, u32[]{:S(2)}, u32[]{:S(2)}) collective-permute-start(bf16[1024,128]{1,0:T(8,128)(2,1)S(1)} %pad_maximum_fusion.8), channel_id=1, source_target_pairs={{0,9},{1,8},{2,11},{3,10},{4,13},{5,12},{6,15},{7,14},{8,1},{9,0},... | collective-permute-start | bytes 786440 | tf_op jit(solution)/shard_map/ppermute | solution.py:113
  39.3 9.2 %collective-permute-start.15 = (bf16[1024,128]{1,0:T(8,128)(2,1)S(1)}, bf16[1024,128]{1,0:T(8,128)(2,1)S(1)}, u32[]{:S(2)}, u32[]{:S(2)}) collective-permute-start(bf16[1024,128]{1,0:T(8,128)(2,1)S(1)} %collective-permute-done.11.refs_2_), channel_id=1, source_target_pairs={{0,16},{1,17},{2,18},{3,19},{4,20},{5,21},{6,22},{7,23},{8,24},{9,... | collective-permute-start | bytes 786440 | tf_op jit(solution)/shard_map/ppermute | solution.py:113
  40.8 10.1 %collective-permute-start.16 = (bf16[1024,128]{1,0:T(8,128)(2,1)S(1)}, bf16[1024,128]{1,0:T(8,128)(2,1)S(1)}, u32[]{:S(2)}, u32[]{:S(2)}) collective-permute-start(bf16[1024,128]{1,0:T(8,128)(2,1)S(1)} %collective-permute-done.14.refs_5_), channel_id=1, source_target_pairs={{0,8},{1,9},{2,10},{3,11},{4,12},{5,13},{6,14},{7,15},{8,0},{9,1},... | collective-permute-start | bytes 786440 | tf_op jit(solution)/shard_map/ppermute | solution.py:113
  42.3 14.5 %collective-permute-start.19 = (bf16[1024,128]{1,0:T(8,128)(2,1)S(1)}, bf16[1024,128]{1,0:T(8,128)(2,1)S(1)}, u32[]{:S(2)}, u32[]{:S(2)}) collective-permute-start(bf16[1024,128]{1,0:T(8,128)(2,1)S(1)} %pad_maximum_fusion.6.refs_0_), channel_id=1, source_target_pairs={{0,8},{1,9},{2,10},{3,11},{4,12},{5,13},{6,14},{7,15},{8,0},{9,1},... | collective-permute-start | bytes 786440 | tf_op jit(solution)/shard_map/ppermute | solution.py:113
  43.7 15.7 %collective-permute-start.22 = (bf16[1024,128]{1,0:T(8,128)(2,1)S(1)}, bf16[1024,128]{1,0:T(8,128)(2,1)S(1)}, u32[]{:S(2)}, u32[]{:S(2)}) collective-permute-start(bf16[1024,128]{1,0:T(8,128)(2,1)S(1)} %pad_maximum_fusion.8), channel_id=1, source_target_pairs={{0,17},{1,16},{2,19},{3,18},{4,21},{5,20},{6,23},{7,22},{8,25},{9,... | collective-permute-start | bytes 786440 | tf_op jit(solution)/shard_map/ppermute | solution.py:113
  48.5 11.6 %collective-permute-start.21 = (bf16[1024,128]{1,0:T(8,128)(2,1)S(1)}, bf16[1024,128]{1,0:T(8,128)(2,1)S(1)}, u32[]{:S(2)}, u32[]{:S(2)}) collective-permute-start(bf16[1024,128]{1,0:T(8,128)(2,1)S(1)} %pad_maximum_fusion.6.refs_0_), channel_id=1, source_target_pairs={{0,16},{1,17},{2,18},{3,19},{4,20},{5,21},{6,22},{7,23},{8,24},{9,... | collective-permute-start | bytes 786440 | tf_op jit(solution)/shard_map/ppermute | solution.py:113
  50.8 11.2 %collective-permute-start.29 = (bf16[1024,128]{1,0:T(8,128)(2,1)S(1)}, bf16[1024,128]{1,0:T(8,128)(2,1)S(1)}, u32[]{:S(2)}, u32[]{:S(2)}) collective-permute-start(bf16[1024,128]{1,0:T(8,128)(2,1)S(1)} %pad_maximum_fusion.10.refs_0_), channel_id=1, source_target_pairs={{0,8},{1,9},{2,10},{3,11},{4,12},{5,13},{6,14},{7,15},{8,0},{9,1},... | collective-permute-start | bytes 786440 | tf_op jit(solution)/shard_map/ppermute | solution.py:113
  56.5 8.7 %collective-permute-start.32 = (bf16[1024,128]{1,0:T(8,128)(2,1)S(1)}, bf16[1024,128]{1,0:T(8,128)(2,1)S(1)}, u32[]{:S(2)}, u32[]{:S(2)}) collective-permute-start(bf16[1024,128]{1,0:T(8,128)(2,1)S(1)} %pad_maximum_fusion.12), channel_id=1, source_target_pairs={{0,17},{1,16},{2,19},{3,18},{4,21},{5,20},{6,23},{7,22},{8,25},{9,... | collective-permute-start | bytes 786440 | tf_op jit(solution)/shard_map/ppermute | solution.py:113
  56.7 10.1 %collective-permute-start.10 = (f16[512,128]{1,0:T(8,128)(2,1)S(1)}, f16[512,128]{1,0:T(8,128)(2,1)S(1)}, u32[]{:S(2)}, u32[]{:S(2)}) collective-permute-start(f16[512,128]{1,0:T(8,128)(2,1)S(1)} %fusion.2), channel_id=1, source_target_pairs={{0,4},{1,5},{2,6},{3,7},{4,0},{5,1},{6,2},{7,3},{8,12},{9,13},{10,... | collective-permute-start | bytes 393224 | tf_op jit(solution)/shard_map/ppermute | solution.py:113
  59.4 11.7 %collective-permute-start.17 = (f16[2,512,128]{2,1,0:T(8,128)(2,1)S(1)}, f16[2,512,128]{2,1,0:T(8,128)(2,1)S(1)}, u32[]{:S(2)}, u32[]{:S(2)}) collective-permute-start(f16[2,512,128]{2,1,0:T(8,128)(2,1)S(1)} %slice_convert_fusion), channel_id=1, source_target_pairs={{0,2},{1,3},{2,0},{3,1},{4,6},{5,7},{6,4},{7,5},{8,10},{9,11},{10,... | collective-permute-start | bytes 786440 | tf_op jit(solution)/shard_map/ppermute | solution.py:113
  60.1 12.1 %collective-permute-start.23 = (bf16[1024,128]{1,0:T(8,128)(2,1)S(1)}, bf16[1024,128]{1,0:T(8,128)(2,1)S(1)}, u32[]{:S(2)}, u32[]{:S(2)}) collective-permute-start(bf16[1024,128]{1,0:T(8,128)(2,1)S(1)} %collective-permute-done.19.refs_2_), channel_id=1, source_target_pairs={{0,16},{1,17},{2,18},{3,19},{4,20},{5,21},{6,22},{7,23},{8,24},{9,... | collective-permute-start | bytes 786440 | tf_op jit(solution)/shard_map/ppermute | solution.py:113
  62.1 11.2 %collective-permute-start.24 = (bf16[1024,128]{1,0:T(8,128)(2,1)S(1)}, bf16[1024,128]{1,0:T(8,128)(2,1)S(1)}, u32[]{:S(2)}, u32[]{:S(2)}) collective-permute-start(bf16[1024,128]{1,0:T(8,128)(2,1)S(1)} %collective-permute-done.22.refs_5_), channel_id=1, source_target_pairs={{0,8},{1,9},{2,10},{3,11},{4,12},{5,13},{6,14},{7,15},{8,0},{9,1},... | collective-permute-start | bytes 786440 | tf_op jit(solution)/shard_map/ppermute | solution.py:113
  65.1 13.3 %collective-permute-start.30 = (bf16[1024,128]{1,0:T(8,128)(2,1)S(1)}, bf16[1024,128]{1,0:T(8,128)(2,1)S(1)}, u32[]{:S(2)}, u32[]{:S(2)}) collective-permute-start(bf16[1024,128]{1,0:T(8,128)(2,1)S(1)} %pad_maximum_fusion.12), channel_id=1, source_target_pairs={{0,9},{1,8},{2,11},{3,10},{4,13},{5,12},{6,15},{7,14},{8,1},{9,0},... | collective-permute-start | bytes 786440 | tf_op jit(solution)/shard_map/ppermute | solution.py:113
  66.8 12.4 %collective-permute-start.31 = (bf16[1024,128]{1,0:T(8,128)(2,1)S(1)}, bf16[1024,128]{1,0:T(8,128)(2,1)S(1)}, u32[]{:S(2)}, u32[]{:S(2)}) collective-permute-start(bf16[1024,128]{1,0:T(8,128)(2,1)S(1)} %pad_maximum_fusion.10.refs_0_), channel_id=1, source_target_pairs={{0,16},{1,17},{2,18},{3,19},{4,20},{5,21},{6,22},{7,23},{8,24},{9,... | collective-permute-start | bytes 786440 | tf_op jit(solution)/shard_map/ppermute | solution.py:113
  71.1 10.8 %collective-permute-start.33 = (bf16[1024,128]{1,0:T(8,128)(2,1)S(1)}, bf16[1024,128]{1,0:T(8,128)(2,1)S(1)}, u32[]{:S(2)}, u32[]{:S(2)}) collective-permute-start(bf16[1024,128]{1,0:T(8,128)(2,1)S(1)} %collective-permute-done.29.refs_2_), channel_id=1, source_target_pairs={{0,16},{1,17},{2,18},{3,19},{4,20},{5,21},{6,22},{7,23},{8,24},{9,... | collective-permute-start | bytes 786440 | tf_op jit(solution)/shard_map/ppermute | solution.py:113
  72.2 10.3 %collective-permute-start.34 = (bf16[1024,128]{1,0:T(8,128)(2,1)S(1)}, bf16[1024,128]{1,0:T(8,128)(2,1)S(1)}, u32[]{:S(2)}, u32[]{:S(2)}) collective-permute-start(bf16[1024,128]{1,0:T(8,128)(2,1)S(1)} %collective-permute-done.32.refs_5_), channel_id=1, source_target_pairs={{0,8},{1,9},{2,10},{3,11},{4,12},{5,13},{6,14},{7,15},{8,0},{9,1},... | collective-permute-start | bytes 786440 | tf_op jit(solution)/shard_map/ppermute | solution.py:113
  73.2 26.8 %collective-permute-start.18 = (f16[512,128]{1,0:T(8,128)(2,1)S(1)}, f16[512,128]{1,0:T(8,128)(2,1)S(1)}, u32[]{:S(2)}, u32[]{:S(2)}) collective-permute-start(f16[512,128]{1,0:T(8,128)(2,1)S(1)} %fusion.3), channel_id=1, source_target_pairs={{0,4},{1,5},{2,6},{3,7},{4,0},{5,1},{6,2},{7,3},{8,12},{9,13},{10,... | collective-permute-start | bytes 393224 | tf_op jit(solution)/shard_map/ppermute | solution.py:113
  78.4 9.6 %collective-permute-start.25 = (f16[2,256,128]{2,1,0:T(8,128)(2,1)S(1)}, f16[2,256,128]{2,1,0:T(8,128)(2,1)S(1)}, u32[]{:S(2)}, u32[]{:S(2)}) collective-permute-start(f16[2,256,128]{2,1,0:T(8,128)(2,1)S(1)} %get-tuple-element.121), channel_id=1, source_target_pairs={{0,2},{1,3},{2,0},{3,1},{4,6},{5,7},{6,4},{7,5},{8,10},{9,11},{10,... | collective-permute-start | bytes 393224 | tf_op jit(solution)/shard_map/ppermute | solution.py:113
  79.2 8.8 %collective-permute-start.27 = (f16[2,256,128]{2,1,0:T(8,128)(2,1)S(1)}, f16[2,256,128]{2,1,0:T(8,128)(2,1)S(1)}, u32[]{:S(2)}, u32[]{:S(2)}) collective-permute-start(f16[2,256,128]{2,1,0:T(8,128)(2,1)S(1)} %get-tuple-element.122), channel_id=1, source_target_pairs={{0,2},{1,3},{2,0},{3,1},{4,6},{5,7},{6,4},{7,5},{8,10},{9,11},{10,... | collective-permute-start | bytes 393224 | tf_op jit(solution)/shard_map/ppermute | solution.py:113
  85.9 8.6 %collective-permute-start.35 = (f16[2,256,128]{2,1,0:T(8,128)(2,1)S(1)}, f16[2,256,128]{2,1,0:T(8,128)(2,1)S(1)}, u32[]{:S(2)}, u32[]{:S(2)}) collective-permute-start(f16[2,256,128]{2,1,0:T(8,128)(2,1)S(1)} %get-tuple-element.119), channel_id=1, source_target_pairs={{0,2},{1,3},{2,0},{3,1},{4,6},{5,7},{6,4},{7,5},{8,10},{9,11},{10,... | collective-permute-start | bytes 393224 | tf_op jit(solution)/shard_map/ppermute | solution.py:113
  86.4 10.4 %collective-permute-start.37 = (f16[2,256,128]{2,1,0:T(8,128)(2,1)S(1)}, f16[2,256,128]{2,1,0:T(8,128)(2,1)S(1)}, u32[]{:S(2)}, u32[]{:S(2)}) collective-permute-start(f16[2,256,128]{2,1,0:T(8,128)(2,1)S(1)} %get-tuple-element.120), channel_id=1, source_target_pairs={{0,2},{1,3},{2,0},{3,1},{4,6},{5,7},{6,4},{7,5},{8,10},{9,11},{10,... | collective-permute-start | bytes 393224 | tf_op jit(solution)/shard_map/ppermute | solution.py:113
  88.1 11.9 %collective-permute-start.28 = (f16[256,128]{1,0:T(8,128)(2,1)S(1)}, f16[256,128]{1,0:T(8,128)(2,1)S(1)}, u32[]{:S(2)}, u32[]{:S(2)}) collective-permute-start(f16[256,128]{1,0:T(8,128)(2,1)S(1)} %fusion.9), channel_id=1, source_target_pairs={{0,4},{1,5},{2,6},{3,7},{4,0},{5,1},{6,2},{7,3},{8,12},{9,13},{10,... | collective-permute-start | bytes 196616 | tf_op jit(solution)/shard_map/ppermute | solution.py:113
  90.8 9.3 %collective-permute-start.26 = (f16[256,128]{1,0:T(8,128)(2,1)S(1)}, f16[256,128]{1,0:T(8,128)(2,1)S(1)}, u32[]{:S(2)}, u32[]{:S(2)}) collective-permute-start(f16[256,128]{1,0:T(8,128)(2,1)S(1)} %fusion.8), channel_id=1, source_target_pairs={{0,4},{1,5},{2,6},{3,7},{4,0},{5,1},{6,2},{7,3},{8,12},{9,13},{10,... | collective-permute-start | bytes 196616 | tf_op jit(solution)/shard_map/ppermute | solution.py:113
  96.9 6.1 %collective-permute-start.38 = (f16[256,128]{1,0:T(8,128)(2,1)S(1)}, f16[256,128]{1,0:T(8,128)(2,1)S(1)}, u32[]{:S(2)}, u32[]{:S(2)}) collective-permute-start(f16[256,128]{1,0:T(8,128)(2,1)S(1)} %fusion.11), channel_id=1, source_target_pairs={{0,4},{1,5},{2,6},{3,7},{4,0},{5,1},{6,2},{7,3},{8,12},{9,13},{10,... | collective-permute-start | bytes 196616 | tf_op jit(solution)/shard_map/ppermute | solution.py:113
  97.9 5.8 %collective-permute-start.36 = (f16[256,128]{1,0:T(8,128)(2,1)S(1)}, f16[256,128]{1,0:T(8,128)(2,1)S(1)}, u32[]{:S(2)}, u32[]{:S(2)}) collective-permute-start(f16[256,128]{1,0:T(8,128)(2,1)S(1)} %fusion.10), channel_id=1, source_target_pairs={{0,4},{1,5},{2,6},{3,7},{4,0},{5,1},{6,2},{7,3},{8,12},{9,13},{10,... | collective-permute-start | bytes 196616 | tf_op jit(solution)/shard_map/ppermute | solution.py:113

commit v4 on v3

--- a/solution.py
+++ b/solution.py
@@ -17,8 +17,8 @@
 STRICT = 1
 ZSPLIT = (1, 1, 2, 2)
 GATES = {('far', 1): [('product', 0)], ('far', 2): [('product', 1)], ('rest', 3): [('pair', 0)], ('product', 2): [('pair', 1)], ('product', 3): [('product', 2)], ('near', 2): ['masked']}
-ROW_TILE = 512
-VMEM_LIMIT = 14 * 1024 * 1024
+ROW_TILE = 1024
+VMEM_LIMIT = 11 * 1024 * 1024
 
 
 def masked_amplitudes(amplitudes, ij_irrep, cd_irrep):

time: 105 us -> 105 us (level)
  no operation moved by 1% of the time
where the time goes in v4:
time: 105 us
  starting transfers between devices  48.2 us (46%)
  waiting for transfers between devices  28.1 us (27%)
  Pallas kernels  14 us (13%)
  other arithmetic  7.3 us (7%)
  local copies, waits for them, and re-layouts  6.9 us (7%)
    ppermute x39, starting transfers between devices, send(): return lax.ppermute(array, ('occ', 'vir'), pairs)  48.2 us
    ppermute x39, waiting for transfers between devices, send(): return lax.ppermute(array, ('occ', 'vir'), pairs)  28.1 us
    pallas_call x4, Pallas kernels, product(): pl.pallas_call(functools.partial(product_kernel, scale), in_specs=[pl.Blo...  12.6 us
    split x3, local copies, waits for them, and re-layouts, piece(): return jnp.concatenate(jnp.split(cut, folds), axis=1)  5.73 us
    concatenate x11, other arithmetic, piece(): return jnp.concatenate(jnp.split(cut, folds), axis=1)  3.64 us
    select_n x1, other arithmetic, masked_amplitudes(): jnp.where(rows[:, None] == columns[None, :], amplitudes, jnp.zeros_like(a...  2.93 us
  transfers between devices with their start and end apart: 39, of which 17 were waited for; matrix products, arithmetic and copies ran while one was open for 13% of the time, Pallas kernels for 12%

profile of v4, /device:TPU:0, one launch (start us, length us, event | category | flops | bytes accessed | tf_op | source)
XLA Modules:
  0.0 105.1 jit_solution(13506341716073507331)
XLA Ops:
  0.5 1.8 %constant_dynamic-slice_fusion.4 = (bf16[1024,64]{1,0:T(8,128)(2,1)S(1)}, bf16[1024,64]{1,0:T(8,128)(2,1)S(1)}, bf16[1024,64]{1,0:T(8,128)(2,1)S(1)}, bf16[1024,64]{1,0:T(8,128)(2,1)S(1)}) fusion(bf16[2048,512]{1,0:T(8,128)(2,1)} %param.5, s32[]{:T(128)S(6)} %select_n.53, s32[]{:T(128)S(6)} %select_n.52, s32[]{:T(128)S(6)} %add.85), kind=kLoop, calls=%fused_computation.52 | loop fusion | bytes 1048588 | tf_op jit(solution)/shard_map/split | solution.py:141
  2.2 1.0 pad_maximum_fusion
  3.2 1.0 constant_dynamic-slice_fusion.7
  4.8 2.5 %collective-permute-start.3 = (bf16[1024,128]{1,0:T(8,128)(2,1)S(1)}, bf16[1024,128]{1,0:T(8,128)(2,1)S(1)}, u32[]{:S(2)}, u32[]{:S(2)}) collective-permute-start(bf16[1024,128]{1,0:T(8,128)(2,1)S(1)} %get-tuple-element.48.refs_0_), channel_id=1, source_target_pairs={{0,8},{1,9},{2,10},{3,11},{4,12},{5,13},{6,14},{7,15},{8,0},{9,1},... | collective-permute-start | bytes 786440 | tf_op jit(solution)/shard_map/ppermute | solution.py:113
  7.3 1.2 %collective-permute-start.6 = (bf16[1024,128]{1,0:T(8,128)(2,1)}, bf16[1024,128]{1,0:T(8,128)(2,1)S(1)}, u32[]{:S(2)}, u32[]{:S(2)}) collective-permute-start(bf16[1024,128]{1,0:T(8,128)(2,1)} %get-tuple-element.50), channel_id=1, source_target_pairs={{0,17},{1,16},{2,19},{3,18},{4,21},{5,20},{6,23},{7,22},{8,25},{9,... | collective-permute-start | bytes 786440 | tf_op jit(solution)/shard_map/ppermute | solution.py:113
  8.4 2.0 %constant_dynamic-slice_fusion.2 = (bf16[1024,64]{1,0:T(8,128)(2,1)}, bf16[1024,64]{1,0:T(8,128)(2,1)}, bf16[1024,64]{1,0:T(8,128)(2,1)}, bf16[1024,64]{1,0:T(8,...) fusion(bf16[2048,512]{1,0:T(8,128)(2,1)S(1)} %copy-done, ...), kind=kLoop, calls=%fused_computation.50 | loop fusion | bytes 3145756 | tf_op jit(solution)/shard_map/split | solution.py:141
  11.1 1.3 %pad_maximum_fusion.10.refs_0_ = bf16[1024,128]{1,0:T(8,128)(2,1)S(1)} fusion(bf16[1024,64]{1,0:T(8,128)(2,1)} %get-tuple-element.102, bf16[1024,64]{1,0:T(8,128)(2,1)} %get-tuple-element.93), kind=kLoop, calls=%fused_computation.26 | loop fusion | flops 524288 | bytes 524288 | tf_op jit(solution)/shard_map/concatenate | solution.py:141
  13.2 0.8 collective-permute-done.3.refs_2_
  14.0 1.8 %collective-permute-start.5 = (bf16[1024,128]{1,0:T(8,128)(2,1)S(1)}, bf16[1024,128]{1,0:T(8,128)(2,1)S(1)}, u32[]{:S(2)}, u32[]{:S(2)}) collective-permute-start(bf16[1024,128]{1,0:T(8,128)(2,1)S(1)} %get-tuple-element.48.refs_0_), channel_id=1, source_target_pairs={{0,16},{1,17},{2,18},{3,19},{4,20},{5,21},{6,22},{7,23},{8,24},{9,... | collective-permute-start | bytes 786440 | tf_op jit(solution)/shard_map/ppermute | solution.py:113
  15.9 2.1 %collective-permute-start.11 = (bf16[1024,128]{1,0:T(8,128)(2,1)S(1)}, bf16[1024,128]{1,0:T(8,128)(2,1)S(1)}, u32[]{:S(2)}, u32[]{:S(2)}) collective-permute-start(bf16[1024,128]{1,0:T(8,128)(2,1)S(1)} %pad_maximum_fusion.3.refs_0_), channel_id=1, source_target_pairs={{0,8},{1,9},{2,10},{3,11},{4,12},{5,13},{6,14},{7,15},{8,0},{9,1},... | collective-permute-start | bytes 786440 | tf_op jit(solution)/shard_map/ppermute | solution.py:113
  17.9 1.9 %fusion.14 = (bf16[1024,64]{1,0:T(8,128)(2,1)S(1)}, bf16[1024,64]{1,0:T(8,128)(2,1)S(1)}, bf16[1024,64]{1,0:T(8,128)(2,1)S(1)}, bf16[1024,64]{1,0:T(8,128)(2,1)S...) fusion(bf16[2048,256]{1,0:T(8,128)(2,1)} %collective-permute-done.2), kind=kLoop, calls=%fused_computation.64 | loop fusion | bytes 2097152 | tf_op jit(solution)/shard_map/split | solution.py:141
  20.0 1.5 %collective-permute-start.8 = (bf16[1024,128]{1,0:T(8,128)(2,1)S(1)}, bf16[1024,128]{1,0:T(8,128)(2,1)S(1)}, u32[]{:S(2)}, u32[]{:S(2)}) collective-permute-start(bf16[1024,128]{1,0:T(8,128)(2,1)S(1)} %collective-permute-done.6.refs_5_), channel_id=1, source_target_pairs={{0,8},{1,9},{2,10},{3,11},{4,12},{5,13},{6,14},{7,15},{8,0},{9,1},... | collective-permute-start | bytes 786440 | tf_op jit(solution)/shard_map/ppermute | solution.py:113
  21.5 2.9 %compare_select_fusion = (bf16[1024,2048]{1,0:T(8,128)(2,1)S(1)}, bf16[1024,2048]{1,0:T(8,128)(2,1)S(1)}) fusion(bf16[1024,2048]{1,0:T(8,128)(2,1)} %collective-permute-done.1, bf16[2048]{0:T(1024)(128)(2,1)S(1)} %convert_element_type.78, bf16[1024]{0:T(1024)(128)(2,1)S(1)} %convert_element_type.76, bf16[1024,2048]{1,0:T(8,128)(2,1)S(1)} %copy-done.1, ...), kind=kLoop, calls=%fused_computation | loop fusion | flops 8388608 | bytes 16787456 | tf_op jit(solution)/shard_map/jit(_where)/select_n | solution.py:26
  24.6 2.3 %collective-permute-start.12 = (bf16[1024,128]{1,0:T(8,128)(2,1)S(1)}, bf16[1024,128]{1,0:T(8,128)(2,1)S(1)}, u32[]{:S(2)}, u32[]{:S(2)}) collective-permute-start(bf16[1024,128]{1,0:T(8,128)(2,1)S(1)} %pad_maximum_fusion.5), channel_id=1, source_target_pairs={{0,9},{1,8},{2,11},{3,10},{4,13},{5,12},{6,15},{7,14},{8,1},{9,0},... | collective-permute-start | bytes 786440 | tf_op jit(solution)/shard_map/ppermute | solution.py:113
  26.8 1.0 collective-permute-done.7.refs_6_
  27.8 2.3 %collective-permute-start.13 = (bf16[1024,128]{1,0:T(8,128)(2,1)S(1)}, bf16[1024,128]{1,0:T(8,128)(2,1)S(1)}, u32[]{:S(2)}, u32[]{:S(2)}) collective-permute-start(bf16[1024,128]{1,0:T(8,128)(2,1)S(1)} %pad_maximum_fusion.3.refs_0_), channel_id=1, source_target_pairs={{0,16},{1,17},{2,18},{3,19},{4,20},{5,21},{6,22},{7,23},{8,24},{9,... | collective-permute-start | bytes 786440 | tf_op jit(solution)/shard_map/ppermute | solution.py:113
  30.1 3.1 %collective-permute-done.8.refs_7_ = bf16[1024,128]{1,0:T(8,128)(2,1)S(1)} collective-permute-done((bf16[1024,128]{1,0:T(8,128)(2,1)S(1)}, bf16[1024,128]{1,0:T(8,128)(2,1)S(1)}, u32[]{:S(2)}, u32[]{:S(2)}) %collective-permute-start.8) | collective-permute-done | bytes 262176 | tf_op jit(solution)/shard_map/ppermute | solution.py:113
  33.2 3.1 %shard_map.46 = f32[4,512,128]{2,1,0:T(8,128)S(1)} custom-call(s32[4]{0:T(128)S(1)} %fusion.13.slot_ref, bf16[1024,2048]{1,0:T(8,128)(2,1)S(1)} %get-tuple-element.124.own_amps, bf16[1024,2048]{1,0:T(8,128)(2,1)S(1)} %get-tuple-element.123.other_amps, bf16[1024,128]{1,0:T(8,128)(2,1)S(1)} %get-tuple-element.48.refs_0_, ...), custom_call_target="tpu_custom_call" | custom-call | tf_op jit(solution)/shard_map/pallas_call | solution.py:64
  36.4 1.6 %collective-permute-start.9 = (f16[2,512,128]{2,1,0:T(8,128)(2,1)S(1)}, f16[2,512,128]{2,1,0:T(8,128)(2,1)S(1)}, u32[]{:S(2)}, u32[]{:S(2)}) collective-permute-start(f16[2,512,128]{2,1,0:T(8,128)(2,1)S(1)} %slice_convert_fusion.1), channel_id=1, source_target_pairs={{0,2},{1,3},{2,0},{3,1},{4,6},{5,7},{6,4},{7,5},{8,10},{9,11},{10,... | collective-permute-start | bytes 786440 | tf_op jit(solution)/shard_map/ppermute | solution.py:113
  39.3 1.5 %collective-permute-start.15 = (bf16[1024,128]{1,0:T(8,128)(2,1)S(1)}, bf16[1024,128]{1,0:T(8,128)(2,1)S(1)}, u32[]{:S(2)}, u32[]{:S(2)}) collective-permute-start(bf16[1024,128]{1,0:T(8,128)(2,1)S(1)} %collective-permute-done.11.refs_2_), channel_id=1, source_target_pairs={{0,16},{1,17},{2,18},{3,19},{4,20},{5,21},{6,22},{7,23},{8,24},{9,... | collective-permute-start | bytes 786440 | tf_op jit(solution)/shard_map/ppermute | solution.py:113
  40.8 1.5 %collective-permute-start.16 = (bf16[1024,128]{1,0:T(8,128)(2,1)S(1)}, bf16[1024,128]{1,0:T(8,128)(2,1)S(1)}, u32[]{:S(2)}, u32[]{:S(2)}) collective-permute-start(bf16[1024,128]{1,0:T(8,128)(2,1)S(1)} %collective-permute-done.14.refs_5_), channel_id=1, source_target_pairs={{0,8},{1,9},{2,10},{3,11},{4,12},{5,13},{6,14},{7,15},{8,0},{9,1},... | collective-permute-start | bytes 786440 | tf_op jit(solution)/shard_map/ppermute | solution.py:113
  43.7 4.8 %collective-permute-done.15.refs_6_ = bf16[1024,128]{1,0:T(8,128)(2,1)S(1)} collective-permute-done((bf16[1024,128]{1,0:T(8,128)(2,1)S(1)}, bf16[1024,128]{1,0:T(8,128)(2,1)S(1)}, u32[]{:S(2)}, u32[]{:S(2)}) %collective-permute-start.15) | collective-permute-done | bytes 262176 | tf_op jit(solution)/shard_map/ppermute | solution.py:113
  48.5 1.1 %collective-permute-start.21 = (bf16[1024,128]{1,0:T(8,128)(2,1)S(1)}, bf16[1024,128]{1,0:T(8,128)(2,1)S(1)}, u32[]{:S(2)}, u32[]{:S(2)}) collective-permute-start(bf16[1024,128]{1,0:T(8,128)(2,1)S(1)} %pad_maximum_fusion.6.refs_0_), channel_id=1, source_target_pairs={{0,16},{1,17},{2,18},{3,19},{4,20},{5,21},{6,22},{7,23},{8,24},{9,... | collective-permute-start | bytes 786440 | tf_op jit(solution)/shard_map/ppermute | solution.py:113
  49.6 1.2 %collective-permute-done.16.refs_7_ = bf16[1024,128]{1,0:T(8,128)(2,1)S(1)} collective-permute-done((bf16[1024,128]{1,0:T(8,128)(2,1)S(1)}, bf16[1024,128]{1,0:T(8,128)(2,1)S(1)}, u32[]{:S(2)}, u32[]{:S(2)}) %collective-permute-start.16) | collective-permute-done | bytes 262176 | tf_op jit(solution)/shard_map/ppermute | solution.py:113
  50.7 2.4 %collective-permute-start.29 = (bf16[1024,128]{1,0:T(8,128)(2,1)S(1)}, bf16[1024,128]{1,0:T(8,128)(2,1)S(1)}, u32[]{:S(2)}, u32[]{:S(2)}) collective-permute-start(bf16[1024,128]{1,0:T(8,128)(2,1)S(1)} %pad_maximum_fusion.10.refs_0_), channel_id=1, source_target_pairs={{0,8},{1,9},{2,10},{3,11},{4,12},{5,13},{6,14},{7,15},{8,0},{9,1},... | collective-permute-start | bytes 786440 | tf_op jit(solution)/shard_map/ppermute | solution.py:113
  53.1 3.2 %shard_map.47 = f32[4,512,128]{2,1,0:T(8,128)S(1)} custom-call(s32[4]{0:T(128)S(1)} %fusion.13.slot_ref, bf16[1024,2048]{1,0:T(8,128)(2,1)S(1)} %get-tuple-element.124.own_amps, bf16[1024,2048]{1,0:T(8,128)(2,1)S(1)} %get-tuple-element.123.other_amps, bf16[1024,128]{1,0:T(8,128)(2,1)S(1)} %pad_maximum_fusion.3.refs_0_, ...), custom_call_target="tpu_custom_call" | custom-call | tf_op jit(solution)/shard_map/pallas_call | solution.py:64
  56.6 2.6 %collective-permute-start.10 = (f16[512,128]{1,0:T(8,128)(2,1)S(1)}, f16[512,128]{1,0:T(8,128)(2,1)S(1)}, u32[]{:S(2)}, u32[]{:S(2)}) collective-permute-start(f16[512,128]{1,0:T(8,128)(2,1)S(1)} %fusion.2), channel_id=1, source_target_pairs={{0,4},{1,5},{2,6},{3,7},{4,0},{5,1},{6,2},{7,3},{8,12},{9,13},{10,... | collective-permute-start | bytes 393224 | tf_op jit(solution)/shard_map/ppermute | solution.py:113
  60.1 1.0 collective-permute-start.23
  61.1 0.8 collective-permute-done.29.refs_2_
  62.0 2.3 %collective-permute-start.24 = (bf16[1024,128]{1,0:T(8,128)(2,1)S(1)}, bf16[1024,128]{1,0:T(8,128)(2,1)S(1)}, u32[]{:S(2)}, u32[]{:S(2)}) collective-permute-start(bf16[1024,128]{1,0:T(8,128)(2,1)S(1)} %collective-permute-done.22.refs_5_), channel_id=1, source_target_pairs={{0,8},{1,9},{2,10},{3,11},{4,12},{5,13},{6,14},{7,15},{8,0},{9,1},... | collective-permute-start | bytes 786440 | tf_op jit(solution)/shard_map/ppermute | solution.py:113
  65.0 1.5 %collective-permute-start.30 = (bf16[1024,128]{1,0:T(8,128)(2,1)S(1)}, bf16[1024,128]{1,0:T(8,128)(2,1)S(1)}, u32[]{:S(2)}, u32[]{:S(2)}) collective-permute-start(bf16[1024,128]{1,0:T(8,128)(2,1)S(1)} %pad_maximum_fusion.12), channel_id=1, source_target_pairs={{0,9},{1,8},{2,11},{3,10},{4,13},{5,12},{6,15},{7,14},{8,1},{9,0},... | collective-permute-start | bytes 786440 | tf_op jit(solution)/shard_map/ppermute | solution.py:113
  66.5 1.2 %collective-permute-start.31 = (bf16[1024,128]{1,0:T(8,128)(2,1)S(1)}, bf16[1024,128]{1,0:T(8,128)(2,1)S(1)}, u32[]{:S(2)}, u32[]{:S(2)}) collective-permute-start(bf16[1024,128]{1,0:T(8,128)(2,1)S(1)} %pad_maximum_fusion.10.refs_0_), channel_id=1, source_target_pairs={{0,16},{1,17},{2,18},{3,19},{4,20},{5,21},{6,22},{7,23},{8,24},{9,... | collective-permute-start | bytes 786440 | tf_op jit(solution)/shard_map/ppermute | solution.py:113
  67.8 2.9 %collective-permute-done.17 = f16[2,512,128]{2,1,0:T(8,128)(2,1)S(1)} collective-permute-done((f16[2,512,128]{2,1,0:T(8,128)(2,1)S(1)}, f16[2,512,128]{2,1,0:T(8,128)(2,1)S(1)}, u32[]{:S(2)}, u32[]{:S(2)}) %collective-permute-start.17) | collective-permute-done | bytes 262176 | tf_op jit(solution)/shard_map/ppermute | solution.py:113
  70.7 1.4 %collective-permute-start.33 = (bf16[1024,128]{1,0:T(8,128)(2,1)S(1)}, bf16[1024,128]{1,0:T(8,128)(2,1)S(1)}, u32[]{:S(2)}, u32[]{:S(2)}) collective-permute-start(bf16[1024,128]{1,0:T(8,128)(2,1)S(1)} %collective-permute-done.29.refs_2_), channel_id=1, source_target_pairs={{0,16},{1,17},{2,18},{3,19},{4,20},{5,21},{6,22},{7,23},{8,24},{9,... | collective-permute-start | bytes 786440 | tf_op jit(solution)/shard_map/ppermute | solution.py:113
  72.1 1.0 collective-permute-start.34
  73.1 1.9 %collective-permute-start.18 = (f16[512,128]{1,0:T(8,128)(2,1)S(1)}, f16[512,128]{1,0:T(8,128)(2,1)S(1)}, u32[]{:S(2)}, u32[]{:S(2)}) collective-permute-start(f16[512,128]{1,0:T(8,128)(2,1)S(1)} %fusion.3), channel_id=1, source_target_pairs={{0,4},{1,5},{2,6},{3,7},{4,0},{5,1},{6,2},{7,3},{8,12},{9,13},{10,... | collective-permute-start | bytes 393224 | tf_op jit(solution)/shard_map/ppermute | solution.py:113
  75.1 3.2 %shard_map.48 = f32[4,512,128]{2,1,0:T(8,128)S(1)} custom-call(s32[4]{0:T(128)S(1)} %fusion.13.slot_ref, bf16[1024,2048]{1,0:T(8,128)(2,1)S(1)} %get-tuple-element.124.own_amps, bf16[1024,2048]{1,0:T(8,128)(2,1)S(1)} %get-tuple-element.123.other_amps, bf16[1024,128]{1,0:T(8,128)(2,1)S(1)} %pad_maximum_fusion.6.refs_0_, ...), custom_call_target="tpu_custom_call" | custom-call | tf_op jit(solution)/shard_map/pallas_call | solution.py:64
  79.2 1.3 %collective-permute-start.27 = (f16[2,256,128]{2,1,0:T(8,128)(2,1)S(1)}, f16[2,256,128]{2,1,0:T(8,128)(2,1)S(1)}, u32[]{:S(2)}, u32[]{:S(2)}) collective-permute-start(f16[2,256,128]{2,1,0:T(8,128)(2,1)S(1)} %get-tuple-element.122), channel_id=1, source_target_pairs={{0,2},{1,3},{2,0},{3,1},{4,6},{5,7},{6,4},{7,5},{8,10},{9,11},{10,... | collective-permute-start | bytes 393224 | tf_op jit(solution)/shard_map/ppermute | solution.py:113
  80.5 1.2 %collective-permute-done.33.refs_6_ = bf16[1024,128]{1,0:T(8,128)(2,1)S(1)} collective-permute-done((bf16[1024,128]{1,0:T(8,128)(2,1)S(1)}, bf16[1024,128]{1,0:T(8,128)(2,1)S(1)}, u32[]{:S(2)}, u32[]{:S(2)}) %collective-permute-start.33) | collective-permute-done | bytes 262176 | tf_op jit(solution)/shard_map/ppermute | solution.py:113
  82.4 3.1 %shard_map.49 = f32[4,512,128]{2,1,0:T(8,128)S(1)} custom-call(s32[4]{0:T(128)S(1)} %fusion.13.slot_ref, bf16[1024,2048]{1,0:T(8,128)(2,1)S(1)} %get-tuple-element.124.own_amps, bf16[1024,2048]{1,0:T(8,128)(2,1)S(1)} %get-tuple-element.123.other_amps, bf16[1024,128]{1,0:T(8,128)(2,1)S(1)} %pad_maximum_fusion.10.refs_0_, ...), custom_call_target="tpu_custom_call" | custom-call | tf_op jit(solution)/shard_map/pallas_call | solution.py:64
  86.2 1.6 %collective-permute-start.37 = (f16[2,256,128]{2,1,0:T(8,128)(2,1)S(1)}, f16[2,256,128]{2,1,0:T(8,128)(2,1)S(1)}, u32[]{:S(2)}, u32[]{:S(2)}) collective-permute-start(f16[2,256,128]{2,1,0:T(8,128)(2,1)S(1)} %get-tuple-element.120), channel_id=1, source_target_pairs={{0,2},{1,3},{2,0},{3,1},{4,6},{5,7},{6,4},{7,5},{8,10},{9,11},{10,... | collective-permute-start | bytes 393224 | tf_op jit(solution)/shard_map/ppermute | solution.py:113
  87.9 2.6 %collective-permute-start.28 = (f16[256,128]{1,0:T(8,128)(2,1)S(1)}, f16[256,128]{1,0:T(8,128)(2,1)S(1)}, u32[]{:S(2)}, u32[]{:S(2)}) collective-permute-start(f16[256,128]{1,0:T(8,128)(2,1)S(1)} %fusion.9), channel_id=1, source_target_pairs={{0,4},{1,5},{2,6},{3,7},{4,0},{5,1},{6,2},{7,3},{8,12},{9,13},{10,... | collective-permute-start | bytes 196616 | tf_op jit(solution)/shard_map/ppermute | solution.py:113
  91.0 3.3 %collective-permute-done.35 = f16[2,256,128]{2,1,0:T(8,128)(2,1)S(1)} collective-permute-done((f16[2,256,128]{2,1,0:T(8,128)(2,1)S(1)}, f16[2,256,128]{2,1,0:T(8,128)(2,1)S(1)}, u32[]{:S(2)}, u32[]{:S(2)}) %collective-permute-start.35) | collective-permute-done | bytes 131104 | tf_op jit(solution)/shard_map/ppermute | solution.py:113
  94.3 2.4 %collective-permute-done.37 = f16[2,256,128]{2,1,0:T(8,128)(2,1)S(1)} collective-permute-done((f16[2,256,128]{2,1,0:T(8,128)(2,1)S(1)}, f16[2,256,128]{2,1,0:T(8,128)(2,1)S(1)}, u32[]{:S(2)}, u32[]{:S(2)}) %collective-permute-start.37) | collective-permute-done | bytes 131104 | tf_op jit(solution)/shard_map/ppermute | solution.py:113
  96.7 1.0 collective-permute-start.38
  97.7 2.1 %collective-permute-start.36 = (f16[256,128]{1,0:T(8,128)(2,1)S(1)}, f16[256,128]{1,0:T(8,128)(2,1)S(1)}, u32[]{:S(2)}, u32[]{:S(2)}) collective-permute-start(f16[256,128]{1,0:T(8,128)(2,1)S(1)} %fusion.10), channel_id=1, source_target_pairs={{0,4},{1,5},{2,6},{3,7},{4,0},{5,1},{6,2},{7,3},{8,12},{9,13},{10,... | collective-permute-start | bytes 196616 | tf_op jit(solution)/shard_map/ppermute | solution.py:113
  99.9 3.0 %collective-permute-done.38 = f16[256,128]{1,0:T(8,128)(2,1)S(1)} collective-permute-done((f16[256,128]{1,0:T(8,128)(2,1)S(1)}, f16[256,128]{1,0:T(8,128)(2,1)S(1)}, u32[]{:S(2)}, u32[]{:S(2)}) %collective-permute-start.38) | collective-permute-done | bytes 65568 | tf_op jit(solution)/shard_map/ppermute | solution.py:113
  103.6 1.4 %shard_map.50 = f32[1024,256]{1,0:T(8,128)} custom-call(f32[512,128]{1,0:T(8,128)S(1)} %fusion.1.refs_0_, f32[512,128]{1,0:T(8,128)S(1)} %fusion.refs_1_, f32[512,128]{1,0:T(8,128)S(1)} %pad_maximum_fusion.9.refs_2_, f32[512,128]{1,0:T(8,128)S(1)} %pad_maximum_fusion.13.refs_3_), custom_call_target="tpu_custom_call" | custom-call | tf_op jit(solution)/shard_map/pallas_call | solution.py:93
  (91 shorter events, 10.9 us)
Async XLA Ops:
  0.0 3.2 %copy-start = (bf16[2048,512]{1,0:T(8,128)(2,1)S(1)}, bf16[2048,512]{1,0:T(8,128)(2,1)}, u32[]{:S(2)}) copy-start(bf16[2048,512]{1,0:T(8,128)(2,1)} %param.5) | copy-start | bytes 6291460
  0.0 4.3 %copy-start.4 = (s32[2048]{0:T(1024)S(1)}, s32[2048]{0:T(1024)}, u32[]{:S(2)}) copy-start(s32[2048]{0:T(1024)} %param.7) | copy-start | bytes 24580
  0.0 20.0 %collective-permute-start.1 = (bf16[1024,2048]{1,0:T(8,128)(2,1)}, bf16[1024,2048]{1,0:T(8,128)(2,1)}, u32[]{:S(2)}, u32[]{:S(2)}) collective-permute-start(bf16[1024,2048]{1,0:T(8,128)(2,1)} %param.4), channel_id=1, source_target_pairs={{0,1},{1,0},{2,3},{3,2},{4,5},{5,4},{6,7},{7,6},{8,9},{9,8},{10,11... | collective-permute-start | bytes 12582920 | tf_op jit(solution)/shard_map/ppermute | solution.py:113
  4.3 13.7 %collective-permute-start.2 = (bf16[2048,256]{1,0:T(8,128)(2,1)}, bf16[2048,256]{1,0:T(8,128)(2,1)}, u32[]{:S(2)}, u32[]{:S(2)}) collective-permute-start(bf16[2048,256]{1,0:T(8,128)(2,1)} %constant_dynamic-slice_fusion.7), channel_id=1, source_target_pairs={{0,1},{1,0},{2,3},{3,2},{4,5},{5,4},{6,7},{7,6},{8,9},{9,8},{10,11... | collective-permute-start | bytes 3145736 | tf_op jit(solution)/shard_map/ppermute | solution.py:113
  4.3 8.2 %collective-permute-start = (s32[2048]{0:T(1024)S(1)}, s32[2048]{0:T(1024)S(1)}, u32[]{:S(2)}, u32[]{:S(2)}) collective-permute-start(s32[2048]{0:T(1024)S(1)} %copy-done.4), channel_id=1, source_target_pairs={{0,1},{1,0},{2,3},{3,2},{4,5},{5,4},{6,7},{7,6},{8,9},{9,8},{10,11... | collective-permute-start | bytes 24584 | tf_op jit(solution)/shard_map/ppermute | solution.py:113
  4.8 9.3 %collective-permute-start.3 = (bf16[1024,128]{1,0:T(8,128)(2,1)S(1)}, bf16[1024,128]{1,0:T(8,128)(2,1)S(1)}, u32[]{:S(2)}, u32[]{:S(2)}) collective-permute-start(bf16[1024,128]{1,0:T(8,128)(2,1)S(1)} %get-tuple-element.48.refs_0_), channel_id=1, source_target_pairs={{0,8},{1,9},{2,10},{3,11},{4,12},{5,13},{6,14},{7,15},{8,0},{9,1},... | collective-permute-start | bytes 786440 | tf_op jit(solution)/shard_map/ppermute | solution.py:113
  7.3 8.6 %collective-permute-start.6 = (bf16[1024,128]{1,0:T(8,128)(2,1)}, bf16[1024,128]{1,0:T(8,128)(2,1)S(1)}, u32[]{:S(2)}, u32[]{:S(2)}) collective-permute-start(bf16[1024,128]{1,0:T(8,128)(2,1)} %get-tuple-element.50), channel_id=1, source_target_pairs={{0,17},{1,16},{2,19},{3,18},{4,21},{5,20},{6,23},{7,22},{8,25},{9,... | collective-permute-start | bytes 786440 | tf_op jit(solution)/shard_map/ppermute | solution.py:113
  8.4 4.1 %copy-start.5 = (s32[1024]{0:T(1024)S(1)}, s32[1024]{0:T(1024)}, u32[]{:S(2)}) copy-start(s32[1024]{0:T(1024)} %param.6) | copy-start | bytes 12292
  11.1 10.4 %copy-start.1 = (bf16[1024,2048]{1,0:T(8,128)(2,1)S(1)}, bf16[1024,2048]{1,0:T(8,128)(2,1)}, u32[]{:S(2)}) copy-start(bf16[1024,2048]{1,0:T(8,128)(2,1)} %param.4) | copy-start | bytes 12582916
  12.5 12.0 %collective-permute-start.4 = (bf16[1024,128]{1,0:T(8,128)(2,1)}, bf16[1024,128]{1,0:T(8,128)(2,1)S(1)}, u32[]{:S(2)}, u32[]{:S(2)}) collective-permute-start(bf16[1024,128]{1,0:T(8,128)(2,1)} %get-tuple-element.50), channel_id=1, source_target_pairs={{0,9},{1,8},{2,11},{3,10},{4,13},{5,12},{6,15},{7,14},{8,1},{9,0},... | collective-permute-start | bytes 786440 | tf_op jit(solution)/shard_map/ppermute | solution.py:113
  14.0 10.5 %collective-permute-start.5 = (bf16[1024,128]{1,0:T(8,128)(2,1)S(1)}, bf16[1024,128]{1,0:T(8,128)(2,1)S(1)}, u32[]{:S(2)}, u32[]{:S(2)}) collective-permute-start(bf16[1024,128]{1,0:T(8,128)(2,1)S(1)} %get-tuple-element.48.refs_0_), channel_id=1, source_target_pairs={{0,16},{1,17},{2,18},{3,19},{4,20},{5,21},{6,22},{7,23},{8,24},{9,... | collective-permute-start | bytes 786440 | tf_op jit(solution)/shard_map/ppermute | solution.py:113
  15.9 22.4 %collective-permute-start.11 = (bf16[1024,128]{1,0:T(8,128)(2,1)S(1)}, bf16[1024,128]{1,0:T(8,128)(2,1)S(1)}, u32[]{:S(2)}, u32[]{:S(2)}) collective-permute-start(bf16[1024,128]{1,0:T(8,128)(2,1)S(1)} %pad_maximum_fusion.3.refs_0_), channel_id=1, source_target_pairs={{0,8},{1,9},{2,10},{3,11},{4,12},{5,13},{6,14},{7,15},{8,0},{9,1},... | collective-permute-start | bytes 786440 | tf_op jit(solution)/shard_map/ppermute | solution.py:113
  17.9 9.9 %collective-permute-start.7 = (bf16[1024,128]{1,0:T(8,128)(2,1)S(1)}, bf16[1024,128]{1,0:T(8,128)(2,1)S(1)}, u32[]{:S(2)}, u32[]{:S(2)}) collective-permute-start(bf16[1024,128]{1,0:T(8,128)(2,1)S(1)} %collective-permute-done.3.refs_2_), channel_id=1, source_target_pairs={{0,16},{1,17},{2,18},{3,19},{4,20},{5,21},{6,22},{7,23},{8,24},{9,... | collective-permute-start | bytes 786440 | tf_op jit(solution)/shard_map/ppermute | solution.py:113
  20.0 13.2 %collective-permute-start.8 = (bf16[1024,128]{1,0:T(8,128)(2,1)S(1)}, bf16[1024,128]{1,0:T(8,128)(2,1)S(1)}, u32[]{:S(2)}, u32[]{:S(2)}) collective-permute-start(bf16[1024,128]{1,0:T(8,128)(2,1)S(1)} %collective-permute-done.6.refs_5_), channel_id=1, source_target_pairs={{0,8},{1,9},{2,10},{3,11},{4,12},{5,13},{6,14},{7,15},{8,0},{9,1},... | collective-permute-start | bytes 786440 | tf_op jit(solution)/shard_map/ppermute | solution.py:113
  24.5 13.8 %collective-permute-start.14 = (bf16[1024,128]{1,0:T(8,128)(2,1)S(1)}, bf16[1024,128]{1,0:T(8,128)(2,1)S(1)}, u32[]{:S(2)}, u32[]{:S(2)}) collective-permute-start(bf16[1024,128]{1,0:T(8,128)(2,1)S(1)} %pad_maximum_fusion.5), channel_id=1, source_target_pairs={{0,17},{1,16},{2,19},{3,18},{4,21},{5,20},{6,23},{7,22},{8,25},{9,... | collective-permute-start | bytes 786440 | tf_op jit(solution)/shard_map/ppermute | solution.py:113
  24.6 13.8 %collective-permute-start.12 = (bf16[1024,128]{1,0:T(8,128)(2,1)S(1)}, bf16[1024,128]{1,0:T(8,128)(2,1)S(1)}, u32[]{:S(2)}, u32[]{:S(2)}) collective-permute-start(bf16[1024,128]{1,0:T(8,128)(2,1)S(1)} %pad_maximum_fusion.5), channel_id=1, source_target_pairs={{0,9},{1,8},{2,11},{3,10},{4,13},{5,12},{6,15},{7,14},{8,1},{9,0},... | collective-permute-start | bytes 786440 | tf_op jit(solution)/shard_map/ppermute | solution.py:113
  27.8 11.1 %collective-permute-start.13 = (bf16[1024,128]{1,0:T(8,128)(2,1)S(1)}, bf16[1024,128]{1,0:T(8,128)(2,1)S(1)}, u32[]{:S(2)}, u32[]{:S(2)}) collective-permute-start(bf16[1024,128]{1,0:T(8,128)(2,1)S(1)} %pad_maximum_fusion.3.refs_0_), channel_id=1, source_target_pairs={{0,16},{1,17},{2,18},{3,19},{4,20},{5,21},{6,22},{7,23},{8,24},{9,... | collective-permute-start | bytes 786440 | tf_op jit(solution)/shard_map/ppermute | solution.py:113
  33.2 4.8 %copy-start.2 = (bf16[1024,64]{1,0:T(8,128)(2,1)S(1)}, bf16[1024,64]{1,0:T(8,128)(2,1)}, u32[]{:S(2)}) copy-start(bf16[1024,64]{1,0:T(8,128)(2,1)} %get-tuple-element.91) | copy-start | bytes 393220
  33.2 4.8 %copy-start.3 = (bf16[1024,64]{1,0:T(8,128)(2,1)S(1)}, bf16[1024,64]{1,0:T(8,128)(2,1)}, u32[]{:S(2)}) copy-start(bf16[1024,64]{1,0:T(8,128)(2,1)} %get-tuple-element.92) | copy-start | bytes 393220
  36.4 7.2 %collective-permute-start.9 = (f16[2,512,128]{2,1,0:T(8,128)(2,1)S(1)}, f16[2,512,128]{2,1,0:T(8,128)(2,1)S(1)}, u32[]{:S(2)}, u32[]{:S(2)}) collective-permute-start(f16[2,512,128]{2,1,0:T(8,128)(2,1)S(1)} %slice_convert_fusion.1), channel_id=1, source_target_pairs={{0,2},{1,3},{2,0},{3,1},{4,6},{5,7},{6,4},{7,5},{8,10},{9,11},{10,... | collective-permute-start | bytes 786440 | tf_op jit(solution)/shard_map/ppermute | solution.py:113
  38.3 18.0 %collective-permute-start.20 = (bf16[1024,128]{1,0:T(8,128)(2,1)S(1)}, bf16[1024,128]{1,0:T(8,128)(2,1)S(1)}, u32[]{:S(2)}, u32[]{:S(2)}) collective-permute-start(bf16[1024,128]{1,0:T(8,128)(2,1)S(1)} %pad_maximum_fusion.8), channel_id=1, source_target_pairs={{0,9},{1,8},{2,11},{3,10},{4,13},{5,12},{6,15},{7,14},{8,1},{9,0},... | collective-permute-start | bytes 786440 | tf_op jit(solution)/shard_map/ppermute | solution.py:113
  39.3 9.2 %collective-permute-start.15 = (bf16[1024,128]{1,0:T(8,128)(2,1)S(1)}, bf16[1024,128]{1,0:T(8,128)(2,1)S(1)}, u32[]{:S(2)}, u32[]{:S(2)}) collective-permute-start(bf16[1024,128]{1,0:T(8,128)(2,1)S(1)} %collective-permute-done.11.refs_2_), channel_id=1, source_target_pairs={{0,16},{1,17},{2,18},{3,19},{4,20},{5,21},{6,22},{7,23},{8,24},{9,... | collective-permute-start | bytes 786440 | tf_op jit(solution)/shard_map/ppermute | solution.py:113
  40.8 10.0 %collective-permute-start.16 = (bf16[1024,128]{1,0:T(8,128)(2,1)S(1)}, bf16[1024,128]{1,0:T(8,128)(2,1)S(1)}, u32[]{:S(2)}, u32[]{:S(2)}) collective-permute-start(bf16[1024,128]{1,0:T(8,128)(2,1)S(1)} %collective-permute-done.14.refs_5_), channel_id=1, source_target_pairs={{0,8},{1,9},{2,10},{3,11},{4,12},{5,13},{6,14},{7,15},{8,0},{9,1},... | collective-permute-start | bytes 786440 | tf_op jit(solution)/shard_map/ppermute | solution.py:113
  42.3 14.3 %collective-permute-start.19 = (bf16[1024,128]{1,0:T(8,128)(2,1)S(1)}, bf16[1024,128]{1,0:T(8,128)(2,1)S(1)}, u32[]{:S(2)}, u32[]{:S(2)}) collective-permute-start(bf16[1024,128]{1,0:T(8,128)(2,1)S(1)} %pad_maximum_fusion.6.refs_0_), channel_id=1, source_target_pairs={{0,8},{1,9},{2,10},{3,11},{4,12},{5,13},{6,14},{7,15},{8,0},{9,1},... | collective-permute-start | bytes 786440 | tf_op jit(solution)/shard_map/ppermute | solution.py:113
  43.6 15.6 %collective-permute-start.22 = (bf16[1024,128]{1,0:T(8,128)(2,1)S(1)}, bf16[1024,128]{1,0:T(8,128)(2,1)S(1)}, u32[]{:S(2)}, u32[]{:S(2)}) collective-permute-start(bf16[1024,128]{1,0:T(8,128)(2,1)S(1)} %pad_maximum_fusion.8), channel_id=1, source_target_pairs={{0,17},{1,16},{2,19},{3,18},{4,21},{5,20},{6,23},{7,22},{8,25},{9,... | collective-permute-start | bytes 786440 | tf_op jit(solution)/shard_map/ppermute | solution.py:113
  48.5 11.6 %collective-permute-start.21 = (bf16[1024,128]{1,0:T(8,128)(2,1)S(1)}, bf16[1024,128]{1,0:T(8,128)(2,1)S(1)}, u32[]{:S(2)}, u32[]{:S(2)}) collective-permute-start(bf16[1024,128]{1,0:T(8,128)(2,1)S(1)} %pad_maximum_fusion.6.refs_0_), channel_id=1, source_target_pairs={{0,16},{1,17},{2,18},{3,19},{4,20},{5,21},{6,22},{7,23},{8,24},{9,... | collective-permute-start | bytes 786440 | tf_op jit(solution)/shard_map/ppermute | solution.py:113
  50.7 11.2 %collective-permute-start.29 = (bf16[1024,128]{1,0:T(8,128)(2,1)S(1)}, bf16[1024,128]{1,0:T(8,128)(2,1)S(1)}, u32[]{:S(2)}, u32[]{:S(2)}) collective-permute-start(bf16[1024,128]{1,0:T(8,128)(2,1)S(1)} %pad_maximum_fusion.10.refs_0_), channel_id=1, source_target_pairs={{0,8},{1,9},{2,10},{3,11},{4,12},{5,13},{6,14},{7,15},{8,0},{9,1},... | collective-permute-start | bytes 786440 | tf_op jit(solution)/shard_map/ppermute | solution.py:113
  56.3 8.7 %collective-permute-start.32 = (bf16[1024,128]{1,0:T(8,128)(2,1)S(1)}, bf16[1024,128]{1,0:T(8,128)(2,1)S(1)}, u32[]{:S(2)}, u32[]{:S(2)}) collective-permute-start(bf16[1024,128]{1,0:T(8,128)(2,1)S(1)} %pad_maximum_fusion.12), channel_id=1, source_target_pairs={{0,17},{1,16},{2,19},{3,18},{4,21},{5,20},{6,23},{7,22},{8,25},{9,... | collective-permute-start | bytes 786440 | tf_op jit(solution)/shard_map/ppermute | solution.py:113
  56.6 10.0 %collective-permute-start.10 = (f16[512,128]{1,0:T(8,128)(2,1)S(1)}, f16[512,128]{1,0:T(8,128)(2,1)S(1)}, u32[]{:S(2)}, u32[]{:S(2)}) collective-permute-start(f16[512,128]{1,0:T(8,128)(2,1)S(1)} %fusion.2), channel_id=1, source_target_pairs={{0,4},{1,5},{2,6},{3,7},{4,0},{5,1},{6,2},{7,3},{8,12},{9,13},{10,... | collective-permute-start | bytes 393224 | tf_op jit(solution)/shard_map/ppermute | solution.py:113
  59.2 11.5 %collective-permute-start.17 = (f16[2,512,128]{2,1,0:T(8,128)(2,1)S(1)}, f16[2,512,128]{2,1,0:T(8,128)(2,1)S(1)}, u32[]{:S(2)}, u32[]{:S(2)}) collective-permute-start(f16[2,512,128]{2,1,0:T(8,128)(2,1)S(1)} %slice_convert_fusion), channel_id=1, source_target_pairs={{0,2},{1,3},{2,0},{3,1},{4,6},{5,7},{6,4},{7,5},{8,10},{9,11},{10,... | collective-permute-start | bytes 786440 | tf_op jit(solution)/shard_map/ppermute | solution.py:113
  60.1 12.0 %collective-permute-start.23 = (bf16[1024,128]{1,0:T(8,128)(2,1)S(1)}, bf16[1024,128]{1,0:T(8,128)(2,1)S(1)}, u32[]{:S(2)}, u32[]{:S(2)}) collective-permute-start(bf16[1024,128]{1,0:T(8,128)(2,1)S(1)} %collective-permute-done.19.refs_2_), channel_id=1, source_target_pairs={{0,16},{1,17},{2,18},{3,19},{4,20},{5,21},{6,22},{7,23},{8,24},{9,... | collective-permute-start | bytes 786440 | tf_op jit(solution)/shard_map/ppermute | solution.py:113
  62.0 11.2 %collective-permute-start.24 = (bf16[1024,128]{1,0:T(8,128)(2,1)S(1)}, bf16[1024,128]{1,0:T(8,128)(2,1)S(1)}, u32[]{:S(2)}, u32[]{:S(2)}) collective-permute-start(bf16[1024,128]{1,0:T(8,128)(2,1)S(1)} %collective-permute-done.22.refs_5_), channel_id=1, source_target_pairs={{0,8},{1,9},{2,10},{3,11},{4,12},{5,13},{6,14},{7,15},{8,0},{9,1},... | collective-permute-start | bytes 786440 | tf_op jit(solution)/shard_map/ppermute | solution.py:113
  65.0 13.4 %collective-permute-start.30 = (bf16[1024,128]{1,0:T(8,128)(2,1)S(1)}, bf16[1024,128]{1,0:T(8,128)(2,1)S(1)}, u32[]{:S(2)}, u32[]{:S(2)}) collective-permute-start(bf16[1024,128]{1,0:T(8,128)(2,1)S(1)} %pad_maximum_fusion.12), channel_id=1, source_target_pairs={{0,9},{1,8},{2,11},{3,10},{4,13},{5,12},{6,15},{7,14},{8,1},{9,0},... | collective-permute-start | bytes 786440 | tf_op jit(solution)/shard_map/ppermute | solution.py:113
  66.5 12.6 %collective-permute-start.31 = (bf16[1024,128]{1,0:T(8,128)(2,1)S(1)}, bf16[1024,128]{1,0:T(8,128)(2,1)S(1)}, u32[]{:S(2)}, u32[]{:S(2)}) collective-permute-start(bf16[1024,128]{1,0:T(8,128)(2,1)S(1)} %pad_maximum_fusion.10.refs_0_), channel_id=1, source_target_pairs={{0,16},{1,17},{2,18},{3,19},{4,20},{5,21},{6,22},{7,23},{8,24},{9,... | collective-permute-start | bytes 786440 | tf_op jit(solution)/shard_map/ppermute | solution.py:113
  70.7 11.0 %collective-permute-start.33 = (bf16[1024,128]{1,0:T(8,128)(2,1)S(1)}, bf16[1024,128]{1,0:T(8,128)(2,1)S(1)}, u32[]{:S(2)}, u32[]{:S(2)}) collective-permute-start(bf16[1024,128]{1,0:T(8,128)(2,1)S(1)} %collective-permute-done.29.refs_2_), channel_id=1, source_target_pairs={{0,16},{1,17},{2,18},{3,19},{4,20},{5,21},{6,22},{7,23},{8,24},{9,... | collective-permute-start | bytes 786440 | tf_op jit(solution)/shard_map/ppermute | solution.py:113
  72.1 10.3 %collective-permute-start.34 = (bf16[1024,128]{1,0:T(8,128)(2,1)S(1)}, bf16[1024,128]{1,0:T(8,128)(2,1)S(1)}, u32[]{:S(2)}, u32[]{:S(2)}) collective-permute-start(bf16[1024,128]{1,0:T(8,128)(2,1)S(1)} %collective-permute-done.32.refs_5_), channel_id=1, source_target_pairs={{0,8},{1,9},{2,10},{3,11},{4,12},{5,13},{6,14},{7,15},{8,0},{9,1},... | collective-permute-start | bytes 786440 | tf_op jit(solution)/shard_map/ppermute | solution.py:113
  73.1 26.7 %collective-permute-start.18 = (f16[512,128]{1,0:T(8,128)(2,1)S(1)}, f16[512,128]{1,0:T(8,128)(2,1)S(1)}, u32[]{:S(2)}, u32[]{:S(2)}) collective-permute-start(f16[512,128]{1,0:T(8,128)(2,1)S(1)} %fusion.3), channel_id=1, source_target_pairs={{0,4},{1,5},{2,6},{3,7},{4,0},{5,1},{6,2},{7,3},{8,12},{9,13},{10,... | collective-permute-start | bytes 393224 | tf_op jit(solution)/shard_map/ppermute | solution.py:113
  78.4 9.4 %collective-permute-start.25 = (f16[2,256,128]{2,1,0:T(8,128)(2,1)S(1)}, f16[2,256,128]{2,1,0:T(8,128)(2,1)S(1)}, u32[]{:S(2)}, u32[]{:S(2)}) collective-permute-start(f16[2,256,128]{2,1,0:T(8,128)(2,1)S(1)} %get-tuple-element.121), channel_id=1, source_target_pairs={{0,2},{1,3},{2,0},{3,1},{4,6},{5,7},{6,4},{7,5},{8,10},{9,11},{10,... | collective-permute-start | bytes 393224 | tf_op jit(solution)/shard_map/ppermute | solution.py:113
  79.2 8.7 %collective-permute-start.27 = (f16[2,256,128]{2,1,0:T(8,128)(2,1)S(1)}, f16[2,256,128]{2,1,0:T(8,128)(2,1)S(1)}, u32[]{:S(2)}, u32[]{:S(2)}) collective-permute-start(f16[2,256,128]{2,1,0:T(8,128)(2,1)S(1)} %get-tuple-element.122), channel_id=1, source_target_pairs={{0,2},{1,3},{2,0},{3,1},{4,6},{5,7},{6,4},{7,5},{8,10},{9,11},{10,... | collective-permute-start | bytes 393224 | tf_op jit(solution)/shard_map/ppermute | solution.py:113
  85.7 8.6 %collective-permute-start.35 = (f16[2,256,128]{2,1,0:T(8,128)(2,1)S(1)}, f16[2,256,128]{2,1,0:T(8,128)(2,1)S(1)}, u32[]{:S(2)}, u32[]{:S(2)}) collective-permute-start(f16[2,256,128]{2,1,0:T(8,128)(2,1)S(1)} %get-tuple-element.119), channel_id=1, source_target_pairs={{0,2},{1,3},{2,0},{3,1},{4,6},{5,7},{6,4},{7,5},{8,10},{9,11},{10,... | collective-permute-start | bytes 393224 | tf_op jit(solution)/shard_map/ppermute | solution.py:113
  86.2 10.4 %collective-permute-start.37 = (f16[2,256,128]{2,1,0:T(8,128)(2,1)S(1)}, f16[2,256,128]{2,1,0:T(8,128)(2,1)S(1)}, u32[]{:S(2)}, u32[]{:S(2)}) collective-permute-start(f16[2,256,128]{2,1,0:T(8,128)(2,1)S(1)} %get-tuple-element.120), channel_id=1, source_target_pairs={{0,2},{1,3},{2,0},{3,1},{4,6},{5,7},{6,4},{7,5},{8,10},{9,11},{10,... | collective-permute-start | bytes 393224 | tf_op jit(solution)/shard_map/ppermute | solution.py:113
  87.9 11.9 %collective-permute-start.28 = (f16[256,128]{1,0:T(8,128)(2,1)S(1)}, f16[256,128]{1,0:T(8,128)(2,1)S(1)}, u32[]{:S(2)}, u32[]{:S(2)}) collective-permute-start(f16[256,128]{1,0:T(8,128)(2,1)S(1)} %fusion.9), channel_id=1, source_target_pairs={{0,4},{1,5},{2,6},{3,7},{4,0},{5,1},{6,2},{7,3},{8,12},{9,13},{10,... | collective-permute-start | bytes 196616 | tf_op jit(solution)/shard_map/ppermute | solution.py:113
  90.6 9.3 %collective-permute-start.26 = (f16[256,128]{1,0:T(8,128)(2,1)S(1)}, f16[256,128]{1,0:T(8,128)(2,1)S(1)}, u32[]{:S(2)}, u32[]{:S(2)}) collective-permute-start(f16[256,128]{1,0:T(8,128)(2,1)S(1)} %fusion.8), channel_id=1, source_target_pairs={{0,4},{1,5},{2,6},{3,7},{4,0},{5,1},{6,2},{7,3},{8,12},{9,13},{10,... | collective-permute-start | bytes 196616 | tf_op jit(solution)/shard_map/ppermute | solution.py:113
  96.7 6.2 %collective-permute-start.38 = (f16[256,128]{1,0:T(8,128)(2,1)S(1)}, f16[256,128]{1,0:T(8,128)(2,1)S(1)}, u32[]{:S(2)}, u32[]{:S(2)}) collective-permute-start(f16[256,128]{1,0:T(8,128)(2,1)S(1)} %fusion.11), channel_id=1, source_target_pairs={{0,4},{1,5},{2,6},{3,7},{4,0},{5,1},{6,2},{7,3},{8,12},{9,13},{10,... | collective-permute-start | bytes 196616 | tf_op jit(solution)/shard_map/ppermute | solution.py:113
  97.7 5.8 %collective-permute-start.36 = (f16[256,128]{1,0:T(8,128)(2,1)S(1)}, f16[256,128]{1,0:T(8,128)(2,1)S(1)}, u32[]{:S(2)}, u32[]{:S(2)}) collective-permute-start(f16[256,128]{1,0:T(8,128)(2,1)S(1)} %fusion.10), channel_id=1, source_target_pairs={{0,4},{1,5},{2,6},{3,7},{4,0},{5,1},{6,2},{7,3},{8,12},{9,13},{10,... | collective-permute-start | bytes 196616 | tf_op jit(solution)/shard_map/ppermute | solution.py:113

commit v5 on v4

--- a/solution.py
+++ b/solution.py
@@ -176,7 +176,8 @@
             if back >= 0:
                 earlier = [values[name] for name in order[max(back - STRICT, 0) : back + 1]]
                 loads, _ = lax.optimization_barrier((loads, earlier))
-            on_x[kind, g], on_y[kind, g] = ways[0](loads[0]), ways[1](loads[1])
+            on_y[kind, g] = ways[1](loads[1])
+            on_x[kind, g] = ways[0](loads[0])
             values[kind, g] = (on_x[kind, g], on_y[kind, g])
             if not all((k, g) in on_x for k in ("near", "rest", "far")):
                 continue

time: 105 us -> 105 us (level)
  no operation moved by 1% of the time
where the time goes in v5:
time: 105 us
  starting transfers between devices  48.2 us (46%)
  waiting for transfers between devices  28.1 us (27%)
  Pallas kernels  14 us (13%)
  other arithmetic  7.3 us (7%)
  local copies, waits for them, and re-layouts  6.9 us (7%)
    ppermute x39, starting transfers between devices, send(): return lax.ppermute(array, ('occ', 'vir'), pairs)  48.2 us
    ppermute x39, waiting for transfers between devices, send(): return lax.ppermute(array, ('occ', 'vir'), pairs)  28.1 us
    pallas_call x4, Pallas kernels, product(): pl.pallas_call(functools.partial(product_kernel, scale), in_specs=[pl.Blo...  12.6 us
    split x3, local copies, waits for them, and re-layouts, piece(): return jnp.concatenate(jnp.split(cut, folds), axis=1)  5.73 us
    concatenate x11, other arithmetic, piece(): return jnp.concatenate(jnp.split(cut, folds), axis=1)  3.64 us
    select_n x1, other arithmetic, masked_amplitudes(): jnp.where(rows[:, None] == columns[None, :], amplitudes, jnp.zeros_like(a...  2.93 us
  transfers between devices with their start and end apart: 39, of which 17 were waited for; matrix products, arithmetic and copies ran while one was open for 13% of the time, Pallas kernels for 12%

profile of v5, /device:TPU:0, one launch (start us, length us, event | category | flops | bytes accessed | tf_op | source)
XLA Modules:
  0.0 105.1 jit_solution(13506341716073507331)
XLA Ops:
  0.5 1.8 %constant_dynamic-slice_fusion.4 = (bf16[1024,64]{1,0:T(8,128)(2,1)S(1)}, bf16[1024,64]{1,0:T(8,128)(2,1)S(1)}, bf16[1024,64]{1,0:T(8,128)(2,1)S(1)}, bf16[1024,64]{1,0:T(8,128)(2,1)S(1)}) fusion(bf16[2048,512]{1,0:T(8,128)(2,1)} %param.5, s32[]{:T(128)S(6)} %select_n.53, s32[]{:T(128)S(6)} %select_n.52, s32[]{:T(128)S(6)} %add.85), kind=kLoop, calls=%fused_computation.52 | loop fusion | bytes 1048588 | tf_op jit(solution)/shard_map/split | solution.py:141
  2.2 1.0 pad_maximum_fusion
  3.2 1.0 constant_dynamic-slice_fusion.7
  4.8 2.5 %collective-permute-start.3 = (bf16[1024,128]{1,0:T(8,128)(2,1)S(1)}, bf16[1024,128]{1,0:T(8,128)(2,1)S(1)}, u32[]{:S(2)}, u32[]{:S(2)}) collective-permute-start(bf16[1024,128]{1,0:T(8,128)(2,1)S(1)} %get-tuple-element.48.refs_0_), channel_id=1, source_target_pairs={{0,8},{1,9},{2,10},{3,11},{4,12},{5,13},{6,14},{7,15},{8,0},{9,1},... | collective-permute-start | bytes 786440 | tf_op jit(solution)/shard_map/ppermute | solution.py:113
  7.3 1.2 %collective-permute-start.6 = (bf16[1024,128]{1,0:T(8,128)(2,1)}, bf16[1024,128]{1,0:T(8,128)(2,1)S(1)}, u32[]{:S(2)}, u32[]{:S(2)}) collective-permute-start(bf16[1024,128]{1,0:T(8,128)(2,1)} %get-tuple-element.50), channel_id=1, source_target_pairs={{0,17},{1,16},{2,19},{3,18},{4,21},{5,20},{6,23},{7,22},{8,25},{9,... | collective-permute-start | bytes 786440 | tf_op jit(solution)/shard_map/ppermute | solution.py:113
  8.4 2.0 %constant_dynamic-slice_fusion.2 = (bf16[1024,64]{1,0:T(8,128)(2,1)}, bf16[1024,64]{1,0:T(8,128)(2,1)}, bf16[1024,64]{1,0:T(8,128)(2,1)}, bf16[1024,64]{1,0:T(8,...) fusion(bf16[2048,512]{1,0:T(8,128)(2,1)S(1)} %copy-done, ...), kind=kLoop, calls=%fused_computation.50 | loop fusion | bytes 3145756 | tf_op jit(solution)/shard_map/split | solution.py:141
  11.1 1.3 %pad_maximum_fusion.10.refs_0_ = bf16[1024,128]{1,0:T(8,128)(2,1)S(1)} fusion(bf16[1024,64]{1,0:T(8,128)(2,1)} %get-tuple-element.102, bf16[1024,64]{1,0:T(8,128)(2,1)} %get-tuple-element.93), kind=kLoop, calls=%fused_computation.26 | loop fusion | flops 524288 | bytes 524288 | tf_op jit(solution)/shard_map/concatenate | solution.py:141
  13.2 0.8 collective-permute-done.3.refs_2_
  14.0 1.8 %collective-permute-start.5 = (bf16[1024,128]{1,0:T(8,128)(2,1)S(1)}, bf16[1024,128]{1,0:T(8,128)(2,1)S(1)}, u32[]{:S(2)}, u32[]{:S(2)}) collective-permute-start(bf16[1024,128]{1,0:T(8,128)(2,1)S(1)} %get-tuple-element.48.refs_0_), channel_id=1, source_target_pairs={{0,16},{1,17},{2,18},{3,19},{4,20},{5,21},{6,22},{7,23},{8,24},{9,... | collective-permute-start | bytes 786440 | tf_op jit(solution)/shard_map/ppermute | solution.py:113
  15.9 2.1 %collective-permute-start.11 = (bf16[1024,128]{1,0:T(8,128)(2,1)S(1)}, bf16[1024,128]{1,0:T(8,128)(2,1)S(1)}, u32[]{:S(2)}, u32[]{:S(2)}) collective-permute-start(bf16[1024,128]{1,0:T(8,128)(2,1)S(1)} %pad_maximum_fusion.3.refs_0_), channel_id=1, source_target_pairs={{0,8},{1,9},{2,10},{3,11},{4,12},{5,13},{6,14},{7,15},{8,0},{9,1},... | collective-permute-start | bytes 786440 | tf_op jit(solution)/shard_map/ppermute | solution.py:113
  17.9 1.9 %fusion.14 = (bf16[1024,64]{1,0:T(8,128)(2,1)S(1)}, bf16[1024,64]{1,0:T(8,128)(2,1)S(1)}, bf16[1024,64]{1,0:T(8,128)(2,1)S(1)}, bf16[1024,64]{1,0:T(8,128)(2,1)S...) fusion(bf16[2048,256]{1,0:T(8,128)(2,1)} %collective-permute-done.2), kind=kLoop, calls=%fused_computation.64 | loop fusion | bytes 2097152 | tf_op jit(solution)/shard_map/split | solution.py:141
  20.0 1.5 %collective-permute-start.8 = (bf16[1024,128]{1,0:T(8,128)(2,1)S(1)}, bf16[1024,128]{1,0:T(8,128)(2,1)S(1)}, u32[]{:S(2)}, u32[]{:S(2)}) collective-permute-start(bf16[1024,128]{1,0:T(8,128)(2,1)S(1)} %collective-permute-done.6.refs_5_), channel_id=1, source_target_pairs={{0,8},{1,9},{2,10},{3,11},{4,12},{5,13},{6,14},{7,15},{8,0},{9,1},... | collective-permute-start | bytes 786440 | tf_op jit(solution)/shard_map/ppermute | solution.py:113
  21.5 2.9 %compare_select_fusion = (bf16[1024,2048]{1,0:T(8,128)(2,1)S(1)}, bf16[1024,2048]{1,0:T(8,128)(2,1)S(1)}) fusion(bf16[1024,2048]{1,0:T(8,128)(2,1)} %collective-permute-done.1, bf16[2048]{0:T(1024)(128)(2,1)S(1)} %convert_element_type.78, bf16[1024]{0:T(1024)(128)(2,1)S(1)} %convert_element_type.76, bf16[1024,2048]{1,0:T(8,128)(2,1)S(1)} %copy-done.1, ...), kind=kLoop, calls=%fused_computation | loop fusion | flops 8388608 | bytes 16787456 | tf_op jit(solution)/shard_map/jit(_where)/select_n | solution.py:26
  24.6 2.3 %collective-permute-start.12 = (bf16[1024,128]{1,0:T(8,128)(2,1)S(1)}, bf16[1024,128]{1,0:T(8,128)(2,1)S(1)}, u32[]{:S(2)}, u32[]{:S(2)}) collective-permute-start(bf16[1024,128]{1,0:T(8,128)(2,1)S(1)} %pad_maximum_fusion.5), channel_id=1, source_target_pairs={{0,9},{1,8},{2,11},{3,10},{4,13},{5,12},{6,15},{7,14},{8,1},{9,0},... | collective-permute-start | bytes 786440 | tf_op jit(solution)/shard_map/ppermute | solution.py:113
  26.8 1.0 collective-permute-done.7.refs_6_
  27.8 2.3 %collective-permute-start.13 = (bf16[1024,128]{1,0:T(8,128)(2,1)S(1)}, bf16[1024,128]{1,0:T(8,128)(2,1)S(1)}, u32[]{:S(2)}, u32[]{:S(2)}) collective-permute-start(bf16[1024,128]{1,0:T(8,128)(2,1)S(1)} %pad_maximum_fusion.3.refs_0_), channel_id=1, source_target_pairs={{0,16},{1,17},{2,18},{3,19},{4,20},{5,21},{6,22},{7,23},{8,24},{9,... | collective-permute-start | bytes 786440 | tf_op jit(solution)/shard_map/ppermute | solution.py:113
  30.1 3.1 %collective-permute-done.8.refs_7_ = bf16[1024,128]{1,0:T(8,128)(2,1)S(1)} collective-permute-done((bf16[1024,128]{1,0:T(8,128)(2,1)S(1)}, bf16[1024,128]{1,0:T(8,128)(2,1)S(1)}, u32[]{:S(2)}, u32[]{:S(2)}) %collective-permute-start.8) | collective-permute-done | bytes 262176 | tf_op jit(solution)/shard_map/ppermute | solution.py:113
  33.2 3.1 %shard_map.46 = f32[4,512,128]{2,1,0:T(8,128)S(1)} custom-call(s32[4]{0:T(128)S(1)} %fusion.13.slot_ref, bf16[1024,2048]{1,0:T(8,128)(2,1)S(1)} %get-tuple-element.124.own_amps, bf16[1024,2048]{1,0:T(8,128)(2,1)S(1)} %get-tuple-element.123.other_amps, bf16[1024,128]{1,0:T(8,128)(2,1)S(1)} %get-tuple-element.48.refs_0_, ...), custom_call_target="tpu_custom_call" | custom-call | tf_op jit(solution)/shard_map/pallas_call | solution.py:64
  36.4 1.6 %collective-permute-start.9 = (f16[2,512,128]{2,1,0:T(8,128)(2,1)S(1)}, f16[2,512,128]{2,1,0:T(8,128)(2,1)S(1)}, u32[]{:S(2)}, u32[]{:S(2)}) collective-permute-start(f16[2,512,128]{2,1,0:T(8,128)(2,1)S(1)} %slice_convert_fusion.1), channel_id=1, source_target_pairs={{0,2},{1,3},{2,0},{3,1},{4,6},{5,7},{6,4},{7,5},{8,10},{9,11},{10,... | collective-permute-start | bytes 786440 | tf_op jit(solution)/shard_map/ppermute | solution.py:113
  39.3 1.5 %collective-permute-start.15 = (bf16[1024,128]{1,0:T(8,128)(2,1)S(1)}, bf16[1024,128]{1,0:T(8,128)(2,1)S(1)}, u32[]{:S(2)}, u32[]{:S(2)}) collective-permute-start(bf16[1024,128]{1,0:T(8,128)(2,1)S(1)} %collective-permute-done.11.refs_2_), channel_id=1, source_target_pairs={{0,16},{1,17},{2,18},{3,19},{4,20},{5,21},{6,22},{7,23},{8,24},{9,... | collective-permute-start | bytes 786440 | tf_op jit(solution)/shard_map/ppermute | solution.py:113
  40.8 1.5 %collective-permute-start.16 = (bf16[1024,128]{1,0:T(8,128)(2,1)S(1)}, bf16[1024,128]{1,0:T(8,128)(2,1)S(1)}, u32[]{:S(2)}, u32[]{:S(2)}) collective-permute-start(bf16[1024,128]{1,0:T(8,128)(2,1)S(1)} %collective-permute-done.14.refs_5_), channel_id=1, source_target_pairs={{0,8},{1,9},{2,10},{3,11},{4,12},{5,13},{6,14},{7,15},{8,0},{9,1},... | collective-permute-start | bytes 786440 | tf_op jit(solution)/shard_map/ppermute | solution.py:113
  43.7 4.8 %collective-permute-done.15.refs_6_ = bf16[1024,128]{1,0:T(8,128)(2,1)S(1)} collective-permute-done((bf16[1024,128]{1,0:T(8,128)(2,1)S(1)}, bf16[1024,128]{1,0:T(8,128)(2,1)S(1)}, u32[]{:S(2)}, u32[]{:S(2)}) %collective-permute-start.15) | collective-permute-done | bytes 262176 | tf_op jit(solution)/shard_map/ppermute | solution.py:113
  48.5 1.1 %collective-permute-start.21 = (bf16[1024,128]{1,0:T(8,128)(2,1)S(1)}, bf16[1024,128]{1,0:T(8,128)(2,1)S(1)}, u32[]{:S(2)}, u32[]{:S(2)}) collective-permute-start(bf16[1024,128]{1,0:T(8,128)(2,1)S(1)} %pad_maximum_fusion.6.refs_0_), channel_id=1, source_target_pairs={{0,16},{1,17},{2,18},{3,19},{4,20},{5,21},{6,22},{7,23},{8,24},{9,... | collective-permute-start | bytes 786440 | tf_op jit(solution)/shard_map/ppermute | solution.py:113
  49.6 1.2 %collective-permute-done.16.refs_7_ = bf16[1024,128]{1,0:T(8,128)(2,1)S(1)} collective-permute-done((bf16[1024,128]{1,0:T(8,128)(2,1)S(1)}, bf16[1024,128]{1,0:T(8,128)(2,1)S(1)}, u32[]{:S(2)}, u32[]{:S(2)}) %collective-permute-start.16) | collective-permute-done | bytes 262176 | tf_op jit(solution)/shard_map/ppermute | solution.py:113
  50.7 2.4 %collective-permute-start.29 = (bf16[1024,128]{1,0:T(8,128)(2,1)S(1)}, bf16[1024,128]{1,0:T(8,128)(2,1)S(1)}, u32[]{:S(2)}, u32[]{:S(2)}) collective-permute-start(bf16[1024,128]{1,0:T(8,128)(2,1)S(1)} %pad_maximum_fusion.10.refs_0_), channel_id=1, source_target_pairs={{0,8},{1,9},{2,10},{3,11},{4,12},{5,13},{6,14},{7,15},{8,0},{9,1},... | collective-permute-start | bytes 786440 | tf_op jit(solution)/shard_map/ppermute | solution.py:113
  53.1 3.2 %shard_map.47 = f32[4,512,128]{2,1,0:T(8,128)S(1)} custom-call(s32[4]{0:T(128)S(1)} %fusion.13.slot_ref, bf16[1024,2048]{1,0:T(8,128)(2,1)S(1)} %get-tuple-element.124.own_amps, bf16[1024,2048]{1,0:T(8,128)(2,1)S(1)} %get-tuple-element.123.other_amps, bf16[1024,128]{1,0:T(8,128)(2,1)S(1)} %pad_maximum_fusion.3.refs_0_, ...), custom_call_target="tpu_custom_call" | custom-call | tf_op jit(solution)/shard_map/pallas_call | solution.py:64
  56.6 2.6 %collective-permute-start.10 = (f16[512,128]{1,0:T(8,128)(2,1)S(1)}, f16[512,128]{1,0:T(8,128)(2,1)S(1)}, u32[]{:S(2)}, u32[]{:S(2)}) collective-permute-start(f16[512,128]{1,0:T(8,128)(2,1)S(1)} %fusion.2), channel_id=1, source_target_pairs={{0,4},{1,5},{2,6},{3,7},{4,0},{5,1},{6,2},{7,3},{8,12},{9,13},{10,... | collective-permute-start | bytes 393224 | tf_op jit(solution)/shard_map/ppermute | solution.py:113
  60.1 1.0 collective-permute-start.23
  61.1 0.8 collective-permute-done.29.refs_2_
  62.0 2.3 %collective-permute-start.24 = (bf16[1024,128]{1,0:T(8,128)(2,1)S(1)}, bf16[1024,128]{1,0:T(8,128)(2,1)S(1)}, u32[]{:S(2)}, u32[]{:S(2)}) collective-permute-start(bf16[1024,128]{1,0:T(8,128)(2,1)S(1)} %collective-permute-done.22.refs_5_), channel_id=1, source_target_pairs={{0,8},{1,9},{2,10},{3,11},{4,12},{5,13},{6,14},{7,15},{8,0},{9,1},... | collective-permute-start | bytes 786440 | tf_op jit(solution)/shard_map/ppermute | solution.py:113
  65.0 1.5 %collective-permute-start.30 = (bf16[1024,128]{1,0:T(8,128)(2,1)S(1)}, bf16[1024,128]{1,0:T(8,128)(2,1)S(1)}, u32[]{:S(2)}, u32[]{:S(2)}) collective-permute-start(bf16[1024,128]{1,0:T(8,128)(2,1)S(1)} %pad_maximum_fusion.12), channel_id=1, source_target_pairs={{0,9},{1,8},{2,11},{3,10},{4,13},{5,12},{6,15},{7,14},{8,1},{9,0},... | collective-permute-start | bytes 786440 | tf_op jit(solution)/shard_map/ppermute | solution.py:113
  66.5 1.2 %collective-permute-start.31 = (bf16[1024,128]{1,0:T(8,128)(2,1)S(1)}, bf16[1024,128]{1,0:T(8,128)(2,1)S(1)}, u32[]{:S(2)}, u32[]{:S(2)}) collective-permute-start(bf16[1024,128]{1,0:T(8,128)(2,1)S(1)} %pad_maximum_fusion.10.refs_0_), channel_id=1, source_target_pairs={{0,16},{1,17},{2,18},{3,19},{4,20},{5,21},{6,22},{7,23},{8,24},{9,... | collective-permute-start | bytes 786440 | tf_op jit(solution)/shard_map/ppermute | solution.py:113
  67.8 2.9 %collective-permute-done.17 = f16[2,512,128]{2,1,0:T(8,128)(2,1)S(1)} collective-permute-done((f16[2,512,128]{2,1,0:T(8,128)(2,1)S(1)}, f16[2,512,128]{2,1,0:T(8,128)(2,1)S(1)}, u32[]{:S(2)}, u32[]{:S(2)}) %collective-permute-start.17) | collective-permute-done | bytes 262176 | tf_op jit(solution)/shard_map/ppermute | solution.py:113
  70.7 1.4 %collective-permute-start.33 = (bf16[1024,128]{1,0:T(8,128)(2,1)S(1)}, bf16[1024,128]{1,0:T(8,128)(2,1)S(1)}, u32[]{:S(2)}, u32[]{:S(2)}) collective-permute-start(bf16[1024,128]{1,0:T(8,128)(2,1)S(1)} %collective-permute-done.29.refs_2_), channel_id=1, source_target_pairs={{0,16},{1,17},{2,18},{3,19},{4,20},{5,21},{6,22},{7,23},{8,24},{9,... | collective-permute-start | bytes 786440 | tf_op jit(solution)/shard_map/ppermute | solution.py:113
  72.1 1.0 collective-permute-start.34
  73.1 1.9 %collective-permute-start.18 = (f16[512,128]{1,0:T(8,128)(2,1)S(1)}, f16[512,128]{1,0:T(8,128)(2,1)S(1)}, u32[]{:S(2)}, u32[]{:S(2)}) collective-permute-start(f16[512,128]{1,0:T(8,128)(2,1)S(1)} %fusion.3), channel_id=1, source_target_pairs={{0,4},{1,5},{2,6},{3,7},{4,0},{5,1},{6,2},{7,3},{8,12},{9,13},{10,... | collective-permute-start | bytes 393224 | tf_op jit(solution)/shard_map/ppermute | solution.py:113
  75.1 3.2 %shard_map.48 = f32[4,512,128]{2,1,0:T(8,128)S(1)} custom-call(s32[4]{0:T(128)S(1)} %fusion.13.slot_ref, bf16[1024,2048]{1,0:T(8,128)(2,1)S(1)} %get-tuple-element.124.own_amps, bf16[1024,2048]{1,0:T(8,128)(2,1)S(1)} %get-tuple-element.123.other_amps, bf16[1024,128]{1,0:T(8,128)(2,1)S(1)} %pad_maximum_fusion.6.refs_0_, ...), custom_call_target="tpu_custom_call" | custom-call | tf_op jit(solution)/shard_map/pallas_call | solution.py:64
  79.2 1.3 %collective-permute-start.27 = (f16[2,256,128]{2,1,0:T(8,128)(2,1)S(1)}, f16[2,256,128]{2,1,0:T(8,128)(2,1)S(1)}, u32[]{:S(2)}, u32[]{:S(2)}) collective-permute-start(f16[2,256,128]{2,1,0:T(8,128)(2,1)S(1)} %get-tuple-element.122), channel_id=1, source_target_pairs={{0,2},{1,3},{2,0},{3,1},{4,6},{5,7},{6,4},{7,5},{8,10},{9,11},{10,... | collective-permute-start | bytes 393224 | tf_op jit(solution)/shard_map/ppermute | solution.py:113
  80.5 1.2 %collective-permute-done.33.refs_6_ = bf16[1024,128]{1,0:T(8,128)(2,1)S(1)} collective-permute-done((bf16[1024,128]{1,0:T(8,128)(2,1)S(1)}, bf16[1024,128]{1,0:T(8,128)(2,1)S(1)}, u32[]{:S(2)}, u32[]{:S(2)}) %collective-permute-start.33) | collective-permute-done | bytes 262176 | tf_op jit(solution)/shard_map/ppermute | solution.py:113
  82.4 3.1 %shard_map.49 = f32[4,512,128]{2,1,0:T(8,128)S(1)} custom-call(s32[4]{0:T(128)S(1)} %fusion.13.slot_ref, bf16[1024,2048]{1,0:T(8,128)(2,1)S(1)} %get-tuple-element.124.own_amps, bf16[1024,2048]{1,0:T(8,128)(2,1)S(1)} %get-tuple-element.123.other_amps, bf16[1024,128]{1,0:T(8,128)(2,1)S(1)} %pad_maximum_fusion.10.refs_0_, ...), custom_call_target="tpu_custom_call" | custom-call | tf_op jit(solution)/shard_map/pallas_call | solution.py:64
  86.2 1.6 %collective-permute-start.37 = (f16[2,256,128]{2,1,0:T(8,128)(2,1)S(1)}, f16[2,256,128]{2,1,0:T(8,128)(2,1)S(1)}, u32[]{:S(2)}, u32[]{:S(2)}) collective-permute-start(f16[2,256,128]{2,1,0:T(8,128)(2,1)S(1)} %get-tuple-element.120), channel_id=1, source_target_pairs={{0,2},{1,3},{2,0},{3,1},{4,6},{5,7},{6,4},{7,5},{8,10},{9,11},{10,... | collective-permute-start | bytes 393224 | tf_op jit(solution)/shard_map/ppermute | solution.py:113
  87.9 2.6 %collective-permute-start.28 = (f16[256,128]{1,0:T(8,128)(2,1)S(1)}, f16[256,128]{1,0:T(8,128)(2,1)S(1)}, u32[]{:S(2)}, u32[]{:S(2)}) collective-permute-start(f16[256,128]{1,0:T(8,128)(2,1)S(1)} %fusion.9), channel_id=1, source_target_pairs={{0,4},{1,5},{2,6},{3,7},{4,0},{5,1},{6,2},{7,3},{8,12},{9,13},{10,... | collective-permute-start | bytes 196616 | tf_op jit(solution)/shard_map/ppermute | solution.py:113
  91.0 3.3 %collective-permute-done.35 = f16[2,256,128]{2,1,0:T(8,128)(2,1)S(1)} collective-permute-done((f16[2,256,128]{2,1,0:T(8,128)(2,1)S(1)}, f16[2,256,128]{2,1,0:T(8,128)(2,1)S(1)}, u32[]{:S(2)}, u32[]{:S(2)}) %collective-permute-start.35) | collective-permute-done | bytes 131104 | tf_op jit(solution)/shard_map/ppermute | solution.py:113
  94.3 2.4 %collective-permute-done.37 = f16[2,256,128]{2,1,0:T(8,128)(2,1)S(1)} collective-permute-done((f16[2,256,128]{2,1,0:T(8,128)(2,1)S(1)}, f16[2,256,128]{2,1,0:T(8,128)(2,1)S(1)}, u32[]{:S(2)}, u32[]{:S(2)}) %collective-permute-start.37) | collective-permute-done | bytes 131104 | tf_op jit(solution)/shard_map/ppermute | solution.py:113
  96.7 1.0 collective-permute-start.38
  97.7 2.1 %collective-permute-start.36 = (f16[256,128]{1,0:T(8,128)(2,1)S(1)}, f16[256,128]{1,0:T(8,128)(2,1)S(1)}, u32[]{:S(2)}, u32[]{:S(2)}) collective-permute-start(f16[256,128]{1,0:T(8,128)(2,1)S(1)} %fusion.10), channel_id=1, source_target_pairs={{0,4},{1,5},{2,6},{3,7},{4,0},{5,1},{6,2},{7,3},{8,12},{9,13},{10,... | collective-permute-start | bytes 196616 | tf_op jit(solution)/shard_map/ppermute | solution.py:113
  99.9 3.0 %collective-permute-done.38 = f16[256,128]{1,0:T(8,128)(2,1)S(1)} collective-permute-done((f16[256,128]{1,0:T(8,128)(2,1)S(1)}, f16[256,128]{1,0:T(8,128)(2,1)S(1)}, u32[]{:S(2)}, u32[]{:S(2)}) %collective-permute-start.38) | collective-permute-done | bytes 65568 | tf_op jit(solution)/shard_map/ppermute | solution.py:113
  103.6 1.4 %shard_map.50 = f32[1024,256]{1,0:T(8,128)} custom-call(f32[512,128]{1,0:T(8,128)S(1)} %fusion.1.refs_0_, f32[512,128]{1,0:T(8,128)S(1)} %fusion.refs_1_, f32[512,128]{1,0:T(8,128)S(1)} %pad_maximum_fusion.9.refs_2_, f32[512,128]{1,0:T(8,128)S(1)} %pad_maximum_fusion.13.refs_3_), custom_call_target="tpu_custom_call" | custom-call | tf_op jit(solution)/shard_map/pallas_call | solution.py:93
  (91 shorter events, 10.9 us)
Async XLA Ops:
  0.0 3.2 %copy-start = (bf16[2048,512]{1,0:T(8,128)(2,1)S(1)}, bf16[2048,512]{1,0:T(8,128)(2,1)}, u32[]{:S(2)}) copy-start(bf16[2048,512]{1,0:T(8,128)(2,1)} %param.5) | copy-start | bytes 6291460
  0.0 4.3 %copy-start.4 = (s32[2048]{0:T(1024)S(1)}, s32[2048]{0:T(1024)}, u32[]{:S(2)}) copy-start(s32[2048]{0:T(1024)} %param.7) | copy-start | bytes 24580
  0.0 20.0 %collective-permute-start.1 = (bf16[1024,2048]{1,0:T(8,128)(2,1)}, bf16[1024,2048]{1,0:T(8,128)(2,1)}, u32[]{:S(2)}, u32[]{:S(2)}) collective-permute-start(bf16[1024,2048]{1,0:T(8,128)(2,1)} %param.4), channel_id=1, source_target_pairs={{0,1},{1,0},{2,3},{3,2},{4,5},{5,4},{6,7},{7,6},{8,9},{9,8},{10,11... | collective-permute-start | bytes 12582920 | tf_op jit(solution)/shard_map/ppermute | solution.py:113
  4.3 13.7 %collective-permute-start.2 = (bf16[2048,256]{1,0:T(8,128)(2,1)}, bf16[2048,256]{1,0:T(8,128)(2,1)}, u32[]{:S(2)}, u32[]{:S(2)}) collective-permute-start(bf16[2048,256]{1,0:T(8,128)(2,1)} %constant_dynamic-slice_fusion.7), channel_id=1, source_target_pairs={{0,1},{1,0},{2,3},{3,2},{4,5},{5,4},{6,7},{7,6},{8,9},{9,8},{10,11... | collective-permute-start | bytes 3145736 | tf_op jit(solution)/shard_map/ppermute | solution.py:113
  4.3 8.2 %collective-permute-start = (s32[2048]{0:T(1024)S(1)}, s32[2048]{0:T(1024)S(1)}, u32[]{:S(2)}, u32[]{:S(2)}) collective-permute-start(s32[2048]{0:T(1024)S(1)} %copy-done.4), channel_id=1, source_target_pairs={{0,1},{1,0},{2,3},{3,2},{4,5},{5,4},{6,7},{7,6},{8,9},{9,8},{10,11... | collective-permute-start | bytes 24584 | tf_op jit(solution)/shard_map/ppermute | solution.py:113
  4.8 9.3 %collective-permute-start.3 = (bf16[1024,128]{1,0:T(8,128)(2,1)S(1)}, bf16[1024,128]{1,0:T(8,128)(2,1)S(1)}, u32[]{:S(2)}, u32[]{:S(2)}) collective-permute-start(bf16[1024,128]{1,0:T(8,128)(2,1)S(1)} %get-tuple-element.48.refs_0_), channel_id=1, source_target_pairs={{0,8},{1,9},{2,10},{3,11},{4,12},{5,13},{6,14},{7,15},{8,0},{9,1},... | collective-permute-start | bytes 786440 | tf_op jit(solution)/shard_map/ppermute | solution.py:113
  7.3 8.6 %collective-permute-start.6 = (bf16[1024,128]{1,0:T(8,128)(2,1)}, bf16[1024,128]{1,0:T(8,128)(2,1)S(1)}, u32[]{:S(2)}, u32[]{:S(2)}) collective-permute-start(bf16[1024,128]{1,0:T(8,128)(2,1)} %get-tuple-element.50), channel_id=1, source_target_pairs={{0,17},{1,16},{2,19},{3,18},{4,21},{5,20},{6,23},{7,22},{8,25},{9,... | collective-permute-start | bytes 786440 | tf_op jit(solution)/shard_map/ppermute | solution.py:113
  8.4 4.1 %copy-start.5 = (s32[1024]{0:T(1024)S(1)}, s32[1024]{0:T(1024)}, u32[]{:S(2)}) copy-start(s32[1024]{0:T(1024)} %param.6) | copy-start | bytes 12292
  11.1 10.4 %copy-start.1 = (bf16[1024,2048]{1,0:T(8,128)(2,1)S(1)}, bf16[1024,2048]{1,0:T(8,128)(2,1)}, u32[]{:S(2)}) copy-start(bf16[1024,2048]{1,0:T(8,128)(2,1)} %param.4) | copy-start | bytes 12582916
  12.5 12.0 %collective-permute-start.4 = (bf16[1024,128]{1,0:T(8,128)(2,1)}, bf16[1024,128]{1,0:T(8,128)(2,1)S(1)}, u32[]{:S(2)}, u32[]{:S(2)}) collective-permute-start(bf16[1024,128]{1,0:T(8,128)(2,1)} %get-tuple-element.50), channel_id=1, source_target_pairs={{0,9},{1,8},{2,11},{3,10},{4,13},{5,12},{6,15},{7,14},{8,1},{9,0},... | collective-permute-start | bytes 786440 | tf_op jit(solution)/shard_map/ppermute | solution.py:113
  14.0 10.5 %collective-permute-start.5 = (bf16[1024,128]{1,0:T(8,128)(2,1)S(1)}, bf16[1024,128]{1,0:T(8,128)(2,1)S(1)}, u32[]{:S(2)}, u32[]{:S(2)}) collective-permute-start(bf16[1024,128]{1,0:T(8,128)(2,1)S(1)} %get-tuple-element.48.refs_0_), channel_id=1, source_target_pairs={{0,16},{1,17},{2,18},{3,19},{4,20},{5,21},{6,22},{7,23},{8,24},{9,... | collective-permute-start | bytes 786440 | tf_op jit(solution)/shard_map/ppermute | solution.py:113
  15.9 22.4 %collective-permute-start.11 = (bf16[1024,128]{1,0:T(8,128)(2,1)S(1)}, bf16[1024,128]{1,0:T(8,128)(2,1)S(1)}, u32[]{:S(2)}, u32[]{:S(2)}) collective-permute-start(bf16[1024,128]{1,0:T(8,128)(2,1)S(1)} %pad_maximum_fusion.3.refs_0_), channel_id=1, source_target_pairs={{0,8},{1,9},{2,10},{3,11},{4,12},{5,13},{6,14},{7,15},{8,0},{9,1},... | collective-permute-start | bytes 786440 | tf_op jit(solution)/shard_map/ppermute | solution.py:113
  17.9 9.9 %collective-permute-start.7 = (bf16[1024,128]{1,0:T(8,128)(2,1)S(1)}, bf16[1024,128]{1,0:T(8,128)(2,1)S(1)}, u32[]{:S(2)}, u32[]{:S(2)}) collective-permute-start(bf16[1024,128]{1,0:T(8,128)(2,1)S(1)} %collective-permute-done.3.refs_2_), channel_id=1, source_target_pairs={{0,16},{1,17},{2,18},{3,19},{4,20},{5,21},{6,22},{7,23},{8,24},{9,... | collective-permute-start | bytes 786440 | tf_op jit(solution)/shard_map/ppermute | solution.py:113
  20.0 13.2 %collective-permute-start.8 = (bf16[1024,128]{1,0:T(8,128)(2,1)S(1)}, bf16[1024,128]{1,0:T(8,128)(2,1)S(1)}, u32[]{:S(2)}, u32[]{:S(2)}) collective-permute-start(bf16[1024,128]{1,0:T(8,128)(2,1)S(1)} %collective-permute-done.6.refs_5_), channel_id=1, source_target_pairs={{0,8},{1,9},{2,10},{3,11},{4,12},{5,13},{6,14},{7,15},{8,0},{9,1},... | collective-permute-start | bytes 786440 | tf_op jit(solution)/shard_map/ppermute | solution.py:113
  24.5 13.8 %collective-permute-start.14 = (bf16[1024,128]{1,0:T(8,128)(2,1)S(1)}, bf16[1024,128]{1,0:T(8,128)(2,1)S(1)}, u32[]{:S(2)}, u32[]{:S(2)}) collective-permute-start(bf16[1024,128]{1,0:T(8,128)(2,1)S(1)} %pad_maximum_fusion.5), channel_id=1, source_target_pairs={{0,17},{1,16},{2,19},{3,18},{4,21},{5,20},{6,23},{7,22},{8,25},{9,... | collective-permute-start | bytes 786440 | tf_op jit(solution)/shard_map/ppermute | solution.py:113
  24.6 13.8 %collective-permute-start.12 = (bf16[1024,128]{1,0:T(8,128)(2,1)S(1)}, bf16[1024,128]{1,0:T(8,128)(2,1)S(1)}, u32[]{:S(2)}, u32[]{:S(2)}) collective-permute-start(bf16[1024,128]{1,0:T(8,128)(2,1)S(1)} %pad_maximum_fusion.5), channel_id=1, source_target_pairs={{0,9},{1,8},{2,11},{3,10},{4,13},{5,12},{6,15},{7,14},{8,1},{9,0},... | collective-permute-start | bytes 786440 | tf_op jit(solution)/shard_map/ppermute | solution.py:113
  27.8 11.1 %collective-permute-start.13 = (bf16[1024,128]{1,0:T(8,128)(2,1)S(1)}, bf16[1024,128]{1,0:T(8,128)(2,1)S(1)}, u32[]{:S(2)}, u32[]{:S(2)}) collective-permute-start(bf16[1024,128]{1,0:T(8,128)(2,1)S(1)} %pad_maximum_fusion.3.refs_0_), channel_id=1, source_target_pairs={{0,16},{1,17},{2,18},{3,19},{4,20},{5,21},{6,22},{7,23},{8,24},{9,... | collective-permute-start | bytes 786440 | tf_op jit(solution)/shard_map/ppermute | solution.py:113
  33.2 4.8 %copy-start.2 = (bf16[1024,64]{1,0:T(8,128)(2,1)S(1)}, bf16[1024,64]{1,0:T(8,128)(2,1)}, u32[]{:S(2)}) copy-start(bf16[1024,64]{1,0:T(8,128)(2,1)} %get-tuple-element.91) | copy-start | bytes 393220
  33.2 4.8 %copy-start.3 = (bf16[1024,64]{1,0:T(8,128)(2,1)S(1)}, bf16[1024,64]{1,0:T(8,128)(2,1)}, u32[]{:S(2)}) copy-start(bf16[1024,64]{1,0:T(8,128)(2,1)} %get-tuple-element.92) | copy-start | bytes 393220
  36.4 7.2 %collective-permute-start.9 = (f16[2,512,128]{2,1,0:T(8,128)(2,1)S(1)}, f16[2,512,128]{2,1,0:T(8,128)(2,1)S(1)}, u32[]{:S(2)}, u32[]{:S(2)}) collective-permute-start(f16[2,512,128]{2,1,0:T(8,128)(2,1)S(1)} %slice_convert_fusion.1), channel_id=1, source_target_pairs={{0,2},{1,3},{2,0},{3,1},{4,6},{5,7},{6,4},{7,5},{8,10},{9,11},{10,... | collective-permute-start | bytes 786440 | tf_op jit(solution)/shard_map/ppermute | solution.py:113
  38.3 18.0 %collective-permute-start.20 = (bf16[1024,128]{1,0:T(8,128)(2,1)S(1)}, bf16[1024,128]{1,0:T(8,128)(2,1)S(1)}, u32[]{:S(2)}, u32[]{:S(2)}) collective-permute-start(bf16[1024,128]{1,0:T(8,128)(2,1)S(1)} %pad_maximum_fusion.8), channel_id=1, source_target_pairs={{0,9},{1,8},{2,11},{3,10},{4,13},{5,12},{6,15},{7,14},{8,1},{9,0},... | collective-permute-start | bytes 786440 | tf_op jit(solution)/shard_map/ppermute | solution.py:113
  39.3 9.2 %collective-permute-start.15 = (bf16[1024,128]{1,0:T(8,128)(2,1)S(1)}, bf16[1024,128]{1,0:T(8,128)(2,1)S(1)}, u32[]{:S(2)}, u32[]{:S(2)}) collective-permute-start(bf16[1024,128]{1,0:T(8,128)(2,1)S(1)} %collective-permute-done.11.refs_2_), channel_id=1, source_target_pairs={{0,16},{1,17},{2,18},{3,19},{4,20},{5,21},{6,22},{7,23},{8,24},{9,... | collective-permute-start | bytes 786440 | tf_op jit(solution)/shard_map/ppermute | solution.py:113
  40.8 10.0 %collective-permute-start.16 = (bf16[1024,128]{1,0:T(8,128)(2,1)S(1)}, bf16[1024,128]{1,0:T(8,128)(2,1)S(1)}, u32[]{:S(2)}, u32[]{:S(2)}) collective-permute-start(bf16[1024,128]{1,0:T(8,128)(2,1)S(1)} %collective-permute-done.14.refs_5_), channel_id=1, source_target_pairs={{0,8},{1,9},{2,10},{3,11},{4,12},{5,13},{6,14},{7,15},{8,0},{9,1},... | collective-permute-start | bytes 786440 | tf_op jit(solution)/shard_map/ppermute | solution.py:113
  42.3 14.3 %collective-permute-start.19 = (bf16[1024,128]{1,0:T(8,128)(2,1)S(1)}, bf16[1024,128]{1,0:T(8,128)(2,1)S(1)}, u32[]{:S(2)}, u32[]{:S(2)}) collective-permute-start(bf16[1024,128]{1,0:T(8,128)(2,1)S(1)} %pad_maximum_fusion.6.refs_0_), channel_id=1, source_target_pairs={{0,8},{1,9},{2,10},{3,11},{4,12},{5,13},{6,14},{7,15},{8,0},{9,1},... | collective-permute-start | bytes 786440 | tf_op jit(solution)/shard_map/ppermute | solution.py:113
  43.6 15.6 %collective-permute-start.22 = (bf16[1024,128]{1,0:T(8,128)(2,1)S(1)}, bf16[1024,128]{1,0:T(8,128)(2,1)S(1)}, u32[]{:S(2)}, u32[]{:S(2)}) collective-permute-start(bf16[1024,128]{1,0:T(8,128)(2,1)S(1)} %pad_maximum_fusion.8), channel_id=1, source_target_pairs={{0,17},{1,16},{2,19},{3,18},{4,21},{5,20},{6,23},{7,22},{8,25},{9,... | collective-permute-start | bytes 786440 | tf_op jit(solution)/shard_map/ppermute | solution.py:113
  48.5 11.6 %collective-permute-start.21 = (bf16[1024,128]{1,0:T(8,128)(2,1)S(1)}, bf16[1024,128]{1,0:T(8,128)(2,1)S(1)}, u32[]{:S(2)}, u32[]{:S(2)}) collective-permute-start(bf16[1024,128]{1,0:T(8,128)(2,1)S(1)} %pad_maximum_fusion.6.refs_0_), channel_id=1, source_target_pairs={{0,16},{1,17},{2,18},{3,19},{4,20},{5,21},{6,22},{7,23},{8,24},{9,... | collective-permute-start | bytes 786440 | tf_op jit(solution)/shard_map/ppermute | solution.py:113
  50.7 11.2 %collective-permute-start.29 = (bf16[1024,128]{1,0:T(8,128)(2,1)S(1)}, bf16[1024,128]{1,0:T(8,128)(2,1)S(1)}, u32[]{:S(2)}, u32[]{:S(2)}) collective-permute-start(bf16[1024,128]{1,0:T(8,128)(2,1)S(1)} %pad_maximum_fusion.10.refs_0_), channel_id=1, source_target_pairs={{0,8},{1,9},{2,10},{3,11},{4,12},{5,13},{6,14},{7,15},{8,0},{9,1},... | collective-permute-start | bytes 786440 | tf_op jit(solution)/shard_map/ppermute | solution.py:113
  56.3 8.7 %collective-permute-start.32 = (bf16[1024,128]{1,0:T(8,128)(2,1)S(1)}, bf16[1024,128]{1,0:T(8,128)(2,1)S(1)}, u32[]{:S(2)}, u32[]{:S(2)}) collective-permute-start(bf16[1024,128]{1,0:T(8,128)(2,1)S(1)} %pad_maximum_fusion.12), channel_id=1, source_target_pairs={{0,17},{1,16},{2,19},{3,18},{4,21},{5,20},{6,23},{7,22},{8,25},{9,... | collective-permute-start | bytes 786440 | tf_op jit(solution)/shard_map/ppermute | solution.py:113
  56.6 10.0 %collective-permute-start.10 = (f16[512,128]{1,0:T(8,128)(2,1)S(1)}, f16[512,128]{1,0:T(8,128)(2,1)S(1)}, u32[]{:S(2)}, u32[]{:S(2)}) collective-permute-start(f16[512,128]{1,0:T(8,128)(2,1)S(1)} %fusion.2), channel_id=1, source_target_pairs={{0,4},{1,5},{2,6},{3,7},{4,0},{5,1},{6,2},{7,3},{8,12},{9,13},{10,... | collective-permute-start | bytes 393224 | tf_op jit(solution)/shard_map/ppermute | solution.py:113
  59.2 11.5 %collective-permute-start.17 = (f16[2,512,128]{2,1,0:T(8,128)(2,1)S(1)}, f16[2,512,128]{2,1,0:T(8,128)(2,1)S(1)}, u32[]{:S(2)}, u32[]{:S(2)}) collective-permute-start(f16[2,512,128]{2,1,0:T(8,128)(2,1)S(1)} %slice_convert_fusion), channel_id=1, source_target_pairs={{0,2},{1,3},{2,0},{3,1},{4,6},{5,7},{6,4},{7,5},{8,10},{9,11},{10,... | collective-permute-start | bytes 786440 | tf_op jit(solution)/shard_map/ppermute | solution.py:113
  60.1 12.0 %collective-permute-start.23 = (bf16[1024,128]{1,0:T(8,128)(2,1)S(1)}, bf16[1024,128]{1,0:T(8,128)(2,1)S(1)}, u32[]{:S(2)}, u32[]{:S(2)}) collective-permute-start(bf16[1024,128]{1,0:T(8,128)(2,1)S(1)} %collective-permute-done.19.refs_2_), channel_id=1, source_target_pairs={{0,16},{1,17},{2,18},{3,19},{4,20},{5,21},{6,22},{7,23},{8,24},{9,... | collective-permute-start | bytes 786440 | tf_op jit(solution)/shard_map/ppermute | solution.py:113
  62.0 11.2 %collective-permute-start.24 = (bf16[1024,128]{1,0:T(8,128)(2,1)S(1)}, bf16[1024,128]{1,0:T(8,128)(2,1)S(1)}, u32[]{:S(2)}, u32[]{:S(2)}) collective-permute-start(bf16[1024,128]{1,0:T(8,128)(2,1)S(1)} %collective-permute-done.22.refs_5_), channel_id=1, source_target_pairs={{0,8},{1,9},{2,10},{3,11},{4,12},{5,13},{6,14},{7,15},{8,0},{9,1},... | collective-permute-start | bytes 786440 | tf_op jit(solution)/shard_map/ppermute | solution.py:113
  65.0 13.4 %collective-permute-start.30 = (bf16[1024,128]{1,0:T(8,128)(2,1)S(1)}, bf16[1024,128]{1,0:T(8,128)(2,1)S(1)}, u32[]{:S(2)}, u32[]{:S(2)}) collective-permute-start(bf16[1024,128]{1,0:T(8,128)(2,1)S(1)} %pad_maximum_fusion.12), channel_id=1, source_target_pairs={{0,9},{1,8},{2,11},{3,10},{4,13},{5,12},{6,15},{7,14},{8,1},{9,0},... | collective-permute-start | bytes 786440 | tf_op jit(solution)/shard_map/ppermute | solution.py:113
  66.5 12.6 %collective-permute-start.31 = (bf16[1024,128]{1,0:T(8,128)(2,1)S(1)}, bf16[1024,128]{1,0:T(8,128)(2,1)S(1)}, u32[]{:S(2)}, u32[]{:S(2)}) collective-permute-start(bf16[1024,128]{1,0:T(8,128)(2,1)S(1)} %pad_maximum_fusion.10.refs_0_), channel_id=1, source_target_pairs={{0,16},{1,17},{2,18},{3,19},{4,20},{5,21},{6,22},{7,23},{8,24},{9,... | collective-permute-start | bytes 786440 | tf_op jit(solution)/shard_map/ppermute | solution.py:113
  70.7 11.0 %collective-permute-start.33 = (bf16[1024,128]{1,0:T(8,128)(2,1)S(1)}, bf16[1024,128]{1,0:T(8,128)(2,1)S(1)}, u32[]{:S(2)}, u32[]{:S(2)}) collective-permute-start(bf16[1024,128]{1,0:T(8,128)(2,1)S(1)} %collective-permute-done.29.refs_2_), channel_id=1, source_target_pairs={{0,16},{1,17},{2,18},{3,19},{4,20},{5,21},{6,22},{7,23},{8,24},{9,... | collective-permute-start | bytes 786440 | tf_op jit(solution)/shard_map/ppermute | solution.py:113
  72.1 10.3 %collective-permute-start.34 = (bf16[1024,128]{1,0:T(8,128)(2,1)S(1)}, bf16[1024,128]{1,0:T(8,128)(2,1)S(1)}, u32[]{:S(2)}, u32[]{:S(2)}) collective-permute-start(bf16[1024,128]{1,0:T(8,128)(2,1)S(1)} %collective-permute-done.32.refs_5_), channel_id=1, source_target_pairs={{0,8},{1,9},{2,10},{3,11},{4,12},{5,13},{6,14},{7,15},{8,0},{9,1},... | collective-permute-start | bytes 786440 | tf_op jit(solution)/shard_map/ppermute | solution.py:113
  73.1 26.7 %collective-permute-start.18 = (f16[512,128]{1,0:T(8,128)(2,1)S(1)}, f16[512,128]{1,0:T(8,128)(2,1)S(1)}, u32[]{:S(2)}, u32[]{:S(2)}) collective-permute-start(f16[512,128]{1,0:T(8,128)(2,1)S(1)} %fusion.3), channel_id=1, source_target_pairs={{0,4},{1,5},{2,6},{3,7},{4,0},{5,1},{6,2},{7,3},{8,12},{9,13},{10,... | collective-permute-start | bytes 393224 | tf_op jit(solution)/shard_map/ppermute | solution.py:113
  78.4 9.4 %collective-permute-start.25 = (f16[2,256,128]{2,1,0:T(8,128)(2,1)S(1)}, f16[2,256,128]{2,1,0:T(8,128)(2,1)S(1)}, u32[]{:S(2)}, u32[]{:S(2)}) collective-permute-start(f16[2,256,128]{2,1,0:T(8,128)(2,1)S(1)} %get-tuple-element.121), channel_id=1, source_target_pairs={{0,2},{1,3},{2,0},{3,1},{4,6},{5,7},{6,4},{7,5},{8,10},{9,11},{10,... | collective-permute-start | bytes 393224 | tf_op jit(solution)/shard_map/ppermute | solution.py:113
  79.2 8.7 %collective-permute-start.27 = (f16[2,256,128]{2,1,0:T(8,128)(2,1)S(1)}, f16[2,256,128]{2,1,0:T(8,128)(2,1)S(1)}, u32[]{:S(2)}, u32[]{:S(2)}) collective-permute-start(f16[2,256,128]{2,1,0:T(8,128)(2,1)S(1)} %get-tuple-element.122), channel_id=1, source_target_pairs={{0,2},{1,3},{2,0},{3,1},{4,6},{5,7},{6,4},{7,5},{8,10},{9,11},{10,... | collective-permute-start | bytes 393224 | tf_op jit(solution)/shard_map/ppermute | solution.py:113
  85.7 8.6 %collective-permute-start.35 = (f16[2,256,128]{2,1,0:T(8,128)(2,1)S(1)}, f16[2,256,128]{2,1,0:T(8,128)(2,1)S(1)}, u32[]{:S(2)}, u32[]{:S(2)}) collective-permute-start(f16[2,256,128]{2,1,0:T(8,128)(2,1)S(1)} %get-tuple-element.119), channel_id=1, source_target_pairs={{0,2},{1,3},{2,0},{3,1},{4,6},{5,7},{6,4},{7,5},{8,10},{9,11},{10,... | collective-permute-start | bytes 393224 | tf_op jit(solution)/shard_map/ppermute | solution.py:113
  86.2 10.4 %collective-permute-start.37 = (f16[2,256,128]{2,1,0:T(8,128)(2,1)S(1)}, f16[2,256,128]{2,1,0:T(8,128)(2,1)S(1)}, u32[]{:S(2)}, u32[]{:S(2)}) collective-permute-start(f16[2,256,128]{2,1,0:T(8,128)(2,1)S(1)} %get-tuple-element.120), channel_id=1, source_target_pairs={{0,2},{1,3},{2,0},{3,1},{4,6},{5,7},{6,4},{7,5},{8,10},{9,11},{10,... | collective-permute-start | bytes 393224 | tf_op jit(solution)/shard_map/ppermute | solution.py:113
  87.9 11.9 %collective-permute-start.28 = (f16[256,128]{1,0:T(8,128)(2,1)S(1)}, f16[256,128]{1,0:T(8,128)(2,1)S(1)}, u32[]{:S(2)}, u32[]{:S(2)}) collective-permute-start(f16[256,128]{1,0:T(8,128)(2,1)S(1)} %fusion.9), channel_id=1, source_target_pairs={{0,4},{1,5},{2,6},{3,7},{4,0},{5,1},{6,2},{7,3},{8,12},{9,13},{10,... | collective-permute-start | bytes 196616 | tf_op jit(solution)/shard_map/ppermute | solution.py:113
  90.6 9.3 %collective-permute-start.26 = (f16[256,128]{1,0:T(8,128)(2,1)S(1)}, f16[256,128]{1,0:T(8,128)(2,1)S(1)}, u32[]{:S(2)}, u32[]{:S(2)}) collective-permute-start(f16[256,128]{1,0:T(8,128)(2,1)S(1)} %fusion.8), channel_id=1, source_target_pairs={{0,4},{1,5},{2,6},{3,7},{4,0},{5,1},{6,2},{7,3},{8,12},{9,13},{10,... | collective-permute-start | bytes 196616 | tf_op jit(solution)/shard_map/ppermute | solution.py:113
  96.7 6.2 %collective-permute-start.38 = (f16[256,128]{1,0:T(8,128)(2,1)S(1)}, f16[256,128]{1,0:T(8,128)(2,1)S(1)}, u32[]{:S(2)}, u32[]{:S(2)}) collective-permute-start(f16[256,128]{1,0:T(8,128)(2,1)S(1)} %fusion.11), channel_id=1, source_target_pairs={{0,4},{1,5},{2,6},{3,7},{4,0},{5,1},{6,2},{7,3},{8,12},{9,13},{10,... | collective-permute-start | bytes 196616 | tf_op jit(solution)/shard_map/ppermute | solution.py:113
  97.7 5.8 %collective-permute-start.36 = (f16[256,128]{1,0:T(8,128)(2,1)S(1)}, f16[256,128]{1,0:T(8,128)(2,1)S(1)}, u32[]{:S(2)}, u32[]{:S(2)}) collective-permute-start(f16[256,128]{1,0:T(8,128)(2,1)S(1)} %fusion.10), channel_id=1, source_target_pairs={{0,4},{1,5},{2,6},{3,7},{4,0},{5,1},{6,2},{7,3},{8,12},{9,13},{10,... | collective-permute-start | bytes 196616 | tf_op jit(solution)/shard_map/ppermute | solution.py:113
